TPU v7x, 32 devices: a whole 2x2x4 slice. The times are simulated.
32 devices in a mesh: section: 4 (over y, x), dp: 8 (over z, core).
Axes of the slice: x: 2, y: 2, z: 4, core: 2. Of those that a mesh axis runs over, the one named last changes fastest.
Arguments:
- tokens: bfloat16 [2, 2048, 512], P(None, 'dp'), may hold values from -40 to 40
- seq_lengths: int32 [2, 16], P(None, 'dp'), may hold values from 0 to 256, as said below
- out_grad: bfloat16 [2, 2048, 512], P(None, 'dp'), may hold values from -6 to 6
- norm_gain: float32 [2, 512], replicated, may hold values from 0.25 to 1.75
- norm_bias: float32 [2, 512], replicated, may hold values from -3 to 3
- decay_rate: float32 [2, 192], replicated, may hold values from 0.05 to 2
- frequency: float32 [2, 192], replicated, may hold values from -8 to 8
- log_step: float32 [2, 192], replicated, may hold values from -6.9 to -2.3
- input_matrix: bfloat16 [2, 512, 384], replicated, may hold values from -0.25 to 0.25
- output_matrix: bfloat16 [2, 384, 512], replicated, may hold values from -0.625 to 0.625
- skip_gain: float32 [2, 512], replicated, may hold values from -4 to 4
- gate_matrix: bfloat16 [2, 512, 512], replicated, may hold values from -0.25 to 0.25
- gate_bias: float32 [2, 512], replicated, may hold values from -3 to 3
Outputs:
- mixed_out: bfloat16 [2, 2048, 512], P(None, 'dp', 'section')
- token_grad: float32 [2, 2048, 512], P(None, 'dp', 'section')
- norm_gain_grad: float32 [2, 512], replicated
- norm_bias_grad: float32 [2, 512], replicated
- decay_rate_grad: float32 [2, 192], replicated
- frequency_grad: float32 [2, 192], replicated
- log_step_grad: float32 [2, 192], replicated
- input_matrix_grad: float32 [2, 512, 384], replicated
- output_matrix_grad: float32 [2, 384, 512], replicated
- skip_gain_grad: float32 [2, 512], replicated
- gate_matrix_grad: float32 [2, 512, 512], replicated
- gate_bias_grad: float32 [2, 512], replicated
Inputs may be any that keep to these rules, and one draw needn't show every extreme that they name: `seq_lengths`: for each micro-batch and device the two entries are a first length of at least 32 and a second length that is either 0 or 256 minus the first; in every micro-batch some device's first length is 256.
All inputs are finite; a program needn't handle non-finite values.
Results may differ from a plain program's by a relative error of at most 0.012.
Values may be sent and summed in bfloat16 or wider, within the bound.
A program may use at most 320 MiB of HBM per device.

v0:
```python
from functools import partial
from types import SimpleNamespace

import jax
import jax.numpy as jnp
from jax import lax
from jax.experimental import pallas as pl
from jax.experimental.pallas import tpu as pltpu
from jax.sharding import PartitionSpec as P

epsilon = 1e-05
MESH = pl.DeviceIdType.MESH
F32 = jnp.float32
BF16 = jnp.bfloat16
SUB = 8
QUAD = 4
REDUCES = 9


STAGES = tuple(dict(mine=0, theirs=0, chip=0, quad=0, group=0, full=0))


def matmul(left, right):
    return jnp.dot(left, right, preferred_element_type=F32)


def matmul_nt(left, right):
    return lax.dot_general(left, right, (((1,), (1,)), ((), ())), preferred_element_type=F32)


def matmul_tn(left, right):
    return lax.dot_general(left, right, (((0,), (0,)), ((), ())), preferred_element_type=F32)


def cmul(ar, ai, br, bi):
    return ar * br - ai * bi, ar * bi + ai * br


def repeat_lanes(x, times):
    return jnp.concatenate([x] * times, axis=1)


def fold_rows(x):
    return jnp.sum(x.reshape(x.shape[0] // SUB, SUB, x.shape[1]), axis=0)


def unfold(total, first, count):
    return jnp.concatenate([total[first + k : first + k + 1, :] for k in range(count)], axis=1)


class SmallSum:
    def __init__(self, place, own, sibling, slots, send_sems, recv_sems, index):
        self.place, self.own, self.sibling, self.slots = place, own, sibling, slots
        self.send_sems, self.recv_sems, self.index = send_sems, recv_sems, index

    def start(self):
        at = self.place
        self.copy = pltpu.make_async_remote_copy(
            src_ref=self.own,
            dst_ref=self.sibling,
            send_sem=self.send_sems.at[self.index, 0],
            recv_sem=self.recv_sems.at[self.index, 0],
            device_id=(at.section, at.sibling),
            device_id_type=MESH,
        )
        self.copy.start()

    def turn(self):
        at = self.place
        self.copy.wait()
        chip = at.chip
        self.slots[chip] = self.own[...] + self.sibling[...]
        self.copies = []
        for step in range(1, at.chips):
            copy = pltpu.make_async_remote_copy(
                src_ref=self.slots.at[chip],
                dst_ref=self.slots.at[chip],
                send_sem=self.send_sems.at[self.index, step],
                recv_sem=self.recv_sems.at[self.index, step],
                device_id=(at.section, at.chip_peer(step)),
                device_id_type=MESH,
            )
            copy.start()
            self.copies.append(copy)

    def total(self):
        for copy in self.copies:
            copy.wait()
        result = self.slots[0]
        for chip in range(1, self.place.chips):
            result = result + self.slots[chip]
        return result


class GradSum:
    def __init__(self, place, refs, send_sems, recv_sems, index):
        self.place = place
        self.mine, self.theirs, self.chip_part, self.quad_in, self.group_in, self.full = refs
        self.send_sems, self.recv_sems, self.index = send_sems, recv_sems, index
        self.sem = 0

    def remote(self, src, dst, device):
        copy = pltpu.make_async_remote_copy(
            src_ref=src,
            dst_ref=dst,
            send_sem=self.send_sems.at[self.index, self.sem],
            recv_sem=self.recv_sems.at[self.index, self.sem],
            device_id=device,
            device_id_type=MESH,
        )
        self.sem += 1
        copy.start()
        return copy

    def to_core(self):
        at = self.place
        self.copy = self.remote(
            self.mine.at[1 - at.core], self.theirs, (at.section, at.sibling)
        )

    def to_quad(self):
        at = self.place
        self.copy.wait()
        for part in range(QUAD):
            both = self.mine[at.core, part].astype(F32) + self.theirs[part].astype(F32)
            self.chip_part[part] = both.astype(BF16)
        self.copies = []
        for step in range(1, QUAD):
            other = lax.rem(at.quad + step, QUAD)
            self.copies.append(
                self.remote(
                    self.chip_part.at[other],
                    self.quad_in.at[at.quad],
                    (at.section, at.quad_peer(step)),
                )
            )
        self.quad_in[at.quad] = self.chip_part[at.quad]

    def to_groups(self):
        at = self.place
        for copy in self.copies:
            copy.wait()
        total = self.quad_in[0].astype(F32)
        for part in range(1, QUAD):
            total = total + self.quad_in[part].astype(F32)
        if at.groups > 1:
            group = at.group
            self.group_in[group] = total.astype(BF16)
            copies = []
            for step in range(1, at.groups):
                copies.append(
                    self.remote(
                        self.group_in.at[group],
                        self.group_in.at[group],
                        (at.section, at.chip_peer(step * QUAD)),
                    )
                )
            for copy in copies:
                copy.wait()
            total = self.group_in[0].astype(F32)
            for other in range(1, at.groups):
                total = total + self.group_in[other].astype(F32)
        piece = self.full.at[at.core, at.section, at.quad]
        piece[...] = total.astype(BF16)
        self.copies = [
            self.remote(piece, piece, (at.section, at.quad_peer(step)))
            for step in range(1, QUAD)
        ]

    def to_sections(self):
        at = self.place
        for copy in self.copies:
            copy.wait()
        piece = self.full.at[at.core, at.section]
        self.copies = [
            self.remote(piece, piece, (lax.rem(at.section + step, at.sections), at.dp))
            for step in range(1, at.sections)
        ]

    def to_sibling(self):
        at = self.place
        for copy in self.copies:
            copy.wait()
        piece = self.full.at[at.core]
        self.copy = self.remote(piece, piece, (at.section, at.sibling))

    def to_result(self, result, sem):
        self.copy.wait()
        self.out = pltpu.make_async_copy(self.full, result, sem)
        self.out.start()

    def end(self):
        self.out.wait()


def main_kernel(cfg, names, *refs):
    r = SimpleNamespace(**dict(zip(names, refs)))
    rows, width, states, half, lanes = (
        cfg.rows,
        cfg.width,
        cfg.states,
        cfg.half,
        cfg.lanes,
    )
    steps = rows // SUB
    section = lax.axis_index("section")
    dp = lax.axis_index("dp")
    chips = cfg.dp // 2
    core, chip = lax.rem(dp, 2), lax.div(dp, 2)
    quad, group = lax.rem(chip, QUAD), lax.div(chip, QUAD)
    place = SimpleNamespace(
        section=section,
        sections=cfg.sections,
        dp=dp,
        core=core,
        chip=chip,
        chips=chips,
        quad=quad,
        group=group,
        groups=chips // QUAD,
        sibling=dp + 1 - 2 * core,
        chip_peer=lambda step: lax.rem(chip + step, chips) * 2 + core,
        quad_peer=lambda step: (group * QUAD + lax.rem(quad + step, QUAD)) * 2 + core,
    )

    peers = [(section, place.sibling)]
    peers += [(section, place.chip_peer(step)) for step in range(1, chips)]
    peers += [(lax.rem(section + step, cfg.sections), dp) for step in range(1, cfg.sections)]
    barrier = pltpu.get_barrier_semaphore()
    for peer in peers:
        pl.semaphore_signal(barrier, inc=1, device_id=peer, device_id_type=MESH)

    small = [
        SmallSum(
            place,
            r.sum_own.at[k],
            r.sum_sibling.at[k],
            r.sum_slots.at[k],
            r.sum_send,
            r.sum_recv,
            k,
        )
        for k in range(REDUCES)
    ]
    first_sum = small[0]
    mid_sum = [small[1], small[2]]
    upper_sum = [small[3], small[4]]
    lower_sum = [small[5], small[6]]
    layer_sum = [small[8], small[7]]
    batches = [
        GradSum(
            place,
            [getattr(r, f"{part}_{k}") for part in STAGES],
            r.grad_send,
            r.grad_recv,
            k,
        )
        for k in range(3)
    ]
    upper_batch, gate_batch, in_batch = batches

    first_len = [r.lengths[m, 0] for m in range(2)]
    total_len = [r.lengths[m, 0] + r.lengths[m, 1] for m in range(2)]

    def put(index, at, row):
        for k in range(row.shape[1] // 128):
            r.sum_own[index, at + k : at + k + 1, :] = row[:, k * 128 : (k + 1) * 128]

    chunk = 32
    for m in range(2):

        def token_sums(t, carry, m=m):
            at = pl.ds(pl.multiple_of(t * chunk, chunk), chunk)
            v = r.tokens[m, at, :].astype(F32)
            place_row = t * chunk + lax.broadcasted_iota(jnp.int32, (chunk, width), 0)
            kept = jnp.where(place_row < total_len[m], v, 0.0)
            return carry[0] + fold_rows(kept), carry[1] + fold_rows(kept * v)

        zero = jnp.zeros((SUB, width), F32)
        sums, squares = lax.fori_loop(0, rows // chunk, token_sums, (zero, zero))
        put(0, 8 * m, jnp.sum(sums, axis=0, keepdims=True))
        put(0, 8 * m + 4, jnp.sum(squares, axis=0, keepdims=True))
        count = jnp.minimum(total_len[m], rows).astype(F32)
        r.sum_own[0, 16 + m : 17 + m, :] = jnp.full((1, 128), count, F32)

    pl.semaphore_wait(barrier, len(peers))
    first_sum.start()

    at_i = lax.broadcasted_iota(jnp.int32, (rows, rows), 0)
    at_r = lax.broadcasted_iota(jnp.int32, (rows, rows), 1)
    r.spread[...] = jnp.where(
        at_r == (at_i % SUB) * steps + at_i // SUB, 1.0, 0.0
    ).astype(BF16)
    r.gather[...] = jnp.where(
        at_i == (at_r % SUB) * steps + at_r // SUB, 1.0, 0.0
    ).astype(BF16)
    for m in range(2):
        r.first_in[m] = matmul(r.spread[...], r.tokens[m]).astype(BF16)
    first_sum.turn()
    for m in range(2):
        r.out_grads[m] = matmul(r.spread[...], r.out_grad[m]).astype(BF16)
    held = lax.broadcasted_iota(jnp.int32, (rows, 128), 0)
    held = (held % SUB) * steps + held // SUB
    all_start, all_end = [], []
    for m in range(2):
        one, zero = jnp.float32(1.0), jnp.float32(0.0)
        past = held >= total_len[m]
        starts = (held == 0) | (held == first_len[m]) | past
        ends = (held == first_len[m] - 1) | (held == total_len[m] - 1) | past | (held == rows - 1)
        r.valid[m] = jnp.where(past, zero, one)
        r.keep_start[m] = jnp.where(starts, zero, one)
        r.keep_end[m] = jnp.where(ends, zero, one)
        for kept, mask in ((all_start, r.keep_start), (all_end, r.keep_end)):
            kept.append(jnp.min(mask[m].reshape(steps, SUB, 128), axis=0))

    r.par[...] = jnp.zeros((SUB, lanes), F32)
    r.par[0:2, :] = jnp.ones((2, lanes), F32)
    r.par[0:2, 0:half] = r.decay[...]
    r.par[2:4, 0:half] = r.freq[...]
    r.par[4:6, 0:half] = r.lstep[...]
    decay, spin = r.par[0:2, :], r.par[2:4, :]
    step_size = jnp.exp(r.par[4:6, :])
    damping = jnp.exp(-decay * step_size)
    bar_re = damping * jnp.cos(spin * step_size)
    bar_im = damping * jnp.sin(spin * step_size)
    modulus = decay * decay + spin * spin
    fac_re = ((bar_re - 1.0) * -decay + bar_im * spin) / modulus
    fac_im = (bar_im * -decay - (bar_re - 1.0) * spin) / modulus
    pow_re, pow_im = bar_re, bar_im
    power = 1
    while power < steps:
        pow_re, pow_im = cmul(pow_re, pow_im, pow_re, pow_im)
        power *= 2

    lane = lax.broadcasted_iota(jnp.int32, (1, 128), 1)
    low_lanes = lane < half - 128
    turn_by = half - 128

    for l in range(2):

        def pad_in(t, carry, l=l):
            at = pl.ds(pl.multiple_of(t * chunk, chunk), chunk)
            tile = [r.b_in[l, at, k * 128 : (k + 1) * 128].astype(F32) for k in range(3)]
            rolled = [pltpu.roll(x, 64, 1) for x in tile[1:]]
            padded = [
                tile[0],
                jnp.where(low_lanes, tile[1], 0.0),
                jnp.where(low_lanes, rolled[0], rolled[1]),
                jnp.where(low_lanes, rolled[1], 0.0),
            ]
            r.b_pad[l, at, :] = jnp.concatenate(padded, axis=1).astype(BF16)
            return carry

        lax.fori_loop(0, width // chunk, pad_in, 0)
        blank = jnp.zeros((lanes - half, width), BF16)
        r.c_pad[l, 0:half, :] = r.c_out[l, 0:half, :]
        r.c_pad[l, half:lanes, :] = blank
        r.c_pad[l, lanes : lanes + half, :] = r.c_out[l, half:states, :]
        r.c_pad[l, lanes + half : 2 * lanes, :] = blank

    def across(end, coef, reverse):
        end_re, end_im = end
        coef_re, coef_im = coef
        sub = lax.broadcasted_iota(jnp.int32, (SUB, lanes), 0)
        for by in (1, 2, 4):
            turn = SUB - by if reverse else by
            live = sub < SUB - by if reverse else sub >= by

            def moved(x):
                return jnp.where(live, pltpu.roll(x, turn, 0), 0.0)

            add_re, add_im = cmul(coef_re, coef_im, moved(end_re), moved(end_im))
            coef_re, coef_im = cmul(coef_re, coef_im, moved(coef_re), moved(coef_im))
            end_re, end_im = end_re + add_re, end_im + add_im
        turn = SUB - 1 if reverse else 1
        live = sub < SUB - 1 if reverse else sub >= 1
        return tuple(jnp.where(live, pltpu.roll(x, turn, 0), 0.0) for x in (end_re, end_im))

    def wide8(x, l):
        return jnp.broadcast_to(x[l : l + 1, :], (SUB, x.shape[1]))

    def group_rows(p):
        return pl.ds(pl.multiple_of(p * SUB, SUB), SUB)

    def scan_coefs(l, m, reverse):
        keep = r.keep_end if reverse else r.keep_start
        all_kept = repeat_lanes((all_end if reverse else all_start)[m], lanes // 128)
        product = (all_kept * wide8(pow_re, l), all_kept * wide8(pow_im, l))
        return keep, wide8(bar_re, l), wide8(bar_im, l), product

    def advance(keep, m, at, br, bi, re, im, src_re, src_im):
        k = repeat_lanes(keep[m, at, :], lanes // 128)
        kr, ki = k * br, k * bi
        return kr * re - ki * im + src_re, kr * im + ki * re + src_im

    def scan_states(l, m):
        reverse = l == 1
        lead = 0 if reverse else 1
        keep, br, bi, product = scan_coefs(l, m, reverse)
        fr, fi = wide8(fac_re, l), wide8(fac_im, l)
        zero = jnp.zeros((SUB, lanes), F32)

        def ends(t, carry):
            p = steps - 1 - t if reverse else t
            at = group_rows(p)
            v = repeat_lanes(r.valid[m, at, :], lanes // 128)
            drive_re = r.drive[l, m, at, 0:lanes]
            drive_im = r.drive[l, m, at, lanes : 2 * lanes]
            src_re, src_im = cmul(fr, fi, v * drive_re, v * drive_im)
            r.state[l, m, group_rows(p + lead), 0:lanes] = src_re
            r.state[l, m, group_rows(p + lead), lanes : 2 * lanes] = src_im
            return advance(keep, m, at, br, bi, *carry, src_re, src_im)

        end = lax.fori_loop(0, steps, ends, (zero, zero), unroll=4)
        enter = across(end, product, reverse)
        first = steps if reverse else 0
        r.state[l, m, first * SUB : (first + 1) * SUB, 0:lanes] = enter[0]
        r.state[l, m, first * SUB : (first + 1) * SUB, lanes : 2 * lanes] = enter[1]

        def fill(t, carry):
            done = []
            for k in range(2):
                p = steps - 1 - (2 * t + k) if reverse else 2 * t + k
                at, to = group_rows(p), group_rows(p + lead)
                src_re = r.state[l, m, to, 0:lanes]
                src_im = r.state[l, m, to, lanes : 2 * lanes]
                carry = advance(keep, m, at, br, bi, *carry, src_re, src_im)
                r.state[l, m, to, 0:lanes] = carry[0]
                r.state[l, m, to, lanes : 2 * lanes] = carry[1]
                done.append(jnp.concatenate([carry[0], -carry[1]], axis=1))
            pair = steps // 2 - 1 - t if reverse else t
            both = jnp.concatenate(done[::-1] if reverse else done, axis=0)
            to = pl.ds(pl.multiple_of(m * rows + pair * 16, 16), 16)
            r.joined[l, to, :] = both.astype(BF16)
            return carry

        lax.fori_loop(0, steps // 2, fill, enter, unroll=2)

    def scan_grads(l, m):
        reverse = l == 0
        back = 1 if l == 1 else 0
        keep, br, bi, product = scan_coefs(l, m, reverse)
        keep_state = r.keep_start if l == 0 else r.keep_end
        fr, fi = 2.0 * wide8(fac_re, l), 2.0 * wide8(fac_im, l)
        zero = jnp.zeros((SUB, lanes), F32)

        def ends(t, carry):
            p = steps - 1 - t if reverse else t
            at = group_rows(p)
            q_re = r.work[at, 0:lanes]
            q_im = r.work[at, lanes : 2 * lanes]
            return advance(keep, m, at, br, bi, *carry, q_re, q_im)

        end = lax.fori_loop(0, steps, ends, (zero, zero), unroll=4)
        enter = across(end, product, reverse)

        def fill(t, carry):
            w, bar_sum, fac_sum = carry
            done = []
            for k in range(2):
                p = steps - 1 - (2 * t + k) if reverse else 2 * t + k
                at, near = group_rows(p), group_rows(p + back)
                q_re = r.work[at, 0:lanes]
                q_im = r.work[at, lanes : 2 * lanes]
                w = advance(keep, m, at, br, bi, *w, q_re, q_im)
                kept = repeat_lanes(keep_state[m, at, :], lanes // 128)
                near_re = kept * r.state[l, m, near, 0:lanes]
                near_im = kept * r.state[l, m, near, lanes : 2 * lanes]
                term = cmul(*w, near_re, near_im)
                bar_sum = (bar_sum[0] + term[0], bar_sum[1] + term[1])
                v = repeat_lanes(r.valid[m, at, :], lanes // 128)
                vw = (v * w[0], v * w[1])
                drive_re = r.drive[l, m, at, 0:lanes]
                drive_im = r.drive[l, m, at, lanes : 2 * lanes]
                term = cmul(*vw, drive_re, drive_im)
                fac_sum = (fac_sum[0] + term[0], fac_sum[1] + term[1])
                gd_re, gd_im = cmul(fr, fi, *vw)
                im_low = pltpu.roll(-gd_im[:, 0:128], 64, 1)
                im_high = pltpu.roll(-gd_im[:, 128:256], 64, 1)
                done.append(
                    jnp.concatenate(
                        [
                            gd_re[:, 0:128],
                            jnp.where(low_lanes, gd_re[:, 128:256], im_low),
                            jnp.where(low_lanes, im_low, im_high),
                        ],
                        axis=1,
                    )
                )
            pair = steps // 2 - 1 - t if reverse else t
            both = jnp.concatenate(done[::-1] if reverse else done, axis=0)
            to = pl.ds(pl.multiple_of(m * rows + pair * 16, 16), 16)
            r.grad_drive[l, to, :] = both.astype(BF16)
            return w, bar_sum, fac_sum

        none = (zero, zero)
        _, bar_sum, fac_sum = lax.fori_loop(0, steps // 2, fill, (enter, none, none), unroll=2)
        for k, part in enumerate((*bar_sum, *fac_sum)):
            r.state_sums[l, m, k] = part

    def row_of(ref, l):
        return ref[l : l + 1, :]

    def micro_rows(m):
        return slice(m * rows, (m + 1) * rows)

    gelu_chunk = 16

    def mixer(l, m, center, inv, hook=None):
        gain, bias, skip = row_of(r.gain, l), row_of(r.bias, l), row_of(r.skip, l)

        def normalise(t, carry):
            at = pl.ds(pl.multiple_of(t * chunk, chunk), chunk)
            if l == 0:
                v = r.first_in[m, at, :].astype(F32)
            else:
                v = r.second_in[m, at, :]
            normed = (v - center) * inv
            r.normed[l, m, at, :] = normed
            to = pl.ds(pl.multiple_of(m * rows + t * chunk, chunk), chunk)
            r.scaled[l, to, :] = (normed * gain + bias).astype(BF16)
            return carry

        lax.fori_loop(0, rows // chunk, normalise, 0)
        r.drive[l, m] = matmul(r.scaled[l, micro_rows(m), :], r.b_pad[l])
        scan_states(l, m)
        r.work[...] = matmul(r.joined[l, micro_rows(m), :], r.c_pad[l])
        if hook is not None:
            hook()

        def activate(t, carry):
            at = pl.ds(pl.multiple_of(t * gelu_chunk, gelu_chunk), gelu_chunk)
            scaled = r.normed[l, m, at, :] * gain + bias
            y = (2.0 * r.work[at, :] + skip * scaled).astype(BF16).astype(F32)
            below = 0.5 + 0.5 * lax.erf(y * 0.7071067811865476)
            density = jnp.exp(-0.5 * y * y) * 0.3989422804014327
            active = y * below
            r.active[l, m, at, :] = active
            r.slope[l, m, at, :] = below + y * density
            to = pl.ds(pl.multiple_of(m * rows + t * gelu_chunk, gelu_chunk), gelu_chunk)
            r.active_low[l, to, :] = active.astype(BF16)
            return carry

        lax.fori_loop(0, rows // gelu_chunk, activate, 0)
        r.work[...] = matmul(r.active_low[l, micro_rows(m), :], r.gmat[l])

    def first_gate(m):
        gbias = row_of(r.gbias, 0)

        def gate(t, carry):
            at = pl.ds(pl.multiple_of(t * gelu_chunk, gelu_chunk), gelu_chunk)
            opened = jax.nn.sigmoid(r.work[at, :] + gbias)
            r.sig[0, m, at, :] = opened
            v = repeat_lanes(r.valid[m, at, :], width // 128)
            gated = v * r.active[0, m, at, :] * opened
            second = r.first_in[m, at, :].astype(F32) + gated.astype(BF16).astype(F32)
            r.second_in[m, at, :] = second
            kept = v * second
            return carry[0] + fold_rows(kept), carry[1] + fold_rows(kept * second)

        zero = jnp.zeros((SUB, width), F32)
        sums, squares = lax.fori_loop(0, rows // gelu_chunk, gate, (zero, zero))
        put(1 + m, 0, jnp.sum(sums, axis=0, keepdims=True))
        put(1 + m, 4, jnp.sum(squares, axis=0, keepdims=True))

    bias_sums = {}
    skip_sums = {}

    def gate_grad(l, m, grad_of):
        gbias = row_of(r.gbias, l)

        def gate(t, carry):
            at = pl.ds(pl.multiple_of(t * gelu_chunk, gelu_chunk), gelu_chunk)
            if l == 1:
                opened = jax.nn.sigmoid(r.work[at, :] + gbias)
                r.sig[1, m, at, :] = opened
            else:
                opened = r.sig[0, m, at, :]
            v = repeat_lanes(r.valid[m, at, :], width // 128)
            masked = v * grad_of(at, v)
            through = masked * opened
            r.through[at, :] = through
            grad_logits = through * r.active[l, m, at, :] * (1.0 - opened)
            to = pl.ds(pl.multiple_of(m * rows + t * gelu_chunk, gelu_chunk), gelu_chunk)
            r.grad_logits[l, to, :] = grad_logits.astype(BF16)
            return carry + fold_rows(grad_logits)

        zero = jnp.zeros((SUB, width), F32)
        bias_sums[l, m] = lax.fori_loop(0, rows // gelu_chunk, gate, zero)

    def branch_grad(l, m):
        gain, bias = row_of(r.gain, l), row_of(r.bias, l)
        r.work[...] = matmul_nt(r.grad_logits[l, micro_rows(m), :], r.gmat[l])

        def branch(t, carry):
            at = pl.ds(pl.multiple_of(t * chunk, chunk), chunk)
            grad_active = r.through[at, :] + r.work[at, :]
            g = (r.slope[l, m, at, :] * grad_active).astype(BF16)
            to = pl.ds(pl.multiple_of(m * rows + t * chunk, chunk), chunk)
            r.branch[l, to, :] = g
            scaled = r.normed[l, m, at, :] * gain + bias
            return carry + fold_rows(g.astype(F32) * scaled)

        zero = jnp.zeros((SUB, width), F32)
        skip_sums[l, m] = lax.fori_loop(0, rows // chunk, branch, zero)
        r.work[...] = matmul_nt(r.branch[l, micro_rows(m), :], r.c_pad[l])

    def mixer_grad(l, m, index):
        skip = row_of(r.skip, l)
        scan_grads(l, m)
        r.work[...] = matmul_nt(r.grad_drive[l, micro_rows(m), :], r.b_in[l])

        def scaled_grad(t, carry):
            at = pl.ds(pl.multiple_of(t * chunk, chunk), chunk)
            to = pl.ds(pl.multiple_of(m * rows + t * chunk, chunk), chunk)
            grad = r.work[at, :] + skip * r.branch[l, to, :].astype(F32)
            r.grad_scaled[l, m, at, :] = grad
            normed = r.normed[l, m, at, :]
            return carry[0] + fold_rows(grad), carry[1] + fold_rows(grad * normed)

        zero = jnp.zeros((SUB, width), F32)
        sums, products = lax.fori_loop(0, rows // chunk, scaled_grad, (zero, zero))
        put(index, 0, jnp.sum(sums, axis=0, keepdims=True))
        put(index, 4, jnp.sum(products, axis=0, keepdims=True))

    def moments(total, at, count):
        center = unfold(total, at, 4) / count
        return center, lax.rsqrt(unfold(total, at + 4, 4) / count - center * center + epsilon)

    own_columns = pl.ds(pl.multiple_of(section * 128, 128), 128)

    def gate_weights(l, ref):
        grad = matmul_tn(r.active_low[l, :, own_columns], r.grad_logits[l])
        ref[:, :, :, 0:width] = grad.astype(BF16).reshape(2, QUAD, 16, width)

    def out_weights(l, ref, at):
        grad = 2.0 * matmul_tn(r.joined[l], r.branch[l, :, own_columns])
        grad = jnp.concatenate([grad[0:half, :], grad[lanes : lanes + half, :]], axis=0)
        tall = states // (2 * QUAD)
        for k in range(tall // 16):
            for c in range(2):
                for z in range(QUAD):
                    first = (c * QUAD + z) * tall + 16 * k
                    ref[c, z, :, at + 128 * k : at + 128 * (k + 1)] = grad[
                        first : first + 16, :
                    ].astype(BF16)

    def in_weights(l, ref, at):
        grad = matmul_tn(r.scaled[l, :, own_columns], r.grad_drive[l])
        ref[:, :, :, at : at + states] = grad.astype(BF16).reshape(2, QUAD, 16, states)

    def layer_rows(l, index):
        def both(sums):
            return jnp.sum(sums[l, 0] + sums[l, 1], axis=0, keepdims=True)

        put(index, 0, both(skip_sums))
        put(index, 4, both(bias_sums))
        part = [
            jnp.sum(r.state_sums[l, 0, k] + r.state_sums[l, 1, k], axis=0, keepdims=True)
            for k in range(4)
        ]
        gb_re, gb_im = 2.0 * part[0], -2.0 * part[1]
        gf_re, gf_im = 2.0 * part[2], -2.0 * part[3]
        one = slice(l, l + 1)
        lam_re, lam_im, size = -decay[one], spin[one], step_size[one]
        b_re, b_im, f_re, f_im = bar_re[one], bar_im[one], fac_re[one], fac_im[one]
        top_re, top_im = size * b_re - f_re, size * b_im - f_im
        square = modulus[one]
        d_re = (top_re * lam_re + top_im * lam_im) / square
        d_im = (top_im * lam_re - top_re * lam_im) / square
        gl_re = size * (b_re * gb_re + b_im * gb_im) + (d_re * gf_re + d_im * gf_im)
        gl_im = size * (b_re * gb_im - b_im * gb_re) + (d_re * gf_im - d_im * gf_re)
        e_re, e_im = cmul(lam_re, lam_im, b_re, b_im)
        g_step = size * ((e_re * gb_re + e_im * gb_im) + (b_re * gf_re + b_im * gf_im))
        put(index, 8, -gl_re)
        put(index, 10, gl_im)
        put(index, 12, g_step)

    def mixed_rows(m):
        def mix(t, carry):
            at = pl.ds(pl.multiple_of(t * chunk, chunk), chunk)
            gated = (
                r.valid[m, at, :]
                * r.active[1, m, at, own_columns]
                * r.sig[1, m, at, own_columns]
            )
            stream = r.second_in[m, at, own_columns].astype(BF16).astype(F32)
            r.narrow[at, :] = (stream + gated).astype(BF16)
            return carry

        lax.fori_loop(0, rows // chunk, mix, 0)
        r.mixed[m] = matmul(r.gather[...], r.narrow[...]).astype(BF16)

    def stream_grad(l, m, total, count, inv):
        gain = row_of(r.gain, l)
        first = gain * unfold(total, 0, 4) / count
        second = gain * unfold(total, 4, 4) / count
        return gain, first, second, inv

    total0 = first_sum.total()
    counts = [repeat_lanes(total0[16 + m : 17 + m, :], width // 128) for m in range(2)]
    norm0 = [moments(total0, 8 * m, counts[m]) for m in range(2)]

    mixer(0, 0, *norm0[0])
    first_gate(0)
    mid_sum[0].start()
    mixer(0, 1, *norm0[1], hook=mid_sum[0].turn)
    first_gate(1)
    mid_sum[1].start()

    norm1 = [None, None]
    for m in range(2):
        norm1[m] = moments(mid_sum[m].total(), 0, counts[m])
        hook = mid_sum[1].turn if m == 0 else upper_sum[0].turn
        mixer(1, m, *norm1[m], hook=hook)
        gate_grad(1, m, lambda at, v, m=m: r.out_grads[m, at, :].astype(F32))
        branch_grad(1, m)
        mixer_grad(1, m, 3 + m)
        upper_sum[m].start()

    gate_weights(1, r.mine_0)
    out_weights(1, r.mine_0, width)
    in_weights(1, r.mine_0, width + states)
    upper_sum[1].turn()
    upper_batch.to_core()
    layer_rows(1, 7)
    layer_sum[1].start()

    upper_total = [None, None]
    for m in range(2):
        upper_total[m] = upper_sum[m].total()
        gain, first, second, inv = stream_grad(1, m, upper_total[m], counts[m], norm1[m][1])

        def second_grad(at, v, m=m, gain=gain, first=first, second=second, inv=inv):
            grad_normed = r.grad_scaled[1, m, at, :] * gain
            normed = r.normed[1, m, at, :]
            grad_stream = inv * (grad_normed - v * (first + normed * second))
            out_grad = r.out_grads[m, at, :].astype(F32)
            grad = (out_grad + grad_stream.astype(BF16).astype(F32)).astype(BF16)
            r.grad_second[m, at, :] = grad
            return grad.astype(F32)

        gate_grad(0, m, second_grad)
        if m == 0:
            upper_batch.to_quad()
            layer_sum[1].turn()
        else:
            lower_sum[0].turn()
            upper_batch.to_groups()
        branch_grad(0, m)
        if m == 1:
            gate_weights(0, r.mine_1)
            out_weights(0, r.mine_1, width)
            gate_batch.to_core()
        mixer_grad(0, m, 5 + m)
        lower_sum[m].start()

    in_weights(0, r.mine_2, 0)
    in_batch.to_core()
    layer_rows(0, 8)
    layer_sum[0].start()
    gate_batch.to_quad()
    lower_sum[1].turn()
    in_batch.to_quad()
    layer_sum[0].turn()
    upper_batch.to_sections()
    mixed_rows(0)
    gate_batch.to_groups()
    mixed_rows(1)
    in_batch.to_groups()
    upper_batch.to_sibling()

    lower_total = [None, None]
    for m in range(2):
        lower_total[m] = lower_sum[m].total()
        gain, first, second, inv = stream_grad(0, m, lower_total[m], counts[m], norm0[m][1])
        for k, row in enumerate((gain, first, second, inv)):
            r.rows[k : k + 1, :] = row
        gain, first, second, inv = [r.rows[k : k + 1, own_columns] for k in range(4)]

        def token_grad(t, carry, m=m, gain=gain, first=first, second=second, inv=inv):
            at = pl.ds(pl.multiple_of(t * chunk, chunk), chunk)
            grad_normed = r.grad_scaled[0, m, at, own_columns] * gain
            normed = r.normed[0, m, at, own_columns]
            grad_stream = inv * (grad_normed - r.valid[m, at, :] * (first + normed * second))
            grad = r.grad_second[m, at, own_columns].astype(F32) + grad_stream
            high = grad.astype(BF16)
            r.narrow[at, :] = high
            r.narrow_rest[at, :] = (grad - high.astype(F32)).astype(BF16)
            return carry

        lax.fori_loop(0, rows // chunk, token_grad, 0)
        r.token_grad[m] = matmul(r.gather[...], r.narrow[...]) + matmul(
            r.gather[...], r.narrow_rest[...]
        )
        if m == 0:
            gate_batch.to_sections()
            upper_batch.to_result(r.result_0, r.result_sem.at[0])

    in_batch.to_sections()
    gate_batch.to_sibling()
    for l, sums in ((0, lower_total), (1, upper_total)):
        r.small[l, 0:8, :] = (sums[0] + sums[1])[0:8, :]
        r.small[l, 8:24, :] = layer_sum[l].total()[0:16, :]
    gate_batch.to_result(r.result_1, r.result_sem.at[1])
    in_batch.to_sibling()
    in_batch.to_result(r.result_2, r.result_sem.at[2])
    for batch in batches:
        batch.end()


def lay_out_kernel(cfg, *refs):
    upper, gate_out, into, small, mixed, token_grad = refs[:6]
    (
        mixed_out,
        token_grad_out,
        gain_out,
        bias_out,
        decay_out,
        freq_out,
        step_out,
        in_out,
        out_out,
        skip_out,
        gate_out_out,
        gbias_out,
    ) = refs[6:]
    width, states, half = cfg.width, cfg.states, cfg.half
    mixed_out[...] = mixed[...]
    token_grad_out[...] = token_grad[...]
    for l in range(2):
        for out, first, count in (
            (bias_out, 0, 4),
            (gain_out, 4, 4),
            (skip_out, 8, 4),
            (gbias_out, 12, 4),
        ):
            out[l : l + 1, :] = unfold(small[l], first, count)
        for out, first in ((decay_out, 16), (freq_out, 18), (step_out, 20)):
            out[l : l + 1, :] = unfold(small[l], first, 2)[:, 0:half]
    tall = states // (2 * QUAD)
    for l in range(2):
        for s in range(cfg.sections):
            for c in range(2):
                for z in range(QUAD):
                    at = s * 128 + (c * QUAD + z) * 16
                    if l == 1:
                        piece = upper[c, s, z]
                        gate_part = piece[:, 0:width]
                        out_part = piece[:, width : width + states]
                        in_part = piece[:, width + states :]
                    else:
                        gate_part = gate_out[c, s, z, :, 0:width]
                        out_part = gate_out[c, s, z, :, width:]
                        in_part = into[c, s, z]
                    gate_out_out[l, at : at + 16, :] = gate_part.astype(F32)
                    in_out[l, at : at + 16, :] = in_part.astype(F32)
                    for k in range(tall // 16):
                        first = (c * QUAD + z) * tall + 16 * k
                        out_out[l, first : first + 16, s * 128 : (s + 1) * 128] = out_part[
                            :, k * 128 : (k + 1) * 128
                        ].astype(F32)


INPUTS = tuple(
    dict(tokens=0, lengths=0, out_grad=0, gain=0, bias=0, decay=0, freq=0, lstep=0, b_in=0, c_out=0, skip=0, gmat=0, gbias=0)
)


def per_device(cfg, *args):
    rows, width, states, lanes = cfg.rows, cfg.width, cfg.states, cfg.lanes
    sections, chips = cfg.sections, cfg.dp // 2
    groups = chips // QUAD
    steps = rows // SUB
    vmem, dma = pltpu.VMEM, pltpu.SemaphoreType.DMA
    widths = (width + 2 * states, width + states, states)
    outs = {f"result_{k}": ((2, sections, QUAD, 16, w), BF16) for k, w in enumerate(widths)}
    outs.update(
        small=((2, 24, 128), F32), mixed=((2, rows, 128), BF16), token_grad=((2, rows, 128), F32)
    )
    scratch = dict(
        sum_own=vmem((REDUCES, 24, 128), F32),
        sum_sibling=vmem((REDUCES, 24, 128), F32),
        sum_slots=vmem((REDUCES, chips, 24, 128), F32),
        sum_send=dma((REDUCES, chips)),
        sum_recv=dma((REDUCES, chips)),
        grad_send=dma((3, 2 * QUAD + sections + groups)),
        grad_recv=dma((3, 2 * QUAD + sections + groups)),
        result_sem=dma((3,)),
        spread=vmem((rows, rows), BF16),
        gather=vmem((rows, rows), BF16),
        first_in=vmem((2, rows, width), BF16),
        out_grads=vmem((2, rows, width), BF16),
        second_in=vmem((2, rows, width), F32),
        grad_second=vmem((2, rows, width), BF16),
        valid=vmem((2, rows, 128), F32),
        keep_start=vmem((2, rows, 128), F32),
        keep_end=vmem((2, rows, 128), F32),
        par=vmem((SUB, lanes), F32),
        b_pad=vmem((2, width, 2 * lanes), BF16),
        c_pad=vmem((2, 2 * lanes, width), BF16),
        normed=vmem((2, 2, rows, width), F32),
        scaled=vmem((2, 2 * rows, width), BF16),
        drive=vmem((2, 2, rows, 2 * lanes), F32),
        state=vmem((2, 2, (steps + 1) * SUB, 2 * lanes), F32),
        joined=vmem((2, 2 * rows, 2 * lanes), BF16),
        work=vmem((rows, width), F32),
        active=vmem((2, 2, rows, width), F32),
        active_low=vmem((2, 2 * rows, width), BF16),
        slope=vmem((2, 2, rows, width), F32),
        sig=vmem((2, 2, rows, width), F32),
        through=vmem((rows, width), F32),
        grad_logits=vmem((2, 2 * rows, width), BF16),
        branch=vmem((2, 2 * rows, width), BF16),
        grad_drive=vmem((2, 2 * rows, states), BF16),
        grad_scaled=vmem((2, 2, rows, width), F32),
        state_sums=vmem((2, 2, 4, SUB, lanes), F32),
        narrow=vmem((rows, 128), BF16),
        narrow_rest=vmem((rows, 128), BF16),
        rows=vmem((SUB, width), F32),
    )
    for k, w in enumerate(widths):
        blocks = (2, QUAD), (QUAD,), (QUAD,), (QUAD,), (groups,), (2, sections, QUAD)
        for part, block in zip(STAGES, blocks):
            scratch[f"{part}_{k}"] = vmem((*block, 16, w), BF16)
    in_vmem = pl.BlockSpec(memory_space=pltpu.VMEM)
    in_smem = pl.BlockSpec(memory_space=pltpu.SMEM)
    anywhere = pl.BlockSpec(memory_space=pl.ANY)
    names = INPUTS + tuple(outs) + tuple(scratch)
    made = pl.pallas_call(
        partial(main_kernel, cfg, names),
        name="layers",
        out_shape=[jax.ShapeDtypeStruct(*spec) for spec in outs.values()],
        in_specs=[in_smem if name == "lengths" else in_vmem for name in INPUTS],
        out_specs=[anywhere if name.startswith("result") else in_vmem for name in outs],
        scratch_shapes=list(scratch.values()),
        compiler_params=pltpu.CompilerParams(
            collective_id=0, has_side_effects=True, vmem_limit_bytes=56 * 2**20
        ),
    )(*args)
    shapes = [
        ((2, rows, 128), BF16),
        ((2, rows, 128), F32),
        ((2, width), F32),
        ((2, width), F32),
        ((2, states // 2), F32),
        ((2, states // 2), F32),
        ((2, states // 2), F32),
        ((2, width, states), F32),
        ((2, states, width), F32),
        ((2, width), F32),
        ((2, width, width), F32),
        ((2, width), F32),
    ]
    return pl.pallas_call(
        partial(lay_out_kernel, cfg),
        name="lay_out",
        out_shape=[jax.ShapeDtypeStruct(*spec) for spec in shapes],
        in_specs=[in_vmem] * 6,
        out_specs=[in_vmem] * 12,
        compiler_params=pltpu.CompilerParams(vmem_limit_bytes=40 * 2**20),
    )(*made)


def solution(mesh):
    sections, dp = mesh.shape["section"], mesh.shape["dp"]

    def run(*args):
        _, rows, width = args[0].shape
        states = args[8].shape[2]
        cfg = SimpleNamespace(
            rows=rows // dp,
            width=width,
            states=states,
            half=states // 2,
            lanes=-(-states // 256) * 128,
            sections=sections,
            dp=dp,
        )
        split = P(None, "dp", None)
        shared = P()
        placed = P(None, "dp", "section")
        return jax.shard_map(
            partial(per_device, cfg),
            mesh=mesh,
            in_specs=(split, P(None, "dp"), split) + (shared,) * 10,
            out_specs=(placed, placed) + (shared,) * 10,
            check_vma=False,
        )(*args)

    return run
```

profile of v0, /device:TPU:0, one launch (start us, length us, event | category | flops | bytes accessed | tf_op | source)
XLA Modules:
  0.0 72.9 jit_solution(10768186268007708537)
XLA Ops:
  0.6 63.5 %layers.1 = (bf16[2,4,4,16,1280]{4,3,2,1,0:T(8,128)(2,1)}, bf16[2,4,4,16,896]{4,3,2,1,0:T(8,128)(2,1)}, bf16[2,4,4,16,384]{4,3,2,1,0:T(8,128)(2,1)}, f32[2,24,12...) custom-call(bf16[2,256,512]{2,1,0:T(8,128)(2,1)} %refs_0_.1, s32[2,2]{1,0:T(2,128)} %refs_1_.1, ...), custom_call_target="tpu_custom_call" | custom-call | tf_op jit(solution)/shard_map/layers/pallas_call | solution.py:930
  64.2 0.0 copy-start
  64.2 1.3 %copy-done = bf16[2,4,4,16,1280]{4,3,2,1,0:T(8,128)(2,1)S(1)} copy-done((bf16[2,4,4,16,1280]{4,3,2,1,0:T(8,128)(2,1)S(1)}, bf16[2,4,4,16,1280]{4,3,2,1,0:T(8,128)(2,1)}, u32[]{:S(2)}) %copy-start) | copy-done | bytes 1310744
  65.5 0.0 copy-start.1
  65.5 1.2 %copy-done.1 = bf16[2,4,4,16,896]{4,3,2,1,0:T(8,128)(2,1)S(1)} copy-done((bf16[2,4,4,16,896]{4,3,2,1,0:T(8,128)(2,1)S(1)}, bf16[2,4,4,16,896]{4,3,2,1,0:T(8,128)(2,1)}, u32[]{:S(2)}) %copy-start.1) | copy-done | bytes 917528
  66.7 0.0 copy-start.2
  66.7 1.0 %copy-done.2 = bf16[2,4,4,16,384]{4,3,2,1,0:T(8,128)(2,1)S(1)} copy-done((bf16[2,4,4,16,384]{4,3,2,1,0:T(8,128)(2,1)S(1)}, bf16[2,4,4,16,384]{4,3,2,1,0:T(8,128)(2,1)}, u32[]{:S(2)}) %copy-start.2) | copy-done | bytes 393240
  67.7 0.0 copy-start.3
  67.7 0.9 %copy-done.3 = f32[2,256,128]{2,1,0:T(8,128)S(1)} copy-done((f32[2,256,128]{2,1,0:T(8,128)S(1)}, f32[2,256,128]{2,1,0:T(8,128)}, u32[]{:S(2)}) %copy-start.3) | copy-done | bytes 262168
  68.6 0.0 copy-start.4
  68.6 0.9 %copy-done.4 = bf16[2,256,128]{2,1,0:T(8,128)(2,1)S(1)} copy-done((bf16[2,256,128]{2,1,0:T(8,128)(2,1)S(1)}, bf16[2,256,128]{2,1,0:T(8,128)(2,1)}, u32[]{:S(2)}) %copy-start.4) | copy-done | bytes 131096
  69.5 0.0 copy-start.5
  69.5 0.7 %copy-done.5 = f32[2,24,128]{2,1,0:T(8,128)S(1)} copy-done((f32[2,24,128]{2,1,0:T(8,128)S(1)}, f32[2,24,128]{2,1,0:T(8,128)}, u32[]{:S(2)}) %copy-start.5) | copy-done | bytes 24600
  70.3 2.7 %lay_out.1 = (bf16[2,256,128]{2,1,0:T(8,128)(2,1)}, f32[2,256,128]{2,1,0:T(8,128)}, f32[2,512]{1,0:T(2,128)}, f32[2,512]{1,0:T(2,128)}, f32[2,192]{1,0:T(2,128)}...) custom-call(bf16[2,4,4,16,1280]{4,3,2,1,0:T(8,128)(2,1)S(1)} %copy-d, ...), custom_call_target="tpu_custom_call" | custom-call | tf_op jit(solution)/shard_map/lay_out/pallas_call | solution.py:955
Async XLA Ops:
  64.2 1.3 %copy-start = (bf16[2,4,4,16,1280]{4,3,2,1,0:T(8,128)(2,1)S(1)}, bf16[2,4,4,16,1280]{4,3,2,1,0:T(8,128)(2,1)}, u32[]{:S(2)}) copy-start(bf16[2,4,4,16,1280]{4,3,2,1,0:T(8,128)(2,1)} %get-tuple-element.18.refs_0_) | copy-start | bytes 3932164
  65.5 1.2 %copy-start.1 = (bf16[2,4,4,16,896]{4,3,2,1,0:T(8,128)(2,1)S(1)}, bf16[2,4,4,16,896]{4,3,2,1,0:T(8,128)(2,1)}, u32[]{:S(2)}) copy-start(bf16[2,4,4,16,896]{4,3,2,1,0:T(8,128)(2,1)} %get-tuple-element.19.refs_1_) | copy-start | bytes 2752516
  66.7 1.0 %copy-start.2 = (bf16[2,4,4,16,384]{4,3,2,1,0:T(8,128)(2,1)S(1)}, bf16[2,4,4,16,384]{4,3,2,1,0:T(8,128)(2,1)}, u32[]{:S(2)}) copy-start(bf16[2,4,4,16,384]{4,3,2,1,0:T(8,128)(2,1)} %get-tuple-element.20.refs_2_) | copy-start | bytes 1179652
  67.7 0.9 %copy-start.3 = (f32[2,256,128]{2,1,0:T(8,128)S(1)}, f32[2,256,128]{2,1,0:T(8,128)}, u32[]{:S(2)}) copy-start(f32[2,256,128]{2,1,0:T(8,128)} %get-tuple-element.23.refs_5_) | copy-start | bytes 786436
  68.6 0.9 %copy-start.4 = (bf16[2,256,128]{2,1,0:T(8,128)(2,1)S(1)}, bf16[2,256,128]{2,1,0:T(8,128)(2,1)}, u32[]{:S(2)}) copy-start(bf16[2,256,128]{2,1,0:T(8,128)(2,1)} %get-tuple-element.22.refs_4_) | copy-start | bytes 393220
  69.5 0.7 %copy-start.5 = (f32[2,24,128]{2,1,0:T(8,128)S(1)}, f32[2,24,128]{2,1,0:T(8,128)}, u32[]{:S(2)}) copy-start(f32[2,24,128]{2,1,0:T(8,128)} %get-tuple-element.21.refs_3_) | copy-start | bytes 73732
where the time goes:
time: 73.3 us; the launch traced here: 72.9 us
  Pallas kernels  66.2 us (90%)
  local copies, waits for them, and re-layouts  6.07 us (8%)
    pallas_call x1, Pallas kernels, per_device(): pl.pallas_call(partial(main_kernel, cfg, names), name='layers', out_shape...  63.5 us
    unnamed x12, local copies, waits for them, and re-layouts  6.07 us
    pallas_call x1, Pallas kernels, per_device(): pl.pallas_call(partial(lay_out_kernel, cfg), name='lay_out', out_shape=[j...  2.68 us

commit v1 on v0

--- a/solution.py
+++ b/solution.py
@@ -163,34 +163,38 @@
         piece = self.full.at[at.core, at.section, at.quad]
         piece[...] = total.astype(BF16)
         self.copies = [
-            self.remote(piece, piece, (at.section, at.quad_peer(step)))
-            for step in range(1, QUAD)
+            self.remote(piece, piece, (at.section, at.quad_peer(step))) for step in range(1, QUAD)
         ]
-
-    def to_sections(self):
+        self.spread = [self.over_sections(at.quad)]
+
+    def over_sections(self, quad):
         at = self.place
-        for copy in self.copies:
-            copy.wait()
-        piece = self.full.at[at.core, at.section]
-        self.copies = [
+        piece = self.full.at[at.core, at.section, quad]
+        return [
             self.remote(piece, piece, (lax.rem(at.section + step, at.sections), at.dp))
             for step in range(1, at.sections)
         ]
 
+    def to_sections(self):
+        at = self.place
+        for step in range(1, QUAD):
+            self.copies[step - 1].wait()
+            self.spread.append(self.over_sections(lax.rem(at.quad + QUAD - step, QUAD)))
+        piece = self.full.at[at.core, at.section]
+        self.last = [self.remote(piece, piece, (at.section, at.sibling))]
+
     def to_sibling(self):
         at = self.place
-        for copy in self.copies:
+        for step in range(1, at.sections):
+            for copies in self.spread:
+                copies[step - 1].wait()
+            other = lax.rem(at.section + at.sections - step, at.sections)
+            piece = self.full.at[at.core, other]
+            self.last.append(self.remote(piece, piece, (at.section, at.sibling)))
+
+    def end(self):
+        for copy in self.last:
             copy.wait()
-        piece = self.full.at[at.core]
-        self.copy = self.remote(piece, piece, (at.section, at.sibling))
-
-    def to_result(self, result, sem):
-        self.copy.wait()
-        self.out = pltpu.make_async_copy(self.full, result, sem)
-        self.out.start()
-
-    def end(self):
-        self.out.wait()
 
 
 def main_kernel(cfg, names, *refs):
@@ -255,9 +259,21 @@
             r.grad_recv,
             k,
         )
-        for k in range(3)
+        for k in range(4)
     ]
-    upper_batch, gate_batch, in_batch = batches
+    upper_gate, upper_in, lower_gate, lower_in = batches
+
+    fetched = []
+    for k, (held, given) in enumerate(
+        (
+            (r.b_in, r.b_in_far),
+            (r.out_grad, r.out_grad_far),
+            (r.c_out, r.c_out_far),
+            (r.gmat, r.gmat_far),
+        )
+    ):
+        fetched.append(pltpu.make_async_copy(given, held, r.fetch_sem.at[k]))
+        fetched[k].start()
 
     first_len = [r.lengths[m, 0] for m in range(2)]
     total_len = [r.lengths[m, 0] + r.lengths[m, 1] for m in range(2)]
@@ -297,6 +313,7 @@
     for m in range(2):
         r.first_in[m] = matmul(r.spread[...], r.tokens[m]).astype(BF16)
     first_sum.turn()
+    fetched[1].wait()
     for m in range(2):
         r.out_grads[m] = matmul(r.spread[...], r.out_grad[m]).astype(BF16)
     held = lax.broadcasted_iota(jnp.int32, (rows, 128), 0)
@@ -336,22 +353,14 @@
     low_lanes = lane < half - 128
     turn_by = half - 128
 
+    from_column = lax.broadcasted_iota(jnp.int32, (states, 2 * lanes), 0)
+    to_column = lax.broadcasted_iota(jnp.int32, (states, 2 * lanes), 1)
+    moved_to = jnp.where(from_column < half, from_column, from_column + (lanes - half))
+    r.widen[...] = jnp.where(to_column == moved_to, 1.0, 0.0).astype(BF16)
+    for k in (0, 2, 3):
+        fetched[k].wait()
     for l in range(2):
-
-        def pad_in(t, carry, l=l):
-            at = pl.ds(pl.multiple_of(t * chunk, chunk), chunk)
-            tile = [r.b_in[l, at, k * 128 : (k + 1) * 128].astype(F32) for k in range(3)]
-            rolled = [pltpu.roll(x, 64, 1) for x in tile[1:]]
-            padded = [
-                tile[0],
-                jnp.where(low_lanes, tile[1], 0.0),
-                jnp.where(low_lanes, rolled[0], rolled[1]),
-                jnp.where(low_lanes, rolled[1], 0.0),
-            ]
-            r.b_pad[l, at, :] = jnp.concatenate(padded, axis=1).astype(BF16)
-            return carry
-
-        lax.fori_loop(0, width // chunk, pad_in, 0)
+        r.b_pad[l] = matmul(r.b_in[l], r.widen[...]).astype(BF16)
         blank = jnp.zeros((lanes - half, width), BF16)
         r.c_pad[l, 0:half, :] = r.c_out[l, 0:half, :]
         r.c_pad[l, half:lanes, :] = blank
@@ -447,8 +456,8 @@
         def ends(t, carry):
             p = steps - 1 - t if reverse else t
             at = group_rows(p)
-            q_re = r.work[at, 0:lanes]
-            q_im = r.work[at, lanes : 2 * lanes]
+            q_re = r.q[m, at, 0:lanes]
+            q_im = r.q[m, at, lanes : 2 * lanes]
             return advance(keep, m, at, br, bi, *carry, q_re, q_im)
 
         end = lax.fori_loop(0, steps, ends, (zero, zero), unroll=4)
@@ -460,8 +469,8 @@
             for k in range(2):
                 p = steps - 1 - (2 * t + k) if reverse else 2 * t + k
                 at, near = group_rows(p), group_rows(p + back)
-                q_re = r.work[at, 0:lanes]
-                q_im = r.work[at, lanes : 2 * lanes]
+                q_re = r.q[m, at, 0:lanes]
+                q_im = r.q[m, at, lanes : 2 * lanes]
                 w = advance(keep, m, at, br, bi, *w, q_re, q_im)
                 kept = repeat_lanes(keep_state[m, at, :], lanes // 128)
                 near_re = kept * r.state[l, m, near, 0:lanes]
@@ -524,9 +533,9 @@
         lax.fori_loop(0, rows // chunk, normalise, 0)
         r.drive[l, m] = matmul(r.scaled[l, micro_rows(m), :], r.b_pad[l])
         scan_states(l, m)
-        r.work[...] = matmul(r.joined[l, micro_rows(m), :], r.c_pad[l])
         if hook is not None:
             hook()
+        r.work[...] = matmul(r.joined[l, micro_rows(m), :], r.c_pad[l])
 
         def activate(t, carry):
             at = pl.ds(pl.multiple_of(t * gelu_chunk, gelu_chunk), gelu_chunk)
@@ -603,11 +612,13 @@
 
         zero = jnp.zeros((SUB, width), F32)
         skip_sums[l, m] = lax.fori_loop(0, rows // chunk, branch, zero)
-        r.work[...] = matmul_nt(r.branch[l, micro_rows(m), :], r.c_pad[l])
-
-    def mixer_grad(l, m, index):
+        r.q[m] = matmul_nt(r.branch[l, micro_rows(m), :], r.c_pad[l])
+
+    def mixer_grad(l, m, index, hook=None):
         skip = row_of(r.skip, l)
         scan_grads(l, m)
+        if hook is not None:
+            hook()
         r.work[...] = matmul_nt(r.grad_drive[l, micro_rows(m), :], r.b_in[l])
 
         def scaled_grad(t, carry):
@@ -715,23 +726,21 @@
         mixer(1, m, *norm1[m], hook=hook)
         gate_grad(1, m, lambda at, v, m=m: r.out_grads[m, at, :].astype(F32))
         branch_grad(1, m)
-        mixer_grad(1, m, 3 + m)
+        if m == 1:
+            gate_weights(1, r.mine_0)
+            out_weights(1, r.mine_0, width)
+            upper_gate.to_core()
+        mixer_grad(1, m, 3 + m, hook=upper_gate.to_quad if m == 1 else None)
         upper_sum[m].start()
 
-    gate_weights(1, r.mine_0)
-    out_weights(1, r.mine_0, width)
-    in_weights(1, r.mine_0, width + states)
-    upper_sum[1].turn()
-    upper_batch.to_core()
+    in_weights(1, r.mine_1, 0)
+    upper_in.to_core()
     layer_rows(1, 7)
-    layer_sum[1].start()
-
-    upper_total = [None, None]
-    for m in range(2):
-        upper_total[m] = upper_sum[m].total()
-        gain, first, second, inv = stream_grad(1, m, upper_total[m], counts[m], norm1[m][1])
-
-        def second_grad(at, v, m=m, gain=gain, first=first, second=second, inv=inv):
+
+    def second_grad(m, total):
+        gain, first, second, inv = stream_grad(1, m, total, counts[m], norm1[m][1])
+
+        def grad_of(at, v):
             grad_normed = r.grad_scaled[1, m, at, :] * gain
             normed = r.normed[1, m, at, :]
             grad_stream = inv * (grad_normed - v * (first + normed * second))
@@ -740,35 +749,43 @@
             r.grad_second[m, at, :] = grad
             return grad.astype(F32)
 
-        gate_grad(0, m, second_grad)
-        if m == 0:
-            upper_batch.to_quad()
-            layer_sum[1].turn()
-        else:
-            lower_sum[0].turn()
-            upper_batch.to_groups()
-        branch_grad(0, m)
-        if m == 1:
-            gate_weights(0, r.mine_1)
-            out_weights(0, r.mine_1, width)
-            gate_batch.to_core()
-        mixer_grad(0, m, 5 + m)
-        lower_sum[m].start()
-
-    in_weights(0, r.mine_2, 0)
-    in_batch.to_core()
+        return grad_of
+
+    upper_total = [upper_sum[0].total()]
+    gate_grad(0, 0, second_grad(0, upper_total[0]))
+    upper_sum[1].turn()
+    upper_in.to_quad()
+    layer_sum[1].start()
+    branch_grad(0, 0)
+    upper_gate.to_groups()
+    mixer_grad(0, 0, 5, hook=layer_sum[1].turn)
+    lower_sum[0].start()
+    upper_in.to_groups()
+    upper_total.append(upper_sum[1].total())
+    gate_grad(0, 1, second_grad(1, upper_total[1]))
+    lower_sum[0].turn()
+    branch_grad(0, 1)
+    gate_weights(0, r.mine_2)
+    out_weights(0, r.mine_2, width)
+    lower_gate.to_core()
+    upper_gate.to_sections()
+    mixer_grad(0, 1, 6, hook=lower_gate.to_quad)
+    lower_sum[1].start()
+    in_weights(0, r.mine_3, 0)
+    lower_in.to_core()
+    upper_in.to_sections()
     layer_rows(0, 8)
     layer_sum[0].start()
-    gate_batch.to_quad()
     lower_sum[1].turn()
-    in_batch.to_quad()
+    lower_in.to_quad()
     layer_sum[0].turn()
-    upper_batch.to_sections()
     mixed_rows(0)
-    gate_batch.to_groups()
+    lower_gate.to_groups()
     mixed_rows(1)
-    in_batch.to_groups()
-    upper_batch.to_sibling()
+    upper_gate.to_sibling()
+    lower_in.to_groups()
+    upper_in.to_sibling()
+    lower_gate.to_sections()
 
     lower_total = [None, None]
     for m in range(2):
@@ -794,23 +811,20 @@
             r.gather[...], r.narrow_rest[...]
         )
         if m == 0:
-            gate_batch.to_sections()
-            upper_batch.to_result(r.result_0, r.result_sem.at[0])
-
-    in_batch.to_sections()
-    gate_batch.to_sibling()
+            lower_in.to_sections()
+
     for l, sums in ((0, lower_total), (1, upper_total)):
         r.small[l, 0:8, :] = (sums[0] + sums[1])[0:8, :]
         r.small[l, 8:24, :] = layer_sum[l].total()[0:16, :]
-    gate_batch.to_result(r.result_1, r.result_sem.at[1])
-    in_batch.to_sibling()
-    in_batch.to_result(r.result_2, r.result_sem.at[2])
+    lower_gate.to_sibling()
+    lower_in.to_sibling()
     for batch in batches:
         batch.end()
 
 
 def lay_out_kernel(cfg, *refs):
-    upper, gate_out, into, small, mixed, token_grad = refs[:6]
+    full = refs[0:4]
+    small, mixed, token_grad = refs[4:7]
     (
         mixed_out,
         token_grad_out,
@@ -822,48 +836,54 @@
         in_out,
         out_out,
         skip_out,
-        gate_out_out,
+        gate_out,
         gbias_out,
-    ) = refs[6:]
+    ) = refs[7:19]
+    in_held, out_held, gate_held = refs[19:22]
+    rows_held, sems = refs[22:29], refs[29]
     width, states, half = cfg.width, cfg.states, cfg.half
-    mixed_out[...] = mixed[...]
-    token_grad_out[...] = token_grad[...]
-    for l in range(2):
-        for out, first, count in (
-            (bias_out, 0, 4),
-            (gain_out, 4, 4),
-            (skip_out, 8, 4),
-            (gbias_out, 12, 4),
-        ):
-            out[l : l + 1, :] = unfold(small[l], first, count)
-        for out, first in ((decay_out, 16), (freq_out, 18), (step_out, 20)):
-            out[l : l + 1, :] = unfold(small[l], first, 2)[:, 0:half]
     tall = states // (2 * QUAD)
-    for l in range(2):
-        for s in range(cfg.sections):
-            for c in range(2):
-                for z in range(QUAD):
-                    at = s * 128 + (c * QUAD + z) * 16
-                    if l == 1:
-                        piece = upper[c, s, z]
-                        gate_part = piece[:, 0:width]
-                        out_part = piece[:, width : width + states]
-                        in_part = piece[:, width + states :]
-                    else:
-                        gate_part = gate_out[c, s, z, :, 0:width]
-                        out_part = gate_out[c, s, z, :, width:]
-                        in_part = into[c, s, z]
-                    gate_out_out[l, at : at + 16, :] = gate_part.astype(F32)
-                    in_out[l, at : at + 16, :] = in_part.astype(F32)
-                    for k in range(tall // 16):
-                        first = (c * QUAD + z) * tall + 16 * k
-                        out_out[l, first : first + 16, s * 128 : (s + 1) * 128] = out_part[
-                            :, k * 128 : (k + 1) * 128
-                        ].astype(F32)
+    copies = []
+
+    def send(held, out):
+        copies.append(pltpu.make_async_copy(held, out, sems.at[len(copies)]))
+        copies[-1].start()
+
+    send(mixed, mixed_out)
+    send(token_grad, token_grad_out)
+    row_outs = (bias_out, gain_out, skip_out, gbias_out, decay_out, freq_out, step_out)
+    for k, (held, out) in enumerate(zip(rows_held, row_outs)):
+        for l in range(2):
+            if k < 4:
+                held[l : l + 1, :] = unfold(small[l], 4 * k, 4)
+            else:
+                held[l : l + 1, :] = unfold(small[l], 8 + 2 * k, 2)[:, 0:half]
+        send(held, out)
+
+    places = [(s, c, z) for s in range(cfg.sections) for c in range(2) for z in range(QUAD)]
+    for l in (1, 0):
+        gates, ins = full[2 - 2 * l], full[3 - 2 * l]
+        for s, c, z in places:
+            at = s * 128 + (c * QUAD + z) * 16
+            gate_held[l, at : at + 16, :] = gates[c, s, z, :, 0:width].astype(F32)
+        send(gate_held.at[l], gate_out.at[l])
+        for s, c, z in places:
+            for k in range(tall // 16):
+                first = (c * QUAD + z) * tall + 16 * k
+                out_held[l, first : first + 16, s * 128 : (s + 1) * 128] = gates[
+                    c, s, z, :, width + k * 128 : width + (k + 1) * 128
+                ].astype(F32)
+        send(out_held.at[l], out_out.at[l])
+        for s, c, z in places:
+            at = s * 128 + (c * QUAD + z) * 16
+            in_held[l, at : at + 16, :] = ins[c, s, z].astype(F32)
+        send(in_held.at[l], in_out.at[l])
+    for copy in copies:
+        copy.wait()
 
 
 INPUTS = tuple(
-    dict(tokens=0, lengths=0, out_grad=0, gain=0, bias=0, decay=0, freq=0, lstep=0, b_in=0, c_out=0, skip=0, gmat=0, gbias=0)
+    dict(tokens=0, lengths=0, out_grad_far=0, gain=0, bias=0, decay=0, freq=0, lstep=0, b_in_far=0, c_out_far=0, skip=0, gmat_far=0, gbias=0)
 )
 
 
@@ -873,8 +893,8 @@
     groups = chips // QUAD
     steps = rows // SUB
     vmem, dma = pltpu.VMEM, pltpu.SemaphoreType.DMA
-    widths = (width + 2 * states, width + states, states)
-    outs = {f"result_{k}": ((2, sections, QUAD, 16, w), BF16) for k, w in enumerate(widths)}
+    widths = (width + states, states) * 2
+    outs = {f"full_{k}": ((2, sections, QUAD, 16, w), BF16) for k, w in enumerate(widths)}
     outs.update(
         small=((2, 24, 128), F32), mixed=((2, rows, 128), BF16), token_grad=((2, rows, 128), F32)
     )
@@ -884,9 +904,15 @@
         sum_slots=vmem((REDUCES, chips, 24, 128), F32),
         sum_send=dma((REDUCES, chips)),
         sum_recv=dma((REDUCES, chips)),
-        grad_send=dma((3, 2 * QUAD + sections + groups)),
-        grad_recv=dma((3, 2 * QUAD + sections + groups)),
-        result_sem=dma((3,)),
+        grad_send=dma((4, (2 + sections) * QUAD + groups)),
+        grad_recv=dma((4, (2 + sections) * QUAD + groups)),
+        fetch_sem=dma((4,)),
+        b_in=vmem((2, width, states), BF16),
+        c_out=vmem((2, states, width), BF16),
+        gmat=vmem((2, width, width), BF16),
+        out_grad=vmem((2, rows, width), BF16),
+        widen=vmem((states, 2 * lanes), BF16),
+        q=vmem((2, rows, 2 * lanes), F32),
         spread=vmem((rows, rows), BF16),
         gather=vmem((rows, rows), BF16),
         first_in=vmem((2, rows, width), BF16),
@@ -920,19 +946,22 @@
         rows=vmem((SUB, width), F32),
     )
     for k, w in enumerate(widths):
-        blocks = (2, QUAD), (QUAD,), (QUAD,), (QUAD,), (groups,), (2, sections, QUAD)
+        blocks = (2, QUAD), (QUAD,), (QUAD,), (QUAD,), (groups,)
         for part, block in zip(STAGES, blocks):
             scratch[f"{part}_{k}"] = vmem((*block, 16, w), BF16)
     in_vmem = pl.BlockSpec(memory_space=pltpu.VMEM)
     in_smem = pl.BlockSpec(memory_space=pltpu.SMEM)
-    anywhere = pl.BlockSpec(memory_space=pl.ANY)
+    in_hbm = pl.BlockSpec(memory_space=pltpu.HBM)
     names = INPUTS + tuple(outs) + tuple(scratch)
     made = pl.pallas_call(
         partial(main_kernel, cfg, names),
         name="layers",
-        out_shape=[jax.ShapeDtypeStruct(*spec) for spec in outs.values()],
-        in_specs=[in_smem if name == "lengths" else in_vmem for name in INPUTS],
-        out_specs=[anywhere if name.startswith("result") else in_vmem for name in outs],
+        out_shape=[vmem(*spec) for spec in outs.values()],
+        in_specs=[
+            in_smem if name == "lengths" else in_hbm if name.endswith("_far") else in_vmem
+            for name in INPUTS
+        ],
+        out_specs=[in_vmem for name in outs],
         scratch_shapes=list(scratch.values()),
         compiler_params=pltpu.CompilerParams(
             collective_id=0, has_side_effects=True, vmem_limit_bytes=56 * 2**20
@@ -952,13 +981,18 @@
         ((2, width, width), F32),
         ((2, width), F32),
     ]
+    by_copy = (7, 8, 10)
     return pl.pallas_call(
         partial(lay_out_kernel, cfg),
         name="lay_out",
         out_shape=[jax.ShapeDtypeStruct(*spec) for spec in shapes],
-        in_specs=[in_vmem] * 6,
-        out_specs=[in_vmem] * 12,
-        compiler_params=pltpu.CompilerParams(vmem_limit_bytes=40 * 2**20),
+        in_specs=[in_vmem] * 7,
+        out_specs=[in_hbm] * 12,
+        scratch_shapes=[vmem(*shapes[k]) for k in by_copy]
+        + [vmem((2, width), F32)] * 4
+        + [vmem((2, states // 2), F32)] * 3
+        + [dma((15,))],
+        compiler_params=pltpu.CompilerParams(vmem_limit_bytes=24 * 2**20),
     )(*made)
 
 

time: 73.3 us -> 61.9 us (0.84)
  local copies, waits for them, and re-layouts: 6.07 us -> 0 us
  Pallas kernels: 66.2 us -> 61.1 us
    unnamed x12 -> x0, local copies, waits for them, and re-layouts: 6.07 us -> none
    pallas_call x1, Pallas kernels: 63.5 us -> 58.4 us  [per_device(): pl.pallas_call(partial(main_kernel, cfg, names), name='layers', out_shape...]
where the time goes in v1:
time: 61.9 us; the launch traced here: 61.7 us
  Pallas kernels  61.1 us (99%)
  between operations  0.66 us (1%)
    pallas_call x1, Pallas kernels, per_device(): pl.pallas_call(partial(main_kernel, cfg, names), name='layers', out_shape...  58.4 us
    pallas_call x1, Pallas kernels, per_device(): pl.pallas_call(partial(lay_out_kernel, cfg), name='lay_out', out_shape=[j...  2.64 us

profile of v1, /device:TPU:0, one launch (start us, length us, event | category | flops | bytes accessed | tf_op | source)
XLA Modules:
  0.0 61.7 jit_solution(17047550542399103354)
XLA Ops:
  0.6 58.4 %layers.1 = (bf16[2,4,4,16,896]{4,3,2,1,0:T(8,128)(2,1)S(1)}, bf16[2,4,4,16,384]{4,3,2,1,0:T(8,128)(2,1)S(1)}, bf16[2,4,4,16,896]{4,3,2,1,0:T(8,128)(2,1)S(1)}, ...) custom-call(bf16[2,256,512]{2,1,0:T(8,128)(2,1)} %refs_0_.1, ...), custom_call_target="tpu_custom_call" | custom-call | tf_op jit(solution)/shard_map/layers/pallas_call | solution.py:956
  59.1 2.6 %lay_out.1 = (bf16[2,256,128]{2,1,0:T(8,128)(2,1)}, f32[2,256,128]{2,1,0:T(8,128)}, f32[2,512]{1,0:T(2,128)}, f32[2,512]{1,0:T(2,128)}, f32[2,192]{1,0:T(2,128)}...) custom-call(bf16[2,4,4,16,896]{4,3,2,1,0:T(8,128)(2,1)S(1)} %get-tup, ...), custom_call_target="tpu_custom_call" | custom-call | tf_op jit(solution)/shard_map/lay_out/pallas_call | solution.py:985

commit v2 on v1

--- a/solution.py
+++ b/solution.py
@@ -14,7 +14,8 @@
 BF16 = jnp.bfloat16
 SUB = 8
 QUAD = 4
-REDUCES = 9
+LATE_STATES = 3
+SUM_ROWS = (24, 8, 8, 8, 8, 16)
 
 
 STAGES = tuple(dict(mine=0, theirs=0, chip=0, quad=0, group=0, full=0))
@@ -36,6 +37,12 @@
     return ar * br - ai * bi, ar * bi + ai * br
 
 
+def sweep(count, body, carry):
+    for t in range(count):
+        carry = body(t, carry)
+    return carry
+
+
 def repeat_lanes(x, times):
     return jnp.concatenate([x] * times, axis=1)
 
@@ -49,46 +56,49 @@
 
 
 class SmallSum:
-    def __init__(self, place, own, sibling, slots, send_sems, recv_sems, index):
-        self.place, self.own, self.sibling, self.slots = place, own, sibling, slots
+    def __init__(self, place, direct, own, sibling, slots, send_sems, recv_sems, index):
+        self.place, self.direct = place, direct
+        self.own, self.sibling, self.slots = own, sibling, slots
         self.send_sems, self.recv_sems, self.index = send_sems, recv_sems, index
+
+    def remote(self, src, dst, step, device):
+        copy = pltpu.make_async_remote_copy(
+            src_ref=src,
+            dst_ref=dst,
+            send_sem=self.send_sems.at[self.index, step],
+            recv_sem=self.recv_sems.at[self.index, step],
+            device_id=(self.place.section, device),
+            device_id_type=MESH,
+        )
+        copy.start()
+        return copy
+
+    def to_all(self, slot, members, peer):
+        self.members = members
+        block = self.slots.at[slot]
+        self.copies = [self.remote(block, block, step, peer(step)) for step in range(1, members)]
 
     def start(self):
         at = self.place
-        self.copy = pltpu.make_async_remote_copy(
-            src_ref=self.own,
-            dst_ref=self.sibling,
-            send_sem=self.send_sems.at[self.index, 0],
-            recv_sem=self.recv_sems.at[self.index, 0],
-            device_id=(at.section, at.sibling),
-            device_id_type=MESH,
-        )
-        self.copy.start()
+        if self.direct:
+            self.slots[at.dp] = self.own[...]
+            self.to_all(at.dp, at.devices, at.dp_peer)
+        else:
+            self.copy = self.remote(self.own, self.sibling, 0, at.sibling)
 
     def turn(self):
         at = self.place
-        self.copy.wait()
-        chip = at.chip
-        self.slots[chip] = self.own[...] + self.sibling[...]
-        self.copies = []
-        for step in range(1, at.chips):
-            copy = pltpu.make_async_remote_copy(
-                src_ref=self.slots.at[chip],
-                dst_ref=self.slots.at[chip],
-                send_sem=self.send_sems.at[self.index, step],
-                recv_sem=self.recv_sems.at[self.index, step],
-                device_id=(at.section, at.chip_peer(step)),
-                device_id_type=MESH,
-            )
-            copy.start()
-            self.copies.append(copy)
+        if not self.direct:
+            self.copy.wait()
+            self.slots[at.chip] = self.own[...] + self.sibling[...]
+            self.to_all(at.chip, at.chips, at.chip_peer)
 
     def total(self):
         for copy in self.copies:
             copy.wait()
         result = self.slots[0]
-        for chip in range(1, self.place.chips):
-            result = result + self.slots[chip]
+        for member in range(1, self.members):
+            result = result + self.slots[member]
         return result
 
 
@@ -222,13 +232,19 @@
         quad=quad,
         group=group,
         groups=chips // QUAD,
+        devices=cfg.dp,
+        dp_peer=lambda step: lax.rem(dp + step, cfg.dp),
         sibling=dp + 1 - 2 * core,
         chip_peer=lambda step: lax.rem(chip + step, chips) * 2 + core,
         quad_peer=lambda step: (group * QUAD + lax.rem(quad + step, QUAD)) * 2 + core,
     )
 
-    peers = [(section, place.sibling)]
-    peers += [(section, place.chip_peer(step)) for step in range(1, chips)]
+    direct = cfg.dp <= 8
+    if direct:
+        peers = [(section, place.dp_peer(step)) for step in range(1, cfg.dp)]
+    else:
+        peers = [(section, place.sibling)]
+        peers += [(section, place.chip_peer(step)) for step in range(1, chips)]
     peers += [(lax.rem(section + step, cfg.sections), dp) for step in range(1, cfg.sections)]
     barrier = pltpu.get_barrier_semaphore()
     for peer in peers:
@@ -237,20 +253,20 @@
     small = [
         SmallSum(
             place,
-            r.sum_own.at[k],
-            r.sum_sibling.at[k],
-            r.sum_slots.at[k],
+            direct and k < len(SUM_ROWS) - 1,
+            r.sum_own.at[k, 0:tall] if k < len(SUM_ROWS) - 1 else r.late_own.at[section],
+            r.sum_sibling.at[k, 0:tall],
+            r.sum_slots.at[k, :, 0:tall],
             r.sum_send,
             r.sum_recv,
             k,
         )
-        for k in range(REDUCES)
+        for k, tall in enumerate(SUM_ROWS)
     ]
     first_sum = small[0]
     mid_sum = [small[1], small[2]]
     upper_sum = [small[3], small[4]]
-    lower_sum = [small[5], small[6]]
-    layer_sum = [small[8], small[7]]
+    late_sum = small[5]
     batches = [
         GradSum(
             place,
@@ -282,18 +298,22 @@
         for k in range(row.shape[1] // 128):
             r.sum_own[index, at + k : at + k + 1, :] = row[:, k * 128 : (k + 1) * 128]
 
+    def put_late(at, row):
+        for k in range(cfg.sections):
+            r.late_own[k, at : at + 1, :] = row[:, k * 128 : (k + 1) * 128]
+
     chunk = 32
     for m in range(2):
 
         def token_sums(t, carry, m=m):
-            at = pl.ds(pl.multiple_of(t * chunk, chunk), chunk)
+            at = pl.ds(t * chunk, chunk)
             v = r.tokens[m, at, :].astype(F32)
             place_row = t * chunk + lax.broadcasted_iota(jnp.int32, (chunk, width), 0)
             kept = jnp.where(place_row < total_len[m], v, 0.0)
             return carry[0] + fold_rows(kept), carry[1] + fold_rows(kept * v)
 
         zero = jnp.zeros((SUB, width), F32)
-        sums, squares = lax.fori_loop(0, rows // chunk, token_sums, (zero, zero))
+        sums, squares = sweep(rows // chunk, token_sums, (zero, zero))
         put(0, 8 * m, jnp.sum(sums, axis=0, keepdims=True))
         put(0, 8 * m + 4, jnp.sum(squares, axis=0, keepdims=True))
         count = jnp.minimum(total_len[m], rows).astype(F32)
@@ -389,7 +409,7 @@
         return jnp.broadcast_to(x[l : l + 1, :], (SUB, x.shape[1]))
 
     def group_rows(p):
-        return pl.ds(pl.multiple_of(p * SUB, SUB), SUB)
+        return pl.ds(p * SUB, SUB)
 
     def scan_coefs(l, m, reverse):
         keep = r.keep_end if reverse else r.keep_start
@@ -420,7 +440,7 @@
             r.state[l, m, group_rows(p + lead), lanes : 2 * lanes] = src_im
             return advance(keep, m, at, br, bi, *carry, src_re, src_im)
 
-        end = lax.fori_loop(0, steps, ends, (zero, zero), unroll=4)
+        end = sweep(steps, ends, (zero, zero))
         enter = across(end, product, reverse)
         first = steps if reverse else 0
         r.state[l, m, first * SUB : (first + 1) * SUB, 0:lanes] = enter[0]
@@ -439,11 +459,11 @@
                 done.append(jnp.concatenate([carry[0], -carry[1]], axis=1))
             pair = steps // 2 - 1 - t if reverse else t
             both = jnp.concatenate(done[::-1] if reverse else done, axis=0)
-            to = pl.ds(pl.multiple_of(m * rows + pair * 16, 16), 16)
+            to = pl.ds(m * rows + pair * 16, 16)
             r.joined[l, to, :] = both.astype(BF16)
             return carry
 
-        lax.fori_loop(0, steps // 2, fill, enter, unroll=2)
+        sweep(steps // 2, fill, enter)
 
     def scan_grads(l, m):
         reverse = l == 0
@@ -460,7 +480,7 @@
             q_im = r.q[m, at, lanes : 2 * lanes]
             return advance(keep, m, at, br, bi, *carry, q_re, q_im)
 
-        end = lax.fori_loop(0, steps, ends, (zero, zero), unroll=4)
+        end = sweep(steps, ends, (zero, zero))
         enter = across(end, product, reverse)
 
         def fill(t, carry):
@@ -498,12 +518,12 @@
                 )
             pair = steps // 2 - 1 - t if reverse else t
             both = jnp.concatenate(done[::-1] if reverse else done, axis=0)
-            to = pl.ds(pl.multiple_of(m * rows + pair * 16, 16), 16)
+            to = pl.ds(m * rows + pair * 16, 16)
             r.grad_drive[l, to, :] = both.astype(BF16)
             return w, bar_sum, fac_sum
 
         none = (zero, zero)
-        _, bar_sum, fac_sum = lax.fori_loop(0, steps // 2, fill, (enter, none, none), unroll=2)
+        _, bar_sum, fac_sum = sweep(steps // 2, fill, (enter, none, none))
         for k, part in enumerate((*bar_sum, *fac_sum)):
             r.state_sums[l, m, k] = part
 
@@ -519,18 +539,18 @@
         gain, bias, skip = row_of(r.gain, l), row_of(r.bias, l), row_of(r.skip, l)
 
         def normalise(t, carry):
-            at = pl.ds(pl.multiple_of(t * chunk, chunk), chunk)
+            at = pl.ds(t * chunk, chunk)
             if l == 0:
                 v = r.first_in[m, at, :].astype(F32)
             else:
                 v = r.second_in[m, at, :]
             normed = (v - center) * inv
             r.normed[l, m, at, :] = normed
-            to = pl.ds(pl.multiple_of(m * rows + t * chunk, chunk), chunk)
+            to = pl.ds(m * rows + t * chunk, chunk)
             r.scaled[l, to, :] = (normed * gain + bias).astype(BF16)
             return carry
 
-        lax.fori_loop(0, rows // chunk, normalise, 0)
+        sweep(rows // chunk, normalise, 0)
         r.drive[l, m] = matmul(r.scaled[l, micro_rows(m), :], r.b_pad[l])
         scan_states(l, m)
         if hook is not None:
@@ -538,7 +558,7 @@
         r.work[...] = matmul(r.joined[l, micro_rows(m), :], r.c_pad[l])
 
         def activate(t, carry):
-            at = pl.ds(pl.multiple_of(t * gelu_chunk, gelu_chunk), gelu_chunk)
+            at = pl.ds(t * gelu_chunk, gelu_chunk)
             scaled = r.normed[l, m, at, :] * gain + bias
             y = (2.0 * r.work[at, :] + skip * scaled).astype(BF16).astype(F32)
             below = 0.5 + 0.5 * lax.erf(y * 0.7071067811865476)
@@ -546,18 +566,18 @@
             active = y * below
             r.active[l, m, at, :] = active
             r.slope[l, m, at, :] = below + y * density
-            to = pl.ds(pl.multiple_of(m * rows + t * gelu_chunk, gelu_chunk), gelu_chunk)
+            to = pl.ds(m * rows + t * gelu_chunk, gelu_chunk)
             r.active_low[l, to, :] = active.astype(BF16)
             return carry
 
-        lax.fori_loop(0, rows // gelu_chunk, activate, 0)
+        sweep(rows // gelu_chunk, activate, 0)
         r.work[...] = matmul(r.active_low[l, micro_rows(m), :], r.gmat[l])
 
     def first_gate(m):
         gbias = row_of(r.gbias, 0)
 
         def gate(t, carry):
-            at = pl.ds(pl.multiple_of(t * gelu_chunk, gelu_chunk), gelu_chunk)
+            at = pl.ds(t * gelu_chunk, gelu_chunk)
             opened = jax.nn.sigmoid(r.work[at, :] + gbias)
             r.sig[0, m, at, :] = opened
             v = repeat_lanes(r.valid[m, at, :], width // 128)
@@ -568,7 +588,7 @@
             return carry[0] + fold_rows(kept), carry[1] + fold_rows(kept * second)
 
         zero = jnp.zeros((SUB, width), F32)
-        sums, squares = lax.fori_loop(0, rows // gelu_chunk, gate, (zero, zero))
+        sums, squares = sweep(rows // gelu_chunk, gate, (zero, zero))
         put(1 + m, 0, jnp.sum(sums, axis=0, keepdims=True))
         put(1 + m, 4, jnp.sum(squares, axis=0, keepdims=True))
 
@@ -579,7 +599,7 @@
         gbias = row_of(r.gbias, l)
 
         def gate(t, carry):
-            at = pl.ds(pl.multiple_of(t * gelu_chunk, gelu_chunk), gelu_chunk)
+            at = pl.ds(t * gelu_chunk, gelu_chunk)
             if l == 1:
                 opened = jax.nn.sigmoid(r.work[at, :] + gbias)
                 r.sig[1, m, at, :] = opened
@@ -590,31 +610,31 @@
             through = masked * opened
             r.through[at, :] = through
             grad_logits = through * r.active[l, m, at, :] * (1.0 - opened)
-            to = pl.ds(pl.multiple_of(m * rows + t * gelu_chunk, gelu_chunk), gelu_chunk)
+            to = pl.ds(m * rows + t * gelu_chunk, gelu_chunk)
             r.grad_logits[l, to, :] = grad_logits.astype(BF16)
             return carry + fold_rows(grad_logits)
 
         zero = jnp.zeros((SUB, width), F32)
-        bias_sums[l, m] = lax.fori_loop(0, rows // gelu_chunk, gate, zero)
+        bias_sums[l, m] = sweep(rows // gelu_chunk, gate, zero)
 
     def branch_grad(l, m):
         gain, bias = row_of(r.gain, l), row_of(r.bias, l)
         r.work[...] = matmul_nt(r.grad_logits[l, micro_rows(m), :], r.gmat[l])
 
         def branch(t, carry):
-            at = pl.ds(pl.multiple_of(t * chunk, chunk), chunk)
+            at = pl.ds(t * chunk, chunk)
             grad_active = r.through[at, :] + r.work[at, :]
             g = (r.slope[l, m, at, :] * grad_active).astype(BF16)
-            to = pl.ds(pl.multiple_of(m * rows + t * chunk, chunk), chunk)
+            to = pl.ds(m * rows + t * chunk, chunk)
             r.branch[l, to, :] = g
             scaled = r.normed[l, m, at, :] * gain + bias
             return carry + fold_rows(g.astype(F32) * scaled)
 
         zero = jnp.zeros((SUB, width), F32)
-        skip_sums[l, m] = lax.fori_loop(0, rows // chunk, branch, zero)
+        skip_sums[l, m] = sweep(rows // chunk, branch, zero)
         r.q[m] = matmul_nt(r.branch[l, micro_rows(m), :], r.c_pad[l])
 
-    def mixer_grad(l, m, index, hook=None):
+    def mixer_grad(l, m, hook=None):
         skip = row_of(r.skip, l)
         scan_grads(l, m)
         if hook is not None:
@@ -622,17 +642,23 @@
         r.work[...] = matmul_nt(r.grad_drive[l, micro_rows(m), :], r.b_in[l])
 
         def scaled_grad(t, carry):
-            at = pl.ds(pl.multiple_of(t * chunk, chunk), chunk)
-            to = pl.ds(pl.multiple_of(m * rows + t * chunk, chunk), chunk)
+            at = pl.ds(t * chunk, chunk)
+            to = pl.ds(m * rows + t * chunk, chunk)
             grad = r.work[at, :] + skip * r.branch[l, to, :].astype(F32)
             r.grad_scaled[l, m, at, :] = grad
             normed = r.normed[l, m, at, :]
             return carry[0] + fold_rows(grad), carry[1] + fold_rows(grad * normed)
 
         zero = jnp.zeros((SUB, width), F32)
-        sums, products = lax.fori_loop(0, rows // chunk, scaled_grad, (zero, zero))
-        put(index, 0, jnp.sum(sums, axis=0, keepdims=True))
-        put(index, 4, jnp.sum(products, axis=0, keepdims=True))
+        sums, products = sweep(rows // chunk, scaled_grad, (zero, zero))
+        sums = jnp.sum(sums, axis=0, keepdims=True)
+        products = jnp.sum(products, axis=0, keepdims=True)
+        if l == 1:
+            put(3 + m, 0, sums)
+            put(3 + m, 4, products)
+        else:
+            put_late(2 * m, sums)
+            put_late(2 * m + 1, products)
 
     def moments(total, at, count):
         center = unfold(total, at, 4) / count
@@ -660,12 +686,12 @@
         grad = matmul_tn(r.scaled[l, :, own_columns], r.grad_drive[l])
         ref[:, :, :, at : at + states] = grad.astype(BF16).reshape(2, QUAD, 16, states)
 
-    def layer_rows(l, index):
+    def layer_rows(l):
         def both(sums):
             return jnp.sum(sums[l, 0] + sums[l, 1], axis=0, keepdims=True)
 
-        put(index, 0, both(skip_sums))
-        put(index, 4, both(bias_sums))
+        put_late(4 + 2 * l, both(skip_sums))
+        put_late(5 + 2 * l, both(bias_sums))
         part = [
             jnp.sum(r.state_sums[l, 0, k] + r.state_sums[l, 1, k], axis=0, keepdims=True)
             for k in range(4)
@@ -683,13 +709,17 @@
         gl_im = size * (b_re * gb_im - b_im * gb_re) + (d_re * gf_im - d_im * gf_re)
         e_re, e_im = cmul(lam_re, lam_im, b_re, b_im)
         g_step = size * ((e_re * gb_re + e_im * gb_im) + (b_re * gf_re + b_im * gf_im))
-        put(index, 8, -gl_re)
-        put(index, 10, gl_im)
-        put(index, 12, g_step)
+        parts = [
+            row[:, k : k + 128] for row in (-gl_re, gl_im, g_step) for k in range(0, lanes, 128)
+        ]
+        for k, row in enumerate(parts):
+            k += l * len(parts)
+            at = 8 + k % LATE_STATES
+            r.late_own[k // LATE_STATES, at : at + 1, :] = row
 
     def mixed_rows(m):
         def mix(t, carry):
-            at = pl.ds(pl.multiple_of(t * chunk, chunk), chunk)
+            at = pl.ds(t * chunk, chunk)
             gated = (
                 r.valid[m, at, :]
                 * r.active[1, m, at, own_columns]
@@ -699,7 +729,7 @@
             r.narrow[at, :] = (stream + gated).astype(BF16)
             return carry
 
-        lax.fori_loop(0, rows // chunk, mix, 0)
+        sweep(rows // chunk, mix, 0)
         r.mixed[m] = matmul(r.gather[...], r.narrow[...]).astype(BF16)
 
     def stream_grad(l, m, total, count, inv):
@@ -722,7 +752,7 @@
     norm1 = [None, None]
     for m in range(2):
         norm1[m] = moments(mid_sum[m].total(), 0, counts[m])
-        hook = mid_sum[1].turn if m == 0 else upper_sum[0].turn
+        hook = mid_sum[1].turn if m == 0 else None
         mixer(1, m, *norm1[m], hook=hook)
         gate_grad(1, m, lambda at, v, m=m: r.out_grads[m, at, :].astype(F32))
         branch_grad(1, m)
@@ -730,12 +760,14 @@
             gate_weights(1, r.mine_0)
             out_weights(1, r.mine_0, width)
             upper_gate.to_core()
-        mixer_grad(1, m, 3 + m, hook=upper_gate.to_quad if m == 1 else None)
+        mixer_grad(1, m)
         upper_sum[m].start()
+        upper_sum[m].turn()
 
     in_weights(1, r.mine_1, 0)
     upper_in.to_core()
-    layer_rows(1, 7)
+    upper_gate.to_quad()
+    layer_rows(1)
 
     def second_grad(m, total):
         gain, first, second, inv = stream_grad(1, m, total, counts[m], norm1[m][1])
@@ -753,51 +785,62 @@
 
     upper_total = [upper_sum[0].total()]
     gate_grad(0, 0, second_grad(0, upper_total[0]))
-    upper_sum[1].turn()
     upper_in.to_quad()
-    layer_sum[1].start()
     branch_grad(0, 0)
-    upper_gate.to_groups()
-    mixer_grad(0, 0, 5, hook=layer_sum[1].turn)
-    lower_sum[0].start()
-    upper_in.to_groups()
+    mixer_grad(0, 0)
     upper_total.append(upper_sum[1].total())
     gate_grad(0, 1, second_grad(1, upper_total[1]))
-    lower_sum[0].turn()
     branch_grad(0, 1)
+    upper_gate.to_groups()
     gate_weights(0, r.mine_2)
     out_weights(0, r.mine_2, width)
     lower_gate.to_core()
-    upper_gate.to_sections()
-    mixer_grad(0, 1, 6, hook=lower_gate.to_quad)
-    lower_sum[1].start()
+    mixer_grad(0, 1)
+    lower_gate.to_quad()
     in_weights(0, r.mine_3, 0)
     lower_in.to_core()
+    layer_rows(0)
+    late_sum.start()
+    upper_in.to_groups()
+    lower_in.to_quad()
+    late_sum.turn()
+    mixed_rows(0)
+    mixed_rows(1)
+    upper_gate.to_sections()
+    lower_gate.to_groups()
+    lower_in.to_groups()
     upper_in.to_sections()
-    layer_rows(0, 8)
-    layer_sum[0].start()
-    lower_sum[1].turn()
-    lower_in.to_quad()
-    layer_sum[0].turn()
-    mixed_rows(0)
-    lower_gate.to_groups()
-    mixed_rows(1)
+    lower_gate.to_sections()
+    lower_in.to_sections()
     upper_gate.to_sibling()
-    lower_in.to_groups()
     upper_in.to_sibling()
-    lower_gate.to_sections()
-
-    lower_total = [None, None]
+
+    late = late_sum.total()
+    r.late[section] = late
+    to_sections = [
+        pltpu.make_async_remote_copy(
+            src_ref=r.late.at[section],
+            dst_ref=r.late.at[section],
+            send_sem=r.late_send.at[step],
+            recv_sem=r.late_recv.at[step],
+            device_id=(lax.rem(section + step, cfg.sections), dp),
+            device_id_type=MESH,
+        )
+        for step in range(1, cfg.sections)
+    ]
+    for copy in to_sections:
+        copy.start()
+    own_gain = r.gain[0:1, own_columns]
     for m in range(2):
-        lower_total[m] = lower_sum[m].total()
-        gain, first, second, inv = stream_grad(0, m, lower_total[m], counts[m], norm0[m][1])
-        for k, row in enumerate((gain, first, second, inv)):
-            r.rows[k : k + 1, :] = row
-        gain, first, second, inv = [r.rows[k : k + 1, own_columns] for k in range(4)]
-
-        def token_grad(t, carry, m=m, gain=gain, first=first, second=second, inv=inv):
-            at = pl.ds(pl.multiple_of(t * chunk, chunk), chunk)
-            grad_normed = r.grad_scaled[0, m, at, own_columns] * gain
+        count = counts[m][:, 0:128]
+        first = own_gain * late[2 * m : 2 * m + 1, :] / count
+        second = own_gain * late[2 * m + 1 : 2 * m + 2, :] / count
+        r.rows[m : m + 1, :] = norm0[m][1]
+        inv = r.rows[m : m + 1, own_columns]
+
+        def token_grad(t, carry, m=m, first=first, second=second, inv=inv):
+            at = pl.ds(t * chunk, chunk)
+            grad_normed = r.grad_scaled[0, m, at, own_columns] * own_gain
             normed = r.normed[0, m, at, own_columns]
             grad_stream = inv * (grad_normed - r.valid[m, at, :] * (first + normed * second))
             grad = r.grad_second[m, at, own_columns].astype(F32) + grad_stream
@@ -806,16 +849,13 @@
             r.narrow_rest[at, :] = (grad - high.astype(F32)).astype(BF16)
             return carry
 
-        lax.fori_loop(0, rows // chunk, token_grad, 0)
+        sweep(rows // chunk, token_grad, 0)
         r.token_grad[m] = matmul(r.gather[...], r.narrow[...]) + matmul(
             r.gather[...], r.narrow_rest[...]
         )
-        if m == 0:
-            lower_in.to_sections()
-
-    for l, sums in ((0, lower_total), (1, upper_total)):
-        r.small[l, 0:8, :] = (sums[0] + sums[1])[0:8, :]
-        r.small[l, 8:24, :] = layer_sum[l].total()[0:16, :]
+    r.upper_norm[...] = upper_total[0] + upper_total[1]
+    for copy in to_sections:
+        copy.wait()
     lower_gate.to_sibling()
     lower_in.to_sibling()
     for batch in batches:
@@ -824,7 +864,7 @@
 
 def lay_out_kernel(cfg, *refs):
     full = refs[0:4]
-    small, mixed, token_grad = refs[4:7]
+    late, upper_norm, mixed, token_grad = refs[4:8]
     (
         mixed_out,
         token_grad_out,
@@ -838,9 +878,9 @@
         skip_out,
         gate_out,
         gbias_out,
-    ) = refs[7:19]
-    in_held, out_held, gate_held = refs[19:22]
-    rows_held, sems = refs[22:29], refs[29]
+    ) = refs[8:20]
+    in_held, out_held, gate_held = refs[20:23]
+    rows_held, sems = refs[23:30], refs[30]
     width, states, half = cfg.width, cfg.states, cfg.half
     tall = states // (2 * QUAD)
     copies = []
@@ -851,13 +891,23 @@
 
     send(mixed, mixed_out)
     send(token_grad, token_grad_out)
+    def columns(at):
+        return jnp.concatenate([late[s, at : at + 1, :] for s in range(cfg.sections)], axis=1)
+
     row_outs = (bias_out, gain_out, skip_out, gbias_out, decay_out, freq_out, step_out)
-    for k, (held, out) in enumerate(zip(rows_held, row_outs)):
+    values = [
+        (columns(0) + columns(2), unfold(upper_norm, 0, 4)),
+        (columns(1) + columns(3), unfold(upper_norm, 4, 4)),
+        (columns(4), columns(6)),
+        (columns(5), columns(7)),
+    ]
+    for k in range(3):
+        places = [(6 * l + 2 * k + part) for l in range(2) for part in range(2)]
+        row = [late[p // LATE_STATES, 8 + p % LATE_STATES, :][None] for p in places]
+        values.append([jnp.concatenate(row[2 * l : 2 * l + 2], axis=1)[:, 0:half] for l in range(2)])
+    for held, out, value in zip(rows_held, row_outs, values):
         for l in range(2):
-            if k < 4:
-                held[l : l + 1, :] = unfold(small[l], 4 * k, 4)
-            else:
-                held[l : l + 1, :] = unfold(small[l], 8 + 2 * k, 2)[:, 0:half]
+            held[l : l + 1, :] = value[l]
         send(held, out)
 
     places = [(s, c, z) for s in range(cfg.sections) for c in range(2) for z in range(QUAD)]
@@ -889,21 +939,24 @@
 
 def per_device(cfg, *args):
     rows, width, states, lanes = cfg.rows, cfg.width, cfg.states, cfg.lanes
-    sections, chips = cfg.sections, cfg.dp // 2
+    sections, dp, chips = cfg.sections, cfg.dp, cfg.dp // 2
     groups = chips // QUAD
     steps = rows // SUB
     vmem, dma = pltpu.VMEM, pltpu.SemaphoreType.DMA
     widths = (width + states, states) * 2
     outs = {f"full_{k}": ((2, sections, QUAD, 16, w), BF16) for k, w in enumerate(widths)}
     outs.update(
-        small=((2, 24, 128), F32), mixed=((2, rows, 128), BF16), token_grad=((2, rows, 128), F32)
+        late=((sections, 16, 128), F32), upper_norm=((8, 128), F32), mixed=((2, rows, 128), BF16), token_grad=((2, rows, 128), F32)
     )
     scratch = dict(
-        sum_own=vmem((REDUCES, 24, 128), F32),
-        sum_sibling=vmem((REDUCES, 24, 128), F32),
-        sum_slots=vmem((REDUCES, chips, 24, 128), F32),
-        sum_send=dma((REDUCES, chips)),
-        sum_recv=dma((REDUCES, chips)),
+        sum_own=vmem((len(SUM_ROWS), 24, 128), F32),
+        sum_sibling=vmem((len(SUM_ROWS), 24, 128), F32),
+        sum_slots=vmem((len(SUM_ROWS), min(dp, max(chips, 8)), 24, 128), F32),
+        late_own=vmem((sections, 16, 128), F32),
+        late_send=dma((sections,)),
+        late_recv=dma((sections,)),
+        sum_send=dma((len(SUM_ROWS), max(chips, 8))),
+        sum_recv=dma((len(SUM_ROWS), max(chips, 8))),
         grad_send=dma((4, (2 + sections) * QUAD + groups)),
         grad_recv=dma((4, (2 + sections) * QUAD + groups)),
         fetch_sem=dma((4,)),
@@ -986,7 +1039,7 @@
         partial(lay_out_kernel, cfg),
         name="lay_out",
         out_shape=[jax.ShapeDtypeStruct(*spec) for spec in shapes],
-        in_specs=[in_vmem] * 7,
+        in_specs=[in_vmem] * 8,
         out_specs=[in_hbm] * 12,
         scratch_shapes=[vmem(*shapes[k]) for k in by_copy]
         + [vmem((2, width), F32)] * 4

time: 61.9 us -> 53.9 us (0.87)
  Pallas kernels: 61.1 us -> 53 us
    pallas_call x1, Pallas kernels: 58.4 us -> 50.3 us  [per_device(): pl.pallas_call(partial(main_kernel, cfg, names), name='layers', out_shape...]
where the time goes in v2:
time: 53.9 us; the launch traced here: 53.8 us
  Pallas kernels  53 us (98%)
  between operations  0.82 us (2%)
    pallas_call x1, Pallas kernels, per_device(): pl.pallas_call(partial(main_kernel, cfg, names), name='layers', out_shape...  50.3 us
    pallas_call x1, Pallas kernels, per_device(): pl.pallas_call(partial(lay_out_kernel, cfg), name='lay_out', out_shape=[j...  2.65 us

profile of v2, /device:TPU:0, one launch (start us, length us, event | category | flops | bytes accessed | tf_op | source)
XLA Modules:
  0.0 53.8 jit_solution(10272779002744727364)
XLA Ops:
  0.6 50.3 %layers.1 = (bf16[2,4,4,16,896]{4,3,2,1,0:T(8,128)(2,1)S(1)}, bf16[2,4,4,16,384]{4,3,2,1,0:T(8,128)(2,1)S(1)}, bf16[2,4,4,16,896]{4,3,2,1,0:T(8,128)(2,1)S(1)}, ...) custom-call(bf16[2,256,512]{2,1,0:T(8,128)(2,1)} %refs_0_.1, ...), custom_call_target="tpu_custom_call" | custom-call | tf_op jit(solution)/shard_map/layers/pallas_call | solution.py:1009
  51.0 2.6 %lay_out.1 = (bf16[2,256,128]{2,1,0:T(8,128)(2,1)}, f32[2,256,128]{2,1,0:T(8,128)}, f32[2,512]{1,0:T(2,128)}, f32[2,512]{1,0:T(2,128)}, f32[2,192]{1,0:T(2,128)}...) custom-call(bf16[2,4,4,16,896]{4,3,2,1,0:T(8,128)(2,1)S(1)} %get-tup, ...), custom_call_target="tpu_custom_call" | custom-call | tf_op jit(solution)/shard_map/lay_out/pallas_call | solution.py:1038

commit v3 on v2

--- a/solution.py
+++ b/solution.py
@@ -55,28 +55,33 @@
     return jnp.concatenate([total[first + k : first + k + 1, :] for k in range(count)], axis=1)
 
 
+def landed(block, sem):
+    pltpu.make_async_copy(block, block, sem).wait()
+
+
+def remote(src, dst, send_sem, recv_sem, device):
+    pltpu.make_async_remote_copy(
+        src_ref=src,
+        dst_ref=dst,
+        send_sem=send_sem,
+        recv_sem=recv_sem,
+        device_id=device,
+        device_id_type=MESH,
+    ).start()
+
+
 class SmallSum:
-    def __init__(self, place, direct, own, sibling, slots, send_sems, recv_sems, index):
+    def __init__(self, place, direct, own, sibling, slots, send_sems, recv_sems):
         self.place, self.direct = place, direct
         self.own, self.sibling, self.slots = own, sibling, slots
-        self.send_sems, self.recv_sems, self.index = send_sems, recv_sems, index
-
-    def remote(self, src, dst, step, device):
-        copy = pltpu.make_async_remote_copy(
-            src_ref=src,
-            dst_ref=dst,
-            send_sem=self.send_sems.at[self.index, step],
-            recv_sem=self.recv_sems.at[self.index, step],
-            device_id=(self.place.section, device),
-            device_id_type=MESH,
-        )
-        copy.start()
-        return copy
+        self.send_sems, self.recv_sems = send_sems, recv_sems
 
     def to_all(self, slot, members, peer):
         self.members = members
         block = self.slots.at[slot]
-        self.copies = [self.remote(block, block, step, peer(step)) for step in range(1, members)]
+        for step in range(1, members):
+            to = (self.place.section, peer(step))
+            remote(block, block, self.send_sems.at[1], self.recv_sems.at[1], to)
 
     def start(self):
         at = self.place
@@ -84,127 +89,109 @@
             self.slots[at.dp] = self.own[...]
             self.to_all(at.dp, at.devices, at.dp_peer)
         else:
-            self.copy = self.remote(self.own, self.sibling, 0, at.sibling)
+            to = (at.section, at.sibling)
+            remote(self.own, self.sibling, self.send_sems.at[0], self.recv_sems.at[0], to)
 
     def turn(self):
         at = self.place
         if not self.direct:
-            self.copy.wait()
+            landed(self.sibling, self.recv_sems.at[0])
             self.slots[at.chip] = self.own[...] + self.sibling[...]
             self.to_all(at.chip, at.chips, at.chip_peer)
 
     def total(self):
-        for copy in self.copies:
-            copy.wait()
+        landed(self.slots.at[0 : self.members - 1], self.recv_sems.at[1])
         result = self.slots[0]
         for member in range(1, self.members):
             result = result + self.slots[member]
         return result
 
+    def end(self):
+        if not self.direct:
+            landed(self.own, self.send_sems.at[0])
+        landed(self.slots.at[0 : self.members - 1], self.send_sems.at[1])
+
 
 class GradSum:
-    def __init__(self, place, refs, send_sems, recv_sems, index):
+    def __init__(self, place, refs, send_sems, recv_sems):
         self.place = place
         self.mine, self.theirs, self.chip_part, self.quad_in, self.group_in, self.full = refs
-        self.send_sems, self.recv_sems, self.index = send_sems, recv_sems, index
-        self.sem = 0
-
-    def remote(self, src, dst, device):
-        copy = pltpu.make_async_remote_copy(
-            src_ref=src,
-            dst_ref=dst,
-            send_sem=self.send_sems.at[self.index, self.sem],
-            recv_sem=self.recv_sems.at[self.index, self.sem],
-            device_id=device,
-            device_id_type=MESH,
-        )
-        self.sem += 1
-        copy.start()
-        return copy
+        self.send_sems, self.recv_sems = send_sems, recv_sems
+
+    def send(self, src, dst, send, recv, device):
+        remote(src, dst, self.send_sems.at[send], self.recv_sems.at[recv], device)
 
     def to_core(self):
         at = self.place
-        self.copy = self.remote(
-            self.mine.at[1 - at.core], self.theirs, (at.section, at.sibling)
-        )
+        self.send(self.mine.at[1 - at.core], self.theirs, 0, 0, (at.section, at.sibling))
 
     def to_quad(self):
         at = self.place
-        self.copy.wait()
+        landed(self.theirs, self.recv_sems.at[0])
         for part in range(QUAD):
             both = self.mine[at.core, part].astype(F32) + self.theirs[part].astype(F32)
             self.chip_part[part] = both.astype(BF16)
-        self.copies = []
         for step in range(1, QUAD):
             other = lax.rem(at.quad + step, QUAD)
-            self.copies.append(
-                self.remote(
-                    self.chip_part.at[other],
-                    self.quad_in.at[at.quad],
-                    (at.section, at.quad_peer(step)),
-                )
-            )
+            to = (at.section, at.quad_peer(step))
+            self.send(self.chip_part.at[other], self.quad_in.at[at.quad], 1, 1, to)
         self.quad_in[at.quad] = self.chip_part[at.quad]
 
     def to_groups(self):
         at = self.place
-        for copy in self.copies:
-            copy.wait()
+        landed(self.quad_in.at[0 : QUAD - 1], self.recv_sems.at[1])
         total = self.quad_in[0].astype(F32)
         for part in range(1, QUAD):
             total = total + self.quad_in[part].astype(F32)
         if at.groups > 1:
-            group = at.group
-            self.group_in[group] = total.astype(BF16)
-            copies = []
+            mine = self.group_in.at[at.group]
+            mine[...] = total.astype(BF16)
             for step in range(1, at.groups):
-                copies.append(
-                    self.remote(
-                        self.group_in.at[group],
-                        self.group_in.at[group],
-                        (at.section, at.chip_peer(step * QUAD)),
-                    )
-                )
-            for copy in copies:
-                copy.wait()
+                self.send(mine, mine, 5, 9, (at.section, at.chip_peer(step * QUAD)))
+            landed(self.group_in.at[0 : at.groups - 1], self.recv_sems.at[9])
             total = self.group_in[0].astype(F32)
             for other in range(1, at.groups):
                 total = total + self.group_in[other].astype(F32)
         piece = self.full.at[at.core, at.section, at.quad]
         piece[...] = total.astype(BF16)
-        self.copies = [
-            self.remote(piece, piece, (at.section, at.quad_peer(step))) for step in range(1, QUAD)
-        ]
-        self.spread = [self.over_sections(at.quad)]
+        for step in range(1, QUAD):
+            self.send(piece, piece, 2, 1 + step, (at.section, at.quad_peer(step)))
+        self.over_sections(at.quad)
 
     def over_sections(self, quad):
         at = self.place
         piece = self.full.at[at.core, at.section, quad]
-        return [
-            self.remote(piece, piece, (lax.rem(at.section + step, at.sections), at.dp))
-            for step in range(1, at.sections)
-        ]
+        for step in range(1, at.sections):
+            to = (lax.rem(at.section + step, at.sections), at.dp)
+            self.send(piece, piece, 3, 4 + step, to)
 
     def to_sections(self):
         at = self.place
         for step in range(1, QUAD):
-            self.copies[step - 1].wait()
-            self.spread.append(self.over_sections(lax.rem(at.quad + QUAD - step, QUAD)))
+            other = lax.rem(at.quad + QUAD - step, QUAD)
+            landed(self.full.at[at.core, at.section, other], self.recv_sems.at[1 + step])
+            self.over_sections(other)
         piece = self.full.at[at.core, at.section]
-        self.last = [self.remote(piece, piece, (at.section, at.sibling))]
+        self.send(piece, piece, 4, 8, (at.section, at.sibling))
 
     def to_sibling(self):
         at = self.place
         for step in range(1, at.sections):
-            for copies in self.spread:
-                copies[step - 1].wait()
             other = lax.rem(at.section + at.sections - step, at.sections)
             piece = self.full.at[at.core, other]
-            self.last.append(self.remote(piece, piece, (at.section, at.sibling)))
+            landed(piece, self.recv_sems.at[4 + step])
+            self.send(piece, piece, 4, 8, (at.section, at.sibling))
 
     def end(self):
-        for copy in self.last:
-            copy.wait()
+        at = self.place
+        landed(self.full.at[1 - at.core], self.recv_sems.at[8])
+        landed(self.theirs, self.send_sems.at[0])
+        landed(self.quad_in.at[0 : QUAD - 1], self.send_sems.at[1])
+        landed(self.quad_in.at[0 : QUAD - 1], self.send_sems.at[2])
+        landed(self.full.at[at.core, 0 : at.sections - 1], self.send_sems.at[3])
+        landed(self.full.at[at.core], self.send_sems.at[4])
+        if at.groups > 1:
+            landed(self.group_in.at[0 : at.groups - 1], self.send_sems.at[5])
 
 
 def main_kernel(cfg, names, *refs):
@@ -257,9 +244,8 @@
             r.sum_own.at[k, 0:tall] if k < len(SUM_ROWS) - 1 else r.late_own.at[section],
             r.sum_sibling.at[k, 0:tall],
             r.sum_slots.at[k, :, 0:tall],
-            r.sum_send,
-            r.sum_recv,
-            k,
+            r.sum_send.at[k],
+            r.sum_recv.at[k],
         )
         for k, tall in enumerate(SUM_ROWS)
     ]
@@ -271,13 +257,12 @@
         GradSum(
             place,
             [getattr(r, f"{part}_{k}") for part in STAGES],
-            r.grad_send,
-            r.grad_recv,
-            k,
+            r.grad_send.at[k],
+            r.grad_recv.at[k],
         )
-        for k in range(4)
+        for k in range(5)
     ]
-    upper_gate, upper_in, lower_gate, lower_in = batches
+    upper_gate, upper_in, lower_gate, lower_out, lower_in = batches
 
     fetched = []
     for k, (held, given) in enumerate(
@@ -790,46 +775,41 @@
     mixer_grad(0, 0)
     upper_total.append(upper_sum[1].total())
     gate_grad(0, 1, second_grad(1, upper_total[1]))
+    gate_weights(0, r.mine_2)
+    lower_gate.to_core()
+    upper_gate.to_groups()
     branch_grad(0, 1)
-    upper_gate.to_groups()
-    gate_weights(0, r.mine_2)
-    out_weights(0, r.mine_2, width)
-    lower_gate.to_core()
+    out_weights(0, r.mine_3, 0)
+    lower_out.to_core()
+    upper_in.to_groups()
+    lower_gate.to_quad()
     mixer_grad(0, 1)
-    lower_gate.to_quad()
-    in_weights(0, r.mine_3, 0)
+    lower_out.to_quad()
+    in_weights(0, r.mine_4, 0)
     lower_in.to_core()
     layer_rows(0)
     late_sum.start()
-    upper_in.to_groups()
+    upper_gate.to_sections()
     lower_in.to_quad()
     late_sum.turn()
     mixed_rows(0)
     mixed_rows(1)
-    upper_gate.to_sections()
     lower_gate.to_groups()
+    upper_in.to_sections()
+    lower_out.to_groups()
     lower_in.to_groups()
-    upper_in.to_sections()
     lower_gate.to_sections()
-    lower_in.to_sections()
     upper_gate.to_sibling()
     upper_in.to_sibling()
+    lower_out.to_sections()
+    lower_in.to_sections()
 
     late = late_sum.total()
     r.late[section] = late
-    to_sections = [
-        pltpu.make_async_remote_copy(
-            src_ref=r.late.at[section],
-            dst_ref=r.late.at[section],
-            send_sem=r.late_send.at[step],
-            recv_sem=r.late_recv.at[step],
-            device_id=(lax.rem(section + step, cfg.sections), dp),
-            device_id_type=MESH,
-        )
-        for step in range(1, cfg.sections)
-    ]
-    for copy in to_sections:
-        copy.start()
+    block = r.late.at[section]
+    for step in range(1, cfg.sections):
+        to = (lax.rem(section + step, cfg.sections), dp)
+        remote(block, block, r.late_sem.at[0], r.late_sem.at[1], to)
     own_gain = r.gain[0:1, own_columns]
     for m in range(2):
         count = counts[m][:, 0:128]
@@ -854,17 +834,20 @@
             r.gather[...], r.narrow_rest[...]
         )
     r.upper_norm[...] = upper_total[0] + upper_total[1]
-    for copy in to_sections:
-        copy.wait()
+    for k in range(2):
+        landed(r.late.at[0 : cfg.sections - 1], r.late_sem.at[k])
     lower_gate.to_sibling()
+    lower_out.to_sibling()
     lower_in.to_sibling()
     for batch in batches:
         batch.end()
+    for each in small:
+        each.end()
 
 
 def lay_out_kernel(cfg, *refs):
-    full = refs[0:4]
-    late, upper_norm, mixed, token_grad = refs[4:8]
+    full = refs[0:5]
+    late, upper_norm, mixed, token_grad = refs[5:9]
     (
         mixed_out,
         token_grad_out,
@@ -878,16 +861,18 @@
         skip_out,
         gate_out,
         gbias_out,
-    ) = refs[8:20]
-    in_held, out_held, gate_held = refs[20:23]
-    rows_held, sems = refs[23:30], refs[30]
+    ) = refs[9:21]
+    in_held, out_held, gate_held = refs[21:24]
+    rows_held, sems = refs[24:31], refs[31]
     width, states, half = cfg.width, cfg.states, cfg.half
     tall = states // (2 * QUAD)
     copies = []
 
-    def send(held, out):
-        copies.append(pltpu.make_async_copy(held, out, sems.at[len(copies)]))
-        copies[-1].start()
+    def send(held, out, sem=None):
+        copy = pltpu.make_async_copy(held, out, sems.at[3 + len(copies) if sem is None else sem])
+        copy.start()
+        if sem is None:
+            copies.append(copy)
 
     send(mixed, mixed_out)
     send(token_grad, token_grad_out)
@@ -910,26 +895,33 @@
             held[l : l + 1, :] = value[l]
         send(held, out)
 
-    places = [(s, c, z) for s in range(cfg.sections) for c in range(2) for z in range(QUAD)]
     for l in (1, 0):
-        gates, ins = full[2 - 2 * l], full[3 - 2 * l]
-        for s, c, z in places:
-            at = s * 128 + (c * QUAD + z) * 16
-            gate_held[l, at : at + 16, :] = gates[c, s, z, :, 0:width].astype(F32)
-        send(gate_held.at[l], gate_out.at[l])
-        for s, c, z in places:
-            for k in range(tall // 16):
-                first = (c * QUAD + z) * tall + 16 * k
-                out_held[l, first : first + 16, s * 128 : (s + 1) * 128] = gates[
-                    c, s, z, :, width + k * 128 : width + (k + 1) * 128
-                ].astype(F32)
-        send(out_held.at[l], out_out.at[l])
-        for s, c, z in places:
-            at = s * 128 + (c * QUAD + z) * 16
-            in_held[l, at : at + 16, :] = ins[c, s, z].astype(F32)
-        send(in_held.at[l], in_out.at[l])
+        parts = ((full[0], 0), (full[0], width), (full[1], 0))
+        if l == 0:
+            parts = ((full[2], 0), (full[3], 0), (full[4], 0))
+        for s in range(cfg.sections):
+            mine = slice(s * 128, (s + 1) * 128)
+            members = [(c, z) for c in range(2) for z in range(QUAD)]
+            for (part, begin), held, out, wide, sem in (
+                (parts[0], gate_held, gate_out, width, 0),
+                (parts[2], in_held, in_out, states, 1),
+            ):
+                for c, z in members:
+                    at = s * 128 + (c * QUAD + z) * 16
+                    held[l, at : at + 16, :] = part[c, s, z, :, begin : begin + wide].astype(F32)
+                send(held.at[l, mine], out.at[l, mine], sem)
+            part, begin = parts[1]
+            for c, z in members:
+                for k in range(tall // 16):
+                    first = (c * QUAD + z) * tall + 16 * k
+                    out_held[l, first : first + 16, mine] = part[
+                        c, s, z, :, begin + k * 128 : begin + (k + 1) * 128
+                    ].astype(F32)
+        send(out_held.at[l], out_out.at[l], 2)
     for copy in copies:
         copy.wait()
+    for sem, out in enumerate((gate_out, in_out, out_out)):
+        landed(out, sems.at[sem])
 
 
 INPUTS = tuple(
@@ -943,7 +935,7 @@
     groups = chips // QUAD
     steps = rows // SUB
     vmem, dma = pltpu.VMEM, pltpu.SemaphoreType.DMA
-    widths = (width + states, states) * 2
+    widths = (width + states, states, width, states, states)
     outs = {f"full_{k}": ((2, sections, QUAD, 16, w), BF16) for k, w in enumerate(widths)}
     outs.update(
         late=((sections, 16, 128), F32), upper_norm=((8, 128), F32), mixed=((2, rows, 128), BF16), token_grad=((2, rows, 128), F32)
@@ -953,12 +945,11 @@
         sum_sibling=vmem((len(SUM_ROWS), 24, 128), F32),
         sum_slots=vmem((len(SUM_ROWS), min(dp, max(chips, 8)), 24, 128), F32),
         late_own=vmem((sections, 16, 128), F32),
-        late_send=dma((sections,)),
-        late_recv=dma((sections,)),
-        sum_send=dma((len(SUM_ROWS), max(chips, 8))),
-        sum_recv=dma((len(SUM_ROWS), max(chips, 8))),
-        grad_send=dma((4, (2 + sections) * QUAD + groups)),
-        grad_recv=dma((4, (2 + sections) * QUAD + groups)),
+        late_sem=dma((2,)),
+        sum_send=dma((len(SUM_ROWS), 2)),
+        sum_recv=dma((len(SUM_ROWS), 2)),
+        grad_send=dma((5, 5 + (groups > 1))),
+        grad_recv=dma((5, 9 + (groups > 1))),
         fetch_sem=dma((4,)),
         b_in=vmem((2, width, states), BF16),
         c_out=vmem((2, states, width), BF16),
@@ -1039,12 +1030,12 @@
         partial(lay_out_kernel, cfg),
         name="lay_out",
         out_shape=[jax.ShapeDtypeStruct(*spec) for spec in shapes],
-        in_specs=[in_vmem] * 8,
+        in_specs=[in_vmem] * 9,
         out_specs=[in_hbm] * 12,
         scratch_shapes=[vmem(*shapes[k]) for k in by_copy]
         + [vmem((2, width), F32)] * 4
         + [vmem((2, states // 2), F32)] * 3
-        + [dma((15,))],
+        + [dma((12,))],
         compiler_params=pltpu.CompilerParams(vmem_limit_bytes=24 * 2**20),
     )(*made)
 

time: 53.9 us -> 51.9 us (0.963)
  Pallas kernels: 53 us -> 51.1 us
    pallas_call x1, Pallas kernels: 50.3 us -> 48.5 us  [per_device(): pl.pallas_call(partial(main_kernel, cfg, names), name='layers', out_shape...]
where the time goes in v3:
time: 51.9 us; the launch traced here: 51.7 us
  Pallas kernels  51.1 us (98%)
  between operations  0.66 us (1%)
    pallas_call x1, Pallas kernels, per_device(): pl.pallas_call(partial(main_kernel, cfg, names), name='layers', out_shape...  48.5 us
    pallas_call x1, Pallas kernels, per_device(): pl.pallas_call(partial(lay_out_kernel, cfg), name='lay_out', out_shape=[j...  2.59 us

profile of v3, /device:TPU:0, one launch (start us, length us, event | category | flops | bytes accessed | tf_op | source)
XLA Modules:
  0.0 51.7 jit_solution(4448456017615419743)
XLA Ops:
  0.6 48.5 %layers.1 = (bf16[2,4,4,16,896]{4,3,2,1,0:T(8,128)(2,1)S(1)}, bf16[2,4,4,16,384]{4,3,2,1,0:T(8,128)(2,1)S(1)}, bf16[2,4,4,16,512]{4,3,2,1,0:T(8,128)(2,1)S(1)}, ...) custom-call(bf16[2,256,512]{2,1,0:T(8,128)(2,1)} %refs_0_.1, ...), custom_call_target="tpu_custom_call" | custom-call | tf_op jit(solution)/shard_map/layers/pallas_call | solution.py:1000
  49.1 2.6 %lay_out.1 = (bf16[2,256,128]{2,1,0:T(8,128)(2,1)}, f32[2,256,128]{2,1,0:T(8,128)}, f32[2,512]{1,0:T(2,128)}, f32[2,512]{1,0:T(2,128)}, f32[2,192]{1,0:T(2,128)}...) custom-call(bf16[2,4,4,16,896]{4,3,2,1,0:T(8,128)(2,1)S(1)} %get-tup, ...), custom_call_target="tpu_custom_call" | custom-call | tf_op jit(solution)/shard_map/lay_out/pallas_call | solution.py:1029

commit v4 on v3

--- a/solution.py
+++ b/solution.py
@@ -15,7 +15,7 @@
 SUB = 8
 QUAD = 4
 LATE_STATES = 3
-SUM_ROWS = (24, 8, 8, 8, 8, 16)
+SUM_ROWS = (18, 8, 8, 8, 8, 16)
 
 
 STAGES = tuple(dict(mine=0, theirs=0, chip=0, quad=0, group=0, full=0))
@@ -125,12 +125,15 @@
         at = self.place
         self.send(self.mine.at[1 - at.core], self.theirs, 0, 0, (at.section, at.sibling))
 
-    def to_quad(self):
-        at = self.place
+    def add_cores(self):
         landed(self.theirs, self.recv_sems.at[0])
         for part in range(QUAD):
-            both = self.mine[at.core, part].astype(F32) + self.theirs[part].astype(F32)
+            both = self.mine[self.place.core, part].astype(F32) + self.theirs[part].astype(F32)
             self.chip_part[part] = both.astype(BF16)
+
+    def to_quad(self):
+        at = self.place
+        self.add_cores()
         for step in range(1, QUAD):
             other = lax.rem(at.quad + step, QUAD)
             to = (at.section, at.quad_peer(step))
@@ -143,6 +146,18 @@
         total = self.quad_in[0].astype(F32)
         for part in range(1, QUAD):
             total = total + self.quad_in[part].astype(F32)
+        self.own_piece(total)
+        self.to_members()
+        self.over_sections(at.quad)
+
+    def to_members(self):
+        at = self.place
+        piece = self.full.at[at.core, at.section, at.quad]
+        for step in range(1, QUAD):
+            self.send(piece, piece, 2, 1 + step, (at.section, at.quad_peer(step)))
+
+    def own_piece(self, total):
+        at = self.place
         if at.groups > 1:
             mine = self.group_in.at[at.group]
             mine[...] = total.astype(BF16)
@@ -152,18 +167,13 @@
             total = self.group_in[0].astype(F32)
             for other in range(1, at.groups):
                 total = total + self.group_in[other].astype(F32)
-        piece = self.full.at[at.core, at.section, at.quad]
-        piece[...] = total.astype(BF16)
-        for step in range(1, QUAD):
-            self.send(piece, piece, 2, 1 + step, (at.section, at.quad_peer(step)))
-        self.over_sections(at.quad)
+        self.full[at.core, at.section, at.quad] = total.astype(BF16)
 
     def over_sections(self, quad):
         at = self.place
         piece = self.full.at[at.core, at.section, quad]
-        for step in range(1, at.sections):
-            to = (lax.rem(at.section + step, at.sections), at.dp)
-            self.send(piece, piece, 3, 4 + step, to)
+        for k in (1, 2, 3):
+            self.send(piece, piece, 3, 4 + k, (at.beyond(k), at.dp))
 
     def to_sections(self):
         at = self.place
@@ -171,16 +181,15 @@
             other = lax.rem(at.quad + QUAD - step, QUAD)
             landed(self.full.at[at.core, at.section, other], self.recv_sems.at[1 + step])
             self.over_sections(other)
-        piece = self.full.at[at.core, at.section]
-        self.send(piece, piece, 4, 8, (at.section, at.sibling))
+        block = self.full.at[at.core, at.section]
+        self.send(block, block, 4, 8, (at.section, at.sibling))
 
     def to_sibling(self):
         at = self.place
-        for step in range(1, at.sections):
-            other = lax.rem(at.section + at.sections - step, at.sections)
-            piece = self.full.at[at.core, other]
-            landed(piece, self.recv_sems.at[4 + step])
-            self.send(piece, piece, 4, 8, (at.section, at.sibling))
+        for k in (1, 2, 3):
+            block = self.full.at[at.core, at.beyond(k)]
+            landed(block, self.recv_sems.at[4 + k])
+            self.send(block, block, 4, 8, (at.section, at.sibling))
 
     def end(self):
         at = self.place
@@ -192,6 +201,33 @@
         landed(self.full.at[at.core], self.send_sems.at[4])
         if at.groups > 1:
             landed(self.group_in.at[0 : at.groups - 1], self.send_sems.at[5])
+
+
+class RelaySum(GradSum):
+    def to_members(self):
+        at = self.place
+        piece = self.full.at[at.core, at.section, at.quad]
+        self.send(piece, piece, 2, 2, (at.section, at.apart(2)))
+        self.send(piece, piece, 2, 3, (at.section, at.apart(1)))
+
+    def to_near(self):
+        at = self.place
+        far = 2 * (1 - at.high) + at.low
+        piece = self.full.at[at.core, at.section, far]
+        landed(piece, self.recv_sems.at[2])
+        self.send(piece, piece, 2, 4, (at.section, at.apart(1)))
+        self.over_sections(far)
+        near = 2 * at.high + 1 - at.low
+        landed(self.full.at[at.core, at.section, near], self.recv_sems.at[3])
+        self.over_sections(near)
+
+    def to_sections(self):
+        at = self.place
+        last = 2 * (1 - at.high) + 1 - at.low
+        landed(self.full.at[at.core, at.section, last], self.recv_sems.at[4])
+        self.over_sections(last)
+        block = self.full.at[at.core, at.section]
+        self.send(block, block, 4, 8, (at.section, at.sibling))
 
 
 def main_kernel(cfg, names, *refs):
@@ -209,8 +245,14 @@
     chips = cfg.dp // 2
     core, chip = lax.rem(dp, 2), lax.div(dp, 2)
     quad, group = lax.rem(chip, QUAD), lax.div(chip, QUAD)
+    beyond = {
+        1: section + 1 - 2 * lax.rem(section, 2),
+        2: section + 2 - 4 * lax.div(section, 2),
+        3: 3 - section,
+    }
     place = SimpleNamespace(
         section=section,
+        beyond=lambda k: beyond[k],
         sections=cfg.sections,
         dp=dp,
         core=core,
@@ -223,6 +265,13 @@
         dp_peer=lambda step: lax.rem(dp + step, cfg.dp),
         sibling=dp + 1 - 2 * core,
         chip_peer=lambda step: lax.rem(chip + step, chips) * 2 + core,
+        high=lax.div(quad, 2),
+        low=lax.rem(quad, 2),
+        apart=lambda by: (
+            chip + by * (1 - 2 * (lax.rem(quad, 2) if by == 1 else lax.div(quad, 2)))
+        )
+        * 2
+        + core,
         quad_peer=lambda step: (group * QUAD + lax.rem(quad + step, QUAD)) * 2 + core,
     )
 
@@ -232,7 +281,7 @@
     else:
         peers = [(section, place.sibling)]
         peers += [(section, place.chip_peer(step)) for step in range(1, chips)]
-    peers += [(lax.rem(section + step, cfg.sections), dp) for step in range(1, cfg.sections)]
+    peers += [(beyond[k], dp) for k in (1, 2, 3)]
     barrier = pltpu.get_barrier_semaphore()
     for peer in peers:
         pl.semaphore_signal(barrier, inc=1, device_id=peer, device_id_type=MESH)
@@ -254,27 +303,30 @@
     upper_sum = [small[3], small[4]]
     late_sum = small[5]
     batches = [
-        GradSum(
+        (RelaySum if k < 2 else GradSum)(
             place,
             [getattr(r, f"{part}_{k}") for part in STAGES],
             r.grad_send.at[k],
             r.grad_recv.at[k],
         )
-        for k in range(5)
+        for k in range(4)
     ]
-    upper_gate, upper_in, lower_gate, lower_out, lower_in = batches
-
-    fetched = []
-    for k, (held, given) in enumerate(
-        (
-            (r.b_in, r.b_in_far),
-            (r.out_grad, r.out_grad_far),
-            (r.c_out, r.c_out_far),
-            (r.gmat, r.gmat_far),
-        )
-    ):
-        fetched.append(pltpu.make_async_copy(given, held, r.fetch_sem.at[k]))
-        fetched[k].start()
+    upper_gate, upper_in, lower_gate, lower_rest = batches
+
+    r.gain, r.bias, r.skip, r.gbias = [r.wide_par.at[k] for k in range(4)]
+    r.decay, r.freq, r.lstep = [r.state_par.at[k] for k in range(3)]
+    wide_far = (r.gain_far, r.bias_far, r.skip_far, r.gbias_far)
+    state_far = (r.decay_far, r.freq_far, r.lstep_far)
+    fetches = [[(r.lengths_far, r.lengths)]]
+    fetches += [[(r.tokens_far.at[m], r.tokens.at[m])] for m in range(2)]
+    fetches += [[(far, r.state_par.at[k]) for k, far in enumerate(state_far)]]
+    fetches += [[(r.b_in_far, r.b_in)], [(r.out_grad_far, r.out_grad)], [(r.c_out_far, r.c_out)]]
+    fetches += [[(far, r.wide_par.at[k]) for k, far in enumerate(wide_far)]]
+    fetches += [[(r.gmat_far, r.gmat)]]
+    for k, group_of in enumerate(fetches):
+        for far, held in group_of:
+            pltpu.make_async_copy(far, held, r.fetch_sem.at[k]).start()
+    landed(r.lengths, r.fetch_sem.at[0])
 
     first_len = [r.lengths[m, 0] for m in range(2)]
     total_len = [r.lengths[m, 0] + r.lengths[m, 1] for m in range(2)]
@@ -289,6 +341,8 @@
 
     chunk = 32
     for m in range(2):
+
+        landed(r.tokens.at[m], r.fetch_sem.at[1 + m])
 
         def token_sums(t, carry, m=m):
             at = pl.ds(t * chunk, chunk)
@@ -318,7 +372,7 @@
     for m in range(2):
         r.first_in[m] = matmul(r.spread[...], r.tokens[m]).astype(BF16)
     first_sum.turn()
-    fetched[1].wait()
+    landed(r.out_grad, r.fetch_sem.at[5])
     for m in range(2):
         r.out_grads[m] = matmul(r.spread[...], r.out_grad[m]).astype(BF16)
     held = lax.broadcasted_iota(jnp.int32, (rows, 128), 0)
@@ -337,6 +391,7 @@
 
     r.par[...] = jnp.zeros((SUB, lanes), F32)
     r.par[0:2, :] = jnp.ones((2, lanes), F32)
+    landed(r.state_par, r.fetch_sem.at[3])
     r.par[0:2, 0:half] = r.decay[...]
     r.par[2:4, 0:half] = r.freq[...]
     r.par[4:6, 0:half] = r.lstep[...]
@@ -362,8 +417,8 @@
     to_column = lax.broadcasted_iota(jnp.int32, (states, 2 * lanes), 1)
     moved_to = jnp.where(from_column < half, from_column, from_column + (lanes - half))
     r.widen[...] = jnp.where(to_column == moved_to, 1.0, 0.0).astype(BF16)
-    for k in (0, 2, 3):
-        fetched[k].wait()
+    for held, k in ((r.b_in, 4), (r.c_out, 6), (r.wide_par, 7), (r.gmat, 8)):
+        landed(held, r.fetch_sem.at[k])
     for l in range(2):
         r.b_pad[l] = matmul(r.b_in[l], r.widen[...]).astype(BF16)
         blank = jnp.zeros((lanes - half, width), BF16)
@@ -777,39 +832,32 @@
     gate_grad(0, 1, second_grad(1, upper_total[1]))
     gate_weights(0, r.mine_2)
     lower_gate.to_core()
+    branch_grad(0, 1)
     upper_gate.to_groups()
-    branch_grad(0, 1)
     out_weights(0, r.mine_3, 0)
-    lower_out.to_core()
+    lower_gate.to_quad()
     upper_in.to_groups()
-    lower_gate.to_quad()
     mixer_grad(0, 1)
-    lower_out.to_quad()
-    in_weights(0, r.mine_4, 0)
-    lower_in.to_core()
+    in_weights(0, r.mine_3, states)
+    lower_rest.to_core()
     layer_rows(0)
     late_sum.start()
+    mixed_rows(0)
+    lower_rest.to_quad()
+    late_sum.turn()
+    upper_gate.to_near()
+    mixed_rows(1)
+    upper_in.to_near()
+    lower_gate.to_groups()
     upper_gate.to_sections()
-    lower_in.to_quad()
-    late_sum.turn()
-    mixed_rows(0)
-    mixed_rows(1)
-    lower_gate.to_groups()
-    upper_in.to_sections()
-    lower_out.to_groups()
-    lower_in.to_groups()
-    lower_gate.to_sections()
-    upper_gate.to_sibling()
-    upper_in.to_sibling()
-    lower_out.to_sections()
-    lower_in.to_sections()
 
     late = late_sum.total()
     r.late[section] = late
     block = r.late.at[section]
-    for step in range(1, cfg.sections):
-        to = (lax.rem(section + step, cfg.sections), dp)
-        remote(block, block, r.late_sem.at[0], r.late_sem.at[1], to)
+    for k in (1, 2, 3):
+        remote(block, block, r.late_sem.at[0], r.late_sem.at[1], (beyond[k], dp))
+    lower_rest.to_groups()
+    upper_in.to_sections()
     own_gain = r.gain[0:1, own_columns]
     for m in range(2):
         count = counts[m][:, 0:128]
@@ -834,11 +882,14 @@
             r.gather[...], r.narrow_rest[...]
         )
     r.upper_norm[...] = upper_total[0] + upper_total[1]
+    lower_gate.to_sections()
+    lower_rest.to_sections()
+    upper_gate.to_sibling()
+    upper_in.to_sibling()
+    lower_gate.to_sibling()
+    lower_rest.to_sibling()
     for k in range(2):
         landed(r.late.at[0 : cfg.sections - 1], r.late_sem.at[k])
-    lower_gate.to_sibling()
-    lower_out.to_sibling()
-    lower_in.to_sibling()
     for batch in batches:
         batch.end()
     for each in small:
@@ -846,8 +897,8 @@
 
 
 def lay_out_kernel(cfg, *refs):
-    full = refs[0:5]
-    late, upper_norm, mixed, token_grad = refs[5:9]
+    full = refs[0:4]
+    late, upper_norm, mixed, token_grad = refs[4:8]
     (
         mixed_out,
         token_grad_out,
@@ -861,9 +912,9 @@
         skip_out,
         gate_out,
         gbias_out,
-    ) = refs[9:21]
-    in_held, out_held, gate_held = refs[21:24]
-    rows_held, sems = refs[24:31], refs[31]
+    ) = refs[8:20]
+    in_held, out_held, gate_held = refs[20:23]
+    rows_held, sems = refs[23:30], refs[30]
     width, states, half = cfg.width, cfg.states, cfg.half
     tall = states // (2 * QUAD)
     copies = []
@@ -898,7 +949,7 @@
     for l in (1, 0):
         parts = ((full[0], 0), (full[0], width), (full[1], 0))
         if l == 0:
-            parts = ((full[2], 0), (full[3], 0), (full[4], 0))
+            parts = ((full[2], 0), (full[3], 0), (full[3], states))
         for s in range(cfg.sections):
             mine = slice(s * 128, (s + 1) * 128)
             members = [(c, z) for c in range(2) for z in range(QUAD)]
@@ -925,7 +976,21 @@
 
 
 INPUTS = tuple(
-    dict(tokens=0, lengths=0, out_grad_far=0, gain=0, bias=0, decay=0, freq=0, lstep=0, b_in_far=0, c_out_far=0, skip=0, gmat_far=0, gbias=0)
+    dict(
+        tokens=0,
+        lengths=0,
+        out_grad=0,
+        gain=0,
+        bias=0,
+        decay=0,
+        freq=0,
+        lstep=0,
+        b_in=0,
+        c_out=0,
+        skip=0,
+        gmat=0,
+        gbias=0,
+    )
 )
 
 
@@ -935,7 +1000,7 @@
     groups = chips // QUAD
     steps = rows // SUB
     vmem, dma = pltpu.VMEM, pltpu.SemaphoreType.DMA
-    widths = (width + states, states, width, states, states)
+    widths = (width + states, states, width, 2 * states)
     outs = {f"full_{k}": ((2, sections, QUAD, 16, w), BF16) for k, w in enumerate(widths)}
     outs.update(
         late=((sections, 16, 128), F32), upper_norm=((8, 128), F32), mixed=((2, rows, 128), BF16), token_grad=((2, rows, 128), F32)
@@ -948,9 +1013,13 @@
         late_sem=dma((2,)),
         sum_send=dma((len(SUM_ROWS), 2)),
         sum_recv=dma((len(SUM_ROWS), 2)),
-        grad_send=dma((5, 5 + (groups > 1))),
-        grad_recv=dma((5, 9 + (groups > 1))),
-        fetch_sem=dma((4,)),
+        grad_send=dma((4, 5 + (groups > 1))),
+        grad_recv=dma((4, 9 + (groups > 1))),
+        fetch_sem=dma((9,)),
+        lengths=pltpu.SMEM((2, 2), jnp.int32),
+        tokens=vmem((2, rows, width), BF16),
+        wide_par=vmem((4, 2, width), F32),
+        state_par=vmem((3, 2, states // 2), F32),
         b_in=vmem((2, width, states), BF16),
         c_out=vmem((2, states, width), BF16),
         gmat=vmem((2, width, width), BF16),
@@ -994,17 +1063,13 @@
         for part, block in zip(STAGES, blocks):
             scratch[f"{part}_{k}"] = vmem((*block, 16, w), BF16)
     in_vmem = pl.BlockSpec(memory_space=pltpu.VMEM)
-    in_smem = pl.BlockSpec(memory_space=pltpu.SMEM)
     in_hbm = pl.BlockSpec(memory_space=pltpu.HBM)
-    names = INPUTS + tuple(outs) + tuple(scratch)
+    names = tuple(f"{name}_far" for name in INPUTS) + tuple(outs) + tuple(scratch)
     made = pl.pallas_call(
         partial(main_kernel, cfg, names),
         name="layers",
         out_shape=[vmem(*spec) for spec in outs.values()],
-        in_specs=[
-            in_smem if name == "lengths" else in_hbm if name.endswith("_far") else in_vmem
-            for name in INPUTS
-        ],
+        in_specs=[in_hbm for name in INPUTS],
         out_specs=[in_vmem for name in outs],
         scratch_shapes=list(scratch.values()),
         compiler_params=pltpu.CompilerParams(
@@ -1030,7 +1095,7 @@
         partial(lay_out_kernel, cfg),
         name="lay_out",
         out_shape=[jax.ShapeDtypeStruct(*spec) for spec in shapes],
-        in_specs=[in_vmem] * 9,
+        in_specs=[in_vmem] * 8,
         out_specs=[in_hbm] * 12,
         scratch_shapes=[vmem(*shapes[k]) for k in by_copy]
         + [vmem((2, width), F32)] * 4

time: 51.9 us -> 49.4 us (0.952)
  Pallas kernels: 51.1 us -> 48.6 us
    pallas_call x1, Pallas kernels: 48.5 us -> 46 us  [per_device(): pl.pallas_call(partial(main_kernel, cfg, names), name='layers', out_shape...]
where the time goes in v4:
time: 49.4 us; the launch traced here: 49.3 us
  Pallas kernels  48.6 us (98%)
  between operations  0.66 us (1%)
    pallas_call x1, Pallas kernels, per_device(): pl.pallas_call(partial(main_kernel, cfg, names), name='layers', out_shape...  46 us
    pallas_call x1, Pallas kernels, per_device(): pl.pallas_call(partial(lay_out_kernel, cfg), name='lay_out', out_shape=[j...  2.59 us

profile of v4, /device:TPU:0, one launch (start us, length us, event | category | flops | bytes accessed | tf_op | source)
XLA Modules:
  0.0 49.3 jit_solution(13678139696948787907)
XLA Ops:
  0.6 46.0 %layers.1 = (bf16[2,4,4,16,896]{4,3,2,1,0:T(8,128)(2,1)S(1)}, bf16[2,4,4,16,384]{4,3,2,1,0:T(8,128)(2,1)S(1)}, bf16[2,4,4,16,512]{4,3,2,1,0:T(8,128)(2,1)S(1)}, ...) custom-call(bf16[2,256,512]{2,1,0:T(8,128)(2,1)} %refs_0_.1, ...), custom_call_target="tpu_custom_call" | custom-call | tf_op jit(solution)/shard_map/layers/pallas_call | solution.py:1068
  46.7 2.6 %lay_out.1 = (bf16[2,256,128]{2,1,0:T(8,128)(2,1)}, f32[2,256,128]{2,1,0:T(8,128)}, f32[2,512]{1,0:T(2,128)}, f32[2,512]{1,0:T(2,128)}, f32[2,192]{1,0:T(2,128)}...) custom-call(bf16[2,4,4,16,896]{4,3,2,1,0:T(8,128)(2,1)S(1)} %get-tup, ...), custom_call_target="tpu_custom_call" | custom-call | tf_op jit(solution)/shard_map/lay_out/pallas_call | solution.py:1094

commit v5 on v4

--- a/solution.py
+++ b/solution.py
@@ -14,8 +14,9 @@
 BF16 = jnp.bfloat16
 SUB = 8
 QUAD = 4
+PART_SEMS = 8
 LATE_STATES = 3
-SUM_ROWS = (18, 8, 8, 8, 8, 16)
+SUM_ROWS = (10, 8, 8, 8, 8, 8, 16)
 
 
 STAGES = tuple(dict(mine=0, theirs=0, chip=0, quad=0, group=0, full=0))
@@ -70,18 +71,24 @@
     ).start()
 
 
+def first_sems(cfg):
+    begins = [0]
+    for k in range(len(SUM_ROWS)):
+        begins.append(begins[-1] + (2 if cfg.dp <= 8 and k < len(SUM_ROWS) - 1 else 4))
+    return begins
+
+
 class SmallSum:
-    def __init__(self, place, direct, own, sibling, slots, send_sems, recv_sems):
+    def __init__(self, place, direct, own, sibling, slots, sems):
         self.place, self.direct = place, direct
-        self.own, self.sibling, self.slots = own, sibling, slots
-        self.send_sems, self.recv_sems = send_sems, recv_sems
+        self.own, self.sibling, self.slots, self.sems = own, sibling, slots, sems
 
     def to_all(self, slot, members, peer):
         self.members = members
         block = self.slots.at[slot]
         for step in range(1, members):
             to = (self.place.section, peer(step))
-            remote(block, block, self.send_sems.at[1], self.recv_sems.at[1], to)
+            remote(block, block, self.sems.at[0], self.sems.at[1], to)
 
     def start(self):
         at = self.place
@@ -90,17 +97,17 @@
             self.to_all(at.dp, at.devices, at.dp_peer)
         else:
             to = (at.section, at.sibling)
-            remote(self.own, self.sibling, self.send_sems.at[0], self.recv_sems.at[0], to)
+            remote(self.own, self.sibling, self.sems.at[2], self.sems.at[3], to)
 
     def turn(self):
         at = self.place
         if not self.direct:
-            landed(self.sibling, self.recv_sems.at[0])
+            landed(self.sibling, self.sems.at[3])
             self.slots[at.chip] = self.own[...] + self.sibling[...]
             self.to_all(at.chip, at.chips, at.chip_peer)
 
     def total(self):
-        landed(self.slots.at[0 : self.members - 1], self.recv_sems.at[1])
+        landed(self.slots.at[0 : self.members - 1], self.sems.at[1])
         result = self.slots[0]
         for member in range(1, self.members):
             result = result + self.slots[member]
@@ -108,92 +115,100 @@
 
     def end(self):
         if not self.direct:
-            landed(self.own, self.send_sems.at[0])
-        landed(self.slots.at[0 : self.members - 1], self.send_sems.at[1])
+            landed(self.own, self.sems.at[2])
+        landed(self.slots.at[0 : self.members - 1], self.sems.at[0])
 
 
 class GradSum:
-    def __init__(self, place, refs, send_sems, recv_sems):
-        self.place = place
+    def __init__(self, place, parts, refs, send_sems, recv_sems):
+        self.place, self.parts = place, parts
         self.mine, self.theirs, self.chip_part, self.quad_in, self.group_in, self.full = refs
         self.send_sems, self.recv_sems = send_sems, recv_sems
 
-    def send(self, src, dst, send, recv, device):
-        remote(src, dst, self.send_sems.at[send], self.recv_sems.at[recv], device)
-
-    def to_core(self):
+    def recv(self, part, k):
+        if k == PART_SEMS:
+            return self.recv_sems.at[1 + 3 * PART_SEMS + part]
+        return self.recv_sems.at[1 + part * PART_SEMS + k]
+
+    def send(self, part, src, dst, send, recv, device):
+        columns = self.parts[part]
+        sem = self.recv_sems.at[0] if recv is None else self.recv(part, recv)
+        remote(src.at[..., columns], dst.at[..., columns], self.send_sems.at[send], sem, device)
+
+    def landed(self, part, block, k):
+        landed(block.at[..., self.parts[part]], self.recv(part, k))
+
+    def to_core(self, part):
         at = self.place
-        self.send(self.mine.at[1 - at.core], self.theirs, 0, 0, (at.section, at.sibling))
-
-    def add_cores(self):
-        landed(self.theirs, self.recv_sems.at[0])
-        for part in range(QUAD):
-            both = self.mine[self.place.core, part].astype(F32) + self.theirs[part].astype(F32)
-            self.chip_part[part] = both.astype(BF16)
-
-    def to_quad(self):
-        at = self.place
-        self.add_cores()
+        self.send(part, self.mine.at[1 - at.core], self.theirs, 0, 0, (at.section, at.sibling))
+
+    def to_quad(self, part):
+        at, columns = self.place, self.parts[part]
+        self.landed(part, self.theirs, 0)
+        for k in range(QUAD):
+            both = self.mine[at.core, k, :, columns].astype(F32)
+            both = both + self.theirs[k, :, columns].astype(F32)
+            self.chip_part[k, :, columns] = both.astype(BF16)
         for step in range(1, QUAD):
             other = lax.rem(at.quad + step, QUAD)
             to = (at.section, at.quad_peer(step))
-            self.send(self.chip_part.at[other], self.quad_in.at[at.quad], 1, 1, to)
-        self.quad_in[at.quad] = self.chip_part[at.quad]
-
-    def to_groups(self):
-        at = self.place
-        landed(self.quad_in.at[0 : QUAD - 1], self.recv_sems.at[1])
-        total = self.quad_in[0].astype(F32)
-        for part in range(1, QUAD):
-            total = total + self.quad_in[part].astype(F32)
-        self.own_piece(total)
-        self.to_members()
-        self.over_sections(at.quad)
-
-    def to_members(self):
+            self.send(part, self.chip_part.at[other], self.quad_in.at[at.quad], 1, 1, to)
+        self.quad_in[at.quad, :, columns] = self.chip_part[at.quad, :, columns]
+
+    def to_groups(self, part):
+        at, columns = self.place, self.parts[part]
+        self.landed(part, self.quad_in.at[0 : QUAD - 1], 1)
+        total = self.quad_in[0, :, columns].astype(F32)
+        for k in range(1, QUAD):
+            total = total + self.quad_in[k, :, columns].astype(F32)
+        if at.groups > 1:
+            mine = self.group_in.at[at.group]
+            mine[:, columns] = total.astype(BF16)
+            for step in range(1, at.groups):
+                self.send(part, mine, mine, 5, 8, (at.section, at.chip_peer(step * QUAD)))
+            self.landed(part, self.group_in.at[0 : at.groups - 1], 8)
+            total = self.group_in[0, :, columns].astype(F32)
+            for other in range(1, at.groups):
+                total = total + self.group_in[other, :, columns].astype(F32)
+        piece = self.full.at[at.core, at.section, at.quad]
+        piece[:, columns] = total.astype(BF16)
+        self.to_members(part)
+        self.over_sections(part, at.quad)
+
+    def to_members(self, part):
         at = self.place
         piece = self.full.at[at.core, at.section, at.quad]
         for step in range(1, QUAD):
-            self.send(piece, piece, 2, 1 + step, (at.section, at.quad_peer(step)))
-
-    def own_piece(self, total):
-        at = self.place
-        if at.groups > 1:
-            mine = self.group_in.at[at.group]
-            mine[...] = total.astype(BF16)
-            for step in range(1, at.groups):
-                self.send(mine, mine, 5, 9, (at.section, at.chip_peer(step * QUAD)))
-            landed(self.group_in.at[0 : at.groups - 1], self.recv_sems.at[9])
-            total = self.group_in[0].astype(F32)
-            for other in range(1, at.groups):
-                total = total + self.group_in[other].astype(F32)
-        self.full[at.core, at.section, at.quad] = total.astype(BF16)
-
-    def over_sections(self, quad):
+            self.send(part, piece, piece, 2, 1 + step, (at.section, at.quad_peer(step)))
+
+    def over_sections(self, part, quad):
         at = self.place
         piece = self.full.at[at.core, at.section, quad]
         for k in (1, 2, 3):
-            self.send(piece, piece, 3, 4 + k, (at.beyond(k), at.dp))
-
-    def to_sections(self):
+            self.send(part, piece, piece, 3, 4 + k, (at.beyond(k), at.dp))
+
+    def to_sections(self, part):
         at = self.place
         for step in range(1, QUAD):
             other = lax.rem(at.quad + QUAD - step, QUAD)
-            landed(self.full.at[at.core, at.section, other], self.recv_sems.at[1 + step])
-            self.over_sections(other)
-        block = self.full.at[at.core, at.section]
-        self.send(block, block, 4, 8, (at.section, at.sibling))
-
-    def to_sibling(self):
+            self.landed(part, self.full.at[at.core, at.section, other], 1 + step)
+            self.over_sections(part, other)
+        self.to_other(part, at.section)
+
+    def to_other(self, part, section):
+        at = self.place
+        block = self.full.at[at.core, section]
+        self.send(part, block, block, 4, None, (at.section, at.sibling))
+
+    def to_sibling(self, part):
         at = self.place
         for k in (1, 2, 3):
-            block = self.full.at[at.core, at.beyond(k)]
-            landed(block, self.recv_sems.at[4 + k])
-            self.send(block, block, 4, 8, (at.section, at.sibling))
+            self.landed(part, self.full.at[at.core, at.beyond(k)], 4 + k)
+            self.to_other(part, at.beyond(k))
 
     def end(self):
         at = self.place
-        landed(self.full.at[1 - at.core], self.recv_sems.at[8])
+        landed(self.full.at[1 - at.core], self.recv_sems.at[0])
         landed(self.theirs, self.send_sems.at[0])
         landed(self.quad_in.at[0 : QUAD - 1], self.send_sems.at[1])
         landed(self.quad_in.at[0 : QUAD - 1], self.send_sems.at[2])
@@ -204,30 +219,29 @@
 
 
 class RelaySum(GradSum):
-    def to_members(self):
+    def to_members(self, part):
         at = self.place
         piece = self.full.at[at.core, at.section, at.quad]
-        self.send(piece, piece, 2, 2, (at.section, at.apart(2)))
-        self.send(piece, piece, 2, 3, (at.section, at.apart(1)))
-
-    def to_near(self):
+        self.send(part, piece, piece, 2, 2, (at.section, at.apart(2)))
+        self.send(part, piece, piece, 2, 3, (at.section, at.apart(1)))
+
+    def to_near(self, part):
         at = self.place
         far = 2 * (1 - at.high) + at.low
         piece = self.full.at[at.core, at.section, far]
-        landed(piece, self.recv_sems.at[2])
-        self.send(piece, piece, 2, 4, (at.section, at.apart(1)))
-        self.over_sections(far)
+        self.landed(part, piece, 2)
+        self.send(part, piece, piece, 2, 4, (at.section, at.apart(1)))
+        self.over_sections(part, far)
         near = 2 * at.high + 1 - at.low
-        landed(self.full.at[at.core, at.section, near], self.recv_sems.at[3])
-        self.over_sections(near)
-
-    def to_sections(self):
+        self.landed(part, self.full.at[at.core, at.section, near], 3)
+        self.over_sections(part, near)
+
+    def to_sections(self, part):
         at = self.place
         last = 2 * (1 - at.high) + 1 - at.low
-        landed(self.full.at[at.core, at.section, last], self.recv_sems.at[4])
-        self.over_sections(last)
-        block = self.full.at[at.core, at.section]
-        self.send(block, block, 4, 8, (at.section, at.sibling))
+        self.landed(part, self.full.at[at.core, at.section, last], 4)
+        self.over_sections(part, last)
+        self.to_other(part, at.section)
 
 
 def main_kernel(cfg, names, *refs):
@@ -286,6 +300,7 @@
     for peer in peers:
         pl.semaphore_signal(barrier, inc=1, device_id=peer, device_id_type=MESH)
 
+    sum_sems = first_sems(cfg)
     small = [
         SmallSum(
             place,
@@ -293,25 +308,25 @@
             r.sum_own.at[k, 0:tall] if k < len(SUM_ROWS) - 1 else r.late_own.at[section],
             r.sum_sibling.at[k, 0:tall],
             r.sum_slots.at[k, :, 0:tall],
-            r.sum_send.at[k],
-            r.sum_recv.at[k],
+            r.sum_sem.at[sum_sems[k] : sum_sems[k + 1]],
         )
         for k, tall in enumerate(SUM_ROWS)
     ]
-    first_sum = small[0]
-    mid_sum = [small[1], small[2]]
-    upper_sum = [small[3], small[4]]
-    late_sum = small[5]
+    first_sum, mid_sum, upper_sum = small[0:2], small[2:4], small[4:6]
+    late_sum = small[6]
+    gate_part, out_part, in_part = range(3)
+    bounds = (0, width, width + states, width + 2 * states)
     batches = [
-        (RelaySum if k < 2 else GradSum)(
+        (RelaySum if k == 0 else GradSum)(
             place,
+            [slice(*bounds[k : k + 2]) for k in range(3)],
             [getattr(r, f"{part}_{k}") for part in STAGES],
             r.grad_send.at[k],
             r.grad_recv.at[k],
         )
-        for k in range(4)
+        for k in range(2)
     ]
-    upper_gate, upper_in, lower_gate, lower_rest = batches
+    upper, lower = batches
 
     r.gain, r.bias, r.skip, r.gbias = [r.wide_par.at[k] for k in range(4)]
     r.decay, r.freq, r.lstep = [r.state_par.at[k] for k in range(3)]
@@ -353,13 +368,14 @@
 
         zero = jnp.zeros((SUB, width), F32)
         sums, squares = sweep(rows // chunk, token_sums, (zero, zero))
-        put(0, 8 * m, jnp.sum(sums, axis=0, keepdims=True))
-        put(0, 8 * m + 4, jnp.sum(squares, axis=0, keepdims=True))
-        count = jnp.minimum(total_len[m], rows).astype(F32)
-        r.sum_own[0, 16 + m : 17 + m, :] = jnp.full((1, 128), count, F32)
-
-    pl.semaphore_wait(barrier, len(peers))
-    first_sum.start()
+        put(m, 0, jnp.sum(sums, axis=0, keepdims=True))
+        put(m, 4, jnp.sum(squares, axis=0, keepdims=True))
+        if m == 0:
+            for k in range(2):
+                count = jnp.minimum(total_len[k], rows).astype(F32)
+                r.sum_own[0, 8 + k : 9 + k, :] = jnp.full((1, 128), count, F32)
+            pl.semaphore_wait(barrier, len(peers))
+        first_sum[m].start()
 
     at_i = lax.broadcasted_iota(jnp.int32, (rows, rows), 0)
     at_r = lax.broadcasted_iota(jnp.int32, (rows, rows), 1)
@@ -371,7 +387,8 @@
     ).astype(BF16)
     for m in range(2):
         r.first_in[m] = matmul(r.spread[...], r.tokens[m]).astype(BF16)
-    first_sum.turn()
+    for m in range(2):
+        first_sum[m].turn()
     landed(r.out_grad, r.fetch_sem.at[5])
     for m in range(2):
         r.out_grads[m] = matmul(r.spread[...], r.out_grad[m]).astype(BF16)
@@ -575,7 +592,7 @@
 
     gelu_chunk = 16
 
-    def mixer(l, m, center, inv, hook=None):
+    def mixer(l, m, center, inv):
         gain, bias, skip = row_of(r.gain, l), row_of(r.bias, l), row_of(r.skip, l)
 
         def normalise(t, carry):
@@ -591,16 +608,19 @@
             return carry
 
         sweep(rows // chunk, normalise, 0)
+        yield
         r.drive[l, m] = matmul(r.scaled[l, micro_rows(m), :], r.b_pad[l])
+        yield
         scan_states(l, m)
-        if hook is not None:
-            hook()
-        r.work[...] = matmul(r.joined[l, micro_rows(m), :], r.c_pad[l])
+        yield
+        r.work[m] = matmul(r.joined[l, micro_rows(m), :], r.c_pad[l])
+
+        yield
 
         def activate(t, carry):
             at = pl.ds(t * gelu_chunk, gelu_chunk)
             scaled = r.normed[l, m, at, :] * gain + bias
-            y = (2.0 * r.work[at, :] + skip * scaled).astype(BF16).astype(F32)
+            y = (2.0 * r.work[m, at, :] + skip * scaled).astype(BF16).astype(F32)
             below = 0.5 + 0.5 * lax.erf(y * 0.7071067811865476)
             density = jnp.exp(-0.5 * y * y) * 0.3989422804014327
             active = y * below
@@ -611,14 +631,15 @@
             return carry
 
         sweep(rows // gelu_chunk, activate, 0)
-        r.work[...] = matmul(r.active_low[l, micro_rows(m), :], r.gmat[l])
+        yield
+        r.work[m] = matmul(r.active_low[l, micro_rows(m), :], r.gmat[l])
 
     def first_gate(m):
         gbias = row_of(r.gbias, 0)
 
         def gate(t, carry):
             at = pl.ds(t * gelu_chunk, gelu_chunk)
-            opened = jax.nn.sigmoid(r.work[at, :] + gbias)
+            opened = jax.nn.sigmoid(r.work[m, at, :] + gbias)
             r.sig[0, m, at, :] = opened
             v = repeat_lanes(r.valid[m, at, :], width // 128)
             gated = v * r.active[0, m, at, :] * opened
@@ -629,8 +650,8 @@
 
         zero = jnp.zeros((SUB, width), F32)
         sums, squares = sweep(rows // gelu_chunk, gate, (zero, zero))
-        put(1 + m, 0, jnp.sum(sums, axis=0, keepdims=True))
-        put(1 + m, 4, jnp.sum(squares, axis=0, keepdims=True))
+        put(2 + m, 0, jnp.sum(sums, axis=0, keepdims=True))
+        put(2 + m, 4, jnp.sum(squares, axis=0, keepdims=True))
 
     bias_sums = {}
     skip_sums = {}
@@ -641,14 +662,14 @@
         def gate(t, carry):
             at = pl.ds(t * gelu_chunk, gelu_chunk)
             if l == 1:
-                opened = jax.nn.sigmoid(r.work[at, :] + gbias)
+                opened = jax.nn.sigmoid(r.work[m, at, :] + gbias)
                 r.sig[1, m, at, :] = opened
             else:
                 opened = r.sig[0, m, at, :]
             v = repeat_lanes(r.valid[m, at, :], width // 128)
             masked = v * grad_of(at, v)
             through = masked * opened
-            r.through[at, :] = through
+            r.through[m, at, :] = through
             grad_logits = through * r.active[l, m, at, :] * (1.0 - opened)
             to = pl.ds(m * rows + t * gelu_chunk, gelu_chunk)
             r.grad_logits[l, to, :] = grad_logits.astype(BF16)
@@ -656,14 +677,16 @@
 
         zero = jnp.zeros((SUB, width), F32)
         bias_sums[l, m] = sweep(rows // gelu_chunk, gate, zero)
+        yield
 
     def branch_grad(l, m):
         gain, bias = row_of(r.gain, l), row_of(r.bias, l)
-        r.work[...] = matmul_nt(r.grad_logits[l, micro_rows(m), :], r.gmat[l])
+        r.work[m] = matmul_nt(r.grad_logits[l, micro_rows(m), :], r.gmat[l])
+        yield
 
         def branch(t, carry):
             at = pl.ds(t * chunk, chunk)
-            grad_active = r.through[at, :] + r.work[at, :]
+            grad_active = r.through[m, at, :] + r.work[m, at, :]
             g = (r.slope[l, m, at, :] * grad_active).astype(BF16)
             to = pl.ds(m * rows + t * chunk, chunk)
             r.branch[l, to, :] = g
@@ -672,19 +695,21 @@
 
         zero = jnp.zeros((SUB, width), F32)
         skip_sums[l, m] = sweep(rows // chunk, branch, zero)
+        yield
         r.q[m] = matmul_nt(r.branch[l, micro_rows(m), :], r.c_pad[l])
-
-    def mixer_grad(l, m, hook=None):
+        yield
+
+    def mixer_grad(l, m):
         skip = row_of(r.skip, l)
         scan_grads(l, m)
-        if hook is not None:
-            hook()
-        r.work[...] = matmul_nt(r.grad_drive[l, micro_rows(m), :], r.b_in[l])
+        yield
+        r.work[m] = matmul_nt(r.grad_drive[l, micro_rows(m), :], r.b_in[l])
+        yield
 
         def scaled_grad(t, carry):
             at = pl.ds(t * chunk, chunk)
             to = pl.ds(m * rows + t * chunk, chunk)
-            grad = r.work[at, :] + skip * r.branch[l, to, :].astype(F32)
+            grad = r.work[m, at, :] + skip * r.branch[l, to, :].astype(F32)
             r.grad_scaled[l, m, at, :] = grad
             normed = r.normed[l, m, at, :]
             return carry[0] + fold_rows(grad), carry[1] + fold_rows(grad * normed)
@@ -694,8 +719,8 @@
         sums = jnp.sum(sums, axis=0, keepdims=True)
         products = jnp.sum(products, axis=0, keepdims=True)
         if l == 1:
-            put(3 + m, 0, sums)
-            put(3 + m, 4, products)
+            put(4 + m, 0, sums)
+            put(4 + m, 4, products)
         else:
             put_late(2 * m, sums)
             put_late(2 * m + 1, products)
@@ -778,35 +803,41 @@
         second = gain * unfold(total, 4, 4) / count
         return gain, first, second, inv
 
-    total0 = first_sum.total()
-    counts = [repeat_lanes(total0[16 + m : 17 + m, :], width // 128) for m in range(2)]
-    norm0 = [moments(total0, 8 * m, counts[m]) for m in range(2)]
-
-    mixer(0, 0, *norm0[0])
-    first_gate(0)
-    mid_sum[0].start()
-    mixer(0, 1, *norm0[1], hook=mid_sum[0].turn)
-    first_gate(1)
-    mid_sum[1].start()
+    def take(steps):
+        for _ in steps:
+            pass
+
+    counts, norm0 = [None, None], [None, None]
+    for m in range(2):
+        total = first_sum[m].total()
+        if m == 0:
+            counts = [repeat_lanes(total[8 + k : 9 + k, :], width // 128) for k in range(2)]
+        norm0[m] = moments(total, 0, counts[m])
+        take(mixer(0, m, *norm0[m]))
+        first_gate(m)
+        mid_sum[m].start()
+        mid_sum[m].turn()
 
     norm1 = [None, None]
-    for m in range(2):
+
+    def second_layer(m):
         norm1[m] = moments(mid_sum[m].total(), 0, counts[m])
-        hook = mid_sum[1].turn if m == 0 else None
-        mixer(1, m, *norm1[m], hook=hook)
-        gate_grad(1, m, lambda at, v, m=m: r.out_grads[m, at, :].astype(F32))
-        branch_grad(1, m)
-        if m == 1:
-            gate_weights(1, r.mine_0)
-            out_weights(1, r.mine_0, width)
-            upper_gate.to_core()
-        mixer_grad(1, m)
+        yield from mixer(1, m, *norm1[m])
+        yield from gate_grad(1, m, lambda at, v: r.out_grads[m, at, :].astype(F32))
+        yield from branch_grad(1, m)
+        yield from mixer_grad(1, m)
         upper_sum[m].start()
         upper_sum[m].turn()
 
-    in_weights(1, r.mine_1, 0)
-    upper_in.to_core()
-    upper_gate.to_quad()
+    for m in range(2):
+        take(second_layer(m))
+
+    gate_weights(1, r.mine_0)
+    upper.to_core(gate_part)
+    out_weights(1, r.mine_0, width)
+    upper.to_core(out_part)
+    in_weights(1, r.mine_0, width + states)
+    upper.to_core(in_part)
     layer_rows(1)
 
     def second_grad(m, total):
@@ -824,40 +855,52 @@
         return grad_of
 
     upper_total = [upper_sum[0].total()]
-    gate_grad(0, 0, second_grad(0, upper_total[0]))
-    upper_in.to_quad()
-    branch_grad(0, 0)
-    mixer_grad(0, 0)
+    take(gate_grad(0, 0, second_grad(0, upper_total[0])))
+    upper.to_quad(gate_part)
+    take(branch_grad(0, 0))
+    upper.to_quad(out_part)
+    upper.to_quad(in_part)
+    take(mixer_grad(0, 0))
     upper_total.append(upper_sum[1].total())
-    gate_grad(0, 1, second_grad(1, upper_total[1]))
-    gate_weights(0, r.mine_2)
-    lower_gate.to_core()
-    branch_grad(0, 1)
-    upper_gate.to_groups()
-    out_weights(0, r.mine_3, 0)
-    lower_gate.to_quad()
-    upper_in.to_groups()
-    mixer_grad(0, 1)
-    in_weights(0, r.mine_3, states)
-    lower_rest.to_core()
+    take(gate_grad(0, 1, second_grad(1, upper_total[1])))
+    gate_weights(0, r.mine_1)
+    lower.to_core(gate_part)
+    take(branch_grad(0, 1))
+    out_weights(0, r.mine_1, width)
+    lower.to_core(out_part)
+    upper.to_groups(gate_part)
+    lower.to_quad(gate_part)
+    last = mixer_grad(0, 1)
+    next(last)
+    upper.to_groups(out_part)
+    next(last)
+    upper.to_groups(in_part)
+    take(last)
+    lower.to_quad(out_part)
+    in_weights(0, r.mine_1, width + states)
+    lower.to_core(in_part)
     layer_rows(0)
     late_sum.start()
+    upper.to_near(gate_part)
+    lower.to_quad(in_part)
+    late_sum.turn()
     mixed_rows(0)
-    lower_rest.to_quad()
-    late_sum.turn()
-    upper_gate.to_near()
+    upper.to_near(out_part)
+    lower.to_groups(gate_part)
+    upper.to_near(in_part)
     mixed_rows(1)
-    upper_in.to_near()
-    lower_gate.to_groups()
-    upper_gate.to_sections()
+    lower.to_groups(out_part)
+    upper.to_sections(gate_part)
+    upper.to_sections(out_part)
+    lower.to_groups(in_part)
+    lower.to_sections(gate_part)
+    upper.to_sections(in_part)
 
     late = late_sum.total()
     r.late[section] = late
     block = r.late.at[section]
     for k in (1, 2, 3):
         remote(block, block, r.late_sem.at[0], r.late_sem.at[1], (beyond[k], dp))
-    lower_rest.to_groups()
-    upper_in.to_sections()
     own_gain = r.gain[0:1, own_columns]
     for m in range(2):
         count = counts[m][:, 0:128]
@@ -882,12 +925,11 @@
             r.gather[...], r.narrow_rest[...]
         )
     r.upper_norm[...] = upper_total[0] + upper_total[1]
-    lower_gate.to_sections()
-    lower_rest.to_sections()
-    upper_gate.to_sibling()
-    upper_in.to_sibling()
-    lower_gate.to_sibling()
-    lower_rest.to_sibling()
+    lower.to_sections(out_part)
+    lower.to_sections(in_part)
+    for stage in (upper.to_sibling, lower.to_sibling):
+        for part in range(3):
+            stage(part)
     for k in range(2):
         landed(r.late.at[0 : cfg.sections - 1], r.late_sem.at[k])
     for batch in batches:
@@ -897,8 +939,8 @@
 
 
 def lay_out_kernel(cfg, *refs):
-    full = refs[0:4]
-    late, upper_norm, mixed, token_grad = refs[4:8]
+    full = refs[1], refs[0]
+    late, upper_norm, mixed, token_grad = refs[2:6]
     (
         mixed_out,
         token_grad_out,
@@ -912,9 +954,9 @@
         skip_out,
         gate_out,
         gbias_out,
-    ) = refs[8:20]
-    in_held, out_held, gate_held = refs[20:23]
-    rows_held, sems = refs[23:30], refs[30]
+    ) = refs[6:18]
+    in_held, out_held, gate_held = refs[18:21]
+    rows_held, sems = refs[21:28], refs[28]
     width, states, half = cfg.width, cfg.states, cfg.half
     tall = states // (2 * QUAD)
     copies = []
@@ -947,9 +989,7 @@
         send(held, out)
 
     for l in (1, 0):
-        parts = ((full[0], 0), (full[0], width), (full[1], 0))
-        if l == 0:
-            parts = ((full[2], 0), (full[3], 0), (full[3], states))
+        parts = [(full[l], begin) for begin in (0, width, width + states)]
         for s in range(cfg.sections):
             mine = slice(s * 128, (s + 1) * 128)
             members = [(c, z) for c in range(2) for z in range(QUAD)]
@@ -1000,7 +1040,7 @@
     groups = chips // QUAD
     steps = rows // SUB
     vmem, dma = pltpu.VMEM, pltpu.SemaphoreType.DMA
-    widths = (width + states, states, width, 2 * states)
+    widths = (width + 2 * states,) * 2
     outs = {f"full_{k}": ((2, sections, QUAD, 16, w), BF16) for k, w in enumerate(widths)}
     outs.update(
         late=((sections, 16, 128), F32), upper_norm=((8, 128), F32), mixed=((2, rows, 128), BF16), token_grad=((2, rows, 128), F32)
@@ -1011,10 +1051,9 @@
         sum_slots=vmem((len(SUM_ROWS), min(dp, max(chips, 8)), 24, 128), F32),
         late_own=vmem((sections, 16, 128), F32),
         late_sem=dma((2,)),
-        sum_send=dma((len(SUM_ROWS), 2)),
-        sum_recv=dma((len(SUM_ROWS), 2)),
-        grad_send=dma((4, 5 + (groups > 1))),
-        grad_recv=dma((4, 9 + (groups > 1))),
+        sum_sem=dma((first_sems(cfg)[-1],)),
+        grad_send=dma((2, 5 + (groups > 1))),
+        grad_recv=dma((2, 1 + 3 * (PART_SEMS + (groups > 1)))),
         fetch_sem=dma((9,)),
         lengths=pltpu.SMEM((2, 2), jnp.int32),
         tokens=vmem((2, rows, width), BF16),
@@ -1043,12 +1082,12 @@
         drive=vmem((2, 2, rows, 2 * lanes), F32),
         state=vmem((2, 2, (steps + 1) * SUB, 2 * lanes), F32),
         joined=vmem((2, 2 * rows, 2 * lanes), BF16),
-        work=vmem((rows, width), F32),
+        work=vmem((2, rows, width), F32),
         active=vmem((2, 2, rows, width), F32),
         active_low=vmem((2, 2 * rows, width), BF16),
         slope=vmem((2, 2, rows, width), F32),
         sig=vmem((2, 2, rows, width), F32),
-        through=vmem((rows, width), F32),
+        through=vmem((2, rows, width), F32),
         grad_logits=vmem((2, 2 * rows, width), BF16),
         branch=vmem((2, 2 * rows, width), BF16),
         grad_drive=vmem((2, 2 * rows, states), BF16),
@@ -1095,7 +1134,7 @@
         partial(lay_out_kernel, cfg),
         name="lay_out",
         out_shape=[jax.ShapeDtypeStruct(*spec) for spec in shapes],
-        in_specs=[in_vmem] * 8,
+        in_specs=[in_vmem] * 6,
         out_specs=[in_hbm] * 12,
         scratch_shapes=[vmem(*shapes[k]) for k in by_copy]
         + [vmem((2, width), F32)] * 4

time: 49.4 us -> 48.5 us (0.982)
  Pallas kernels: 48.6 us -> 47.5 us
    pallas_call x1, Pallas kernels: 46 us -> 44.9 us  [per_device(): pl.pallas_call(partial(main_kernel, cfg, names), name='layers', out_shape...]
where the time goes in v5:
time: 48.5 us; the launch traced here: 48.3 us
  Pallas kernels  47.5 us (98%)
  between operations  0.82 us (2%)
    pallas_call x1, Pallas kernels, per_device(): pl.pallas_call(partial(main_kernel, cfg, names), name='layers', out_shape...  44.9 us
    pallas_call x1, Pallas kernels, per_device(): pl.pallas_call(partial(lay_out_kernel, cfg), name='lay_out', out_shape=[j...  2.59 us

profile of v5, /device:TPU:0, one launch (start us, length us, event | category | flops | bytes accessed | tf_op | source)
XLA Modules:
  0.0 48.3 jit_solution(4740115383091319456)
XLA Ops:
  0.6 44.9 %layers.1 = (bf16[2,4,4,16,1280]{4,3,2,1,0:T(8,128)(2,1)S(1)}, bf16[2,4,4,16,1280]{4,3,2,1,0:T(8,128)(2,1)S(1)}, f32[4,16,128]{2,1,0:T(8,128)S(1)}, f32[8,128]{1...) custom-call(bf16[2,256,512]{2,1,0:T(8,128)(2,1)} %refs_0_.1, s32[2,2]{1,0:T(2,128)} %refs_1_.1, ...), custom_call_target="tpu_custom_call" | custom-call | tf_op jit(solution)/shard_map/layers/pallas_call | solution.py:1107
  45.6 2.6 %lay_out.1 = (bf16[2,256,128]{2,1,0:T(8,128)(2,1)}, f32[2,256,128]{2,1,0:T(8,128)}, f32[2,512]{1,0:T(2,128)}, f32[2,512]{1,0:T(2,128)}, f32[2,192]{1,0:T(2,128)}...) custom-call(bf16[2,4,4,16,1280]{4,3,2,1,0:T(8,128)(2,1)S(1)} %get-tu, ...), custom_call_target="tpu_custom_call" | custom-call | tf_op jit(solution)/shard_map/lay_out/pallas_call | solution.py:1133

commit v6 on v5

--- a/solution.py
+++ b/solution.py
@@ -14,7 +14,7 @@
 BF16 = jnp.bfloat16
 SUB = 8
 QUAD = 4
-PART_SEMS = 8
+PART_SEMS = 9
 LATE_STATES = 3
 SUM_ROWS = (10, 8, 8, 8, 8, 8, 16)
 
@@ -165,8 +165,8 @@
             mine = self.group_in.at[at.group]
             mine[:, columns] = total.astype(BF16)
             for step in range(1, at.groups):
-                self.send(part, mine, mine, 5, 8, (at.section, at.chip_peer(step * QUAD)))
-            self.landed(part, self.group_in.at[0 : at.groups - 1], 8)
+                self.send(part, mine, mine, 7, PART_SEMS, (at.section, at.chip_peer(step * QUAD)))
+            self.landed(part, self.group_in.at[0 : at.groups - 1], PART_SEMS)
             total = self.group_in[0, :, columns].astype(F32)
             for other in range(1, at.groups):
                 total = total + self.group_in[other, :, columns].astype(F32)
@@ -212,10 +212,50 @@
         landed(self.theirs, self.send_sems.at[0])
         landed(self.quad_in.at[0 : QUAD - 1], self.send_sems.at[1])
         landed(self.quad_in.at[0 : QUAD - 1], self.send_sems.at[2])
-        landed(self.full.at[at.core, 0 : at.sections - 1], self.send_sems.at[3])
+        self.end_sections()
         landed(self.full.at[at.core], self.send_sems.at[4])
         if at.groups > 1:
-            landed(self.group_in.at[0 : at.groups - 1], self.send_sems.at[5])
+            landed(self.group_in.at[0 : at.groups - 1], self.send_sems.at[7])
+
+
+    def end_sections(self):
+        at = self.place
+        landed(self.full.at[at.core, 0 : at.sections - 1], self.send_sems.at[3])
+
+
+class CornerSum(GradSum):
+    def to_groups(self, part):
+        super().to_groups(part)
+        at = self.place
+        piece = self.full.at[at.core, at.section, at.quad]
+        self.send(part, piece, piece, 5, 7, (at.beyond(3), at.dp))
+
+    def over_sections(self, part, quad):
+        at = self.place
+        piece = self.full.at[at.core, at.section, quad]
+        for k in (1, 2):
+            self.send(part, piece, piece, 3, 4 + k, (at.beyond(k), at.dp))
+
+    def to_corner(self, part):
+        at = self.place
+        piece = self.full.at[at.core, at.beyond(3), at.quad]
+        self.landed(part, piece, 7)
+        for step in range(1, QUAD):
+            self.send(part, piece, piece, 6, 8, (at.section, at.quad_peer(step)))
+
+    def to_sibling(self, part):
+        at = self.place
+        for k in (1, 2):
+            self.landed(part, self.full.at[at.core, at.beyond(k)], 4 + k)
+            self.to_other(part, at.beyond(k))
+        self.landed(part, self.full.at[at.core, at.beyond(3), 0 : QUAD - 1], 8)
+        self.to_other(part, at.beyond(3))
+
+    def end_sections(self):
+        at = self.place
+        landed(self.full.at[at.core, 0:2], self.send_sems.at[3])
+        landed(self.full.at[at.core, 0, 0], self.send_sems.at[5])
+        landed(self.full.at[at.core, 0, 0 : QUAD - 1], self.send_sems.at[6])
 
 
 class RelaySum(GradSum):
@@ -317,7 +357,7 @@
     gate_part, out_part, in_part = range(3)
     bounds = (0, width, width + states, width + 2 * states)
     batches = [
-        (RelaySum if k == 0 else GradSum)(
+        (RelaySum if k == 0 else CornerSum)(
             place,
             [slice(*bounds[k : k + 2]) for k in range(3)],
             [getattr(r, f"{part}_{k}") for part in STAGES],
@@ -885,16 +925,17 @@
     lower.to_quad(in_part)
     late_sum.turn()
     mixed_rows(0)
+    lower.to_groups(gate_part)
     upper.to_near(out_part)
-    lower.to_groups(gate_part)
     upper.to_near(in_part)
     mixed_rows(1)
     lower.to_groups(out_part)
     upper.to_sections(gate_part)
+    lower.to_groups(in_part)
+    lower.to_corner(gate_part)
     upper.to_sections(out_part)
-    lower.to_groups(in_part)
+    upper.to_sections(in_part)
     lower.to_sections(gate_part)
-    upper.to_sections(in_part)
 
     late = late_sum.total()
     r.late[section] = late
@@ -925,11 +966,16 @@
             r.gather[...], r.narrow_rest[...]
         )
     r.upper_norm[...] = upper_total[0] + upper_total[1]
+    lower.to_corner(out_part)
     lower.to_sections(out_part)
+    lower.to_corner(in_part)
     lower.to_sections(in_part)
-    for stage in (upper.to_sibling, lower.to_sibling):
-        for part in range(3):
-            stage(part)
+    upper.to_sibling(gate_part)
+    upper.to_sibling(out_part)
+    upper.to_sibling(in_part)
+    lower.to_sibling(gate_part)
+    lower.to_sibling(out_part)
+    lower.to_sibling(in_part)
     for k in range(2):
         landed(r.late.at[0 : cfg.sections - 1], r.late_sem.at[k])
     for batch in batches:
@@ -1052,7 +1098,7 @@
         late_own=vmem((sections, 16, 128), F32),
         late_sem=dma((2,)),
         sum_sem=dma((first_sems(cfg)[-1],)),
-        grad_send=dma((2, 5 + (groups > 1))),
+        grad_send=dma((2, 7 + (groups > 1))),
         grad_recv=dma((2, 1 + 3 * (PART_SEMS + (groups > 1)))),
         fetch_sem=dma((9,)),
         lengths=pltpu.SMEM((2, 2), jnp.int32),

time: 48.5 us -> 47.1 us (0.971)
  Pallas kernels: 47.5 us -> 46.1 us
    pallas_call x1, Pallas kernels: 44.9 us -> 43.5 us  [per_device(): pl.pallas_call(partial(main_kernel, cfg, names), name='layers', out_shape...]
where the time goes in v6:
time: 47.1 us; the launch traced here: 46.9 us
  Pallas kernels  46.1 us (98%)
  between operations  0.82 us (2%)
    pallas_call x1, Pallas kernels, per_device(): pl.pallas_call(partial(main_kernel, cfg, names), name='layers', out_shape...  43.5 us
    pallas_call x1, Pallas kernels, per_device(): pl.pallas_call(partial(lay_out_kernel, cfg), name='lay_out', out_shape=[j...  2.59 us

profile of v6, /device:TPU:0, one launch (start us, length us, event | category | flops | bytes accessed | tf_op | source)
XLA Modules:
  0.0 46.9 jit_solution(7395029038625326584)
XLA Ops:
  0.6 43.5 %layers.1 = (bf16[2,4,4,16,1280]{4,3,2,1,0:T(8,128)(2,1)S(1)}, bf16[2,4,4,16,1280]{4,3,2,1,0:T(8,128)(2,1)S(1)}, f32[4,16,128]{2,1,0:T(8,128)S(1)}, f32[8,128]{1...) custom-call(bf16[2,256,512]{2,1,0:T(8,128)(2,1)} %refs_0_.1, s32[2,2]{1,0:T(2,128)} %refs_1_.1, ...), custom_call_target="tpu_custom_call" | custom-call | tf_op jit(solution)/shard_map/layers/pallas_call | solution.py:1153
  44.2 2.6 %lay_out.1 = (bf16[2,256,128]{2,1,0:T(8,128)(2,1)}, f32[2,256,128]{2,1,0:T(8,128)}, f32[2,512]{1,0:T(2,128)}, f32[2,512]{1,0:T(2,128)}, f32[2,192]{1,0:T(2,128)}...) custom-call(bf16[2,4,4,16,1280]{4,3,2,1,0:T(8,128)(2,1)S(1)} %get-tu, ...), custom_call_target="tpu_custom_call" | custom-call | tf_op jit(solution)/shard_map/lay_out/pallas_call | solution.py:1179

commit v7 on v6

--- a/solution.py
+++ b/solution.py
@@ -224,11 +224,11 @@
 
 
 class CornerSum(GradSum):
-    def to_groups(self, part):
-        super().to_groups(part)
+    def to_members(self, part):
         at = self.place
         piece = self.full.at[at.core, at.section, at.quad]
         self.send(part, piece, piece, 5, 7, (at.beyond(3), at.dp))
+        super().to_members(part)
 
     def over_sections(self, part, quad):
         at = self.place
@@ -927,11 +927,11 @@
     mixed_rows(0)
     lower.to_groups(gate_part)
     upper.to_near(out_part)
+    lower.to_groups(out_part)
     upper.to_near(in_part)
     mixed_rows(1)
-    lower.to_groups(out_part)
+    lower.to_groups(in_part)
     upper.to_sections(gate_part)
-    lower.to_groups(in_part)
     lower.to_corner(gate_part)
     upper.to_sections(out_part)
     upper.to_sections(in_part)

time: 47.1 us -> 46.1 us (0.979)
  Pallas kernels: 46.1 us -> 45.1 us
    pallas_call x1, Pallas kernels: 43.5 us -> 42.5 us  [per_device(): pl.pallas_call(partial(main_kernel, cfg, names), name='layers', out_shape...]
where the time goes in v7:
time: 46.1 us; the launch traced here: 45.9 us
  Pallas kernels  45.1 us (98%)
  between operations  0.82 us (2%)
    pallas_call x1, Pallas kernels, per_device(): pl.pallas_call(partial(main_kernel, cfg, names), name='layers', out_shape...  42.5 us
    pallas_call x1, Pallas kernels, per_device(): pl.pallas_call(partial(lay_out_kernel, cfg), name='lay_out', out_shape=[j...  2.59 us

profile of v7, /device:TPU:0, one launch (start us, length us, event | category | flops | bytes accessed | tf_op | source)
XLA Modules:
  0.0 45.9 jit_solution(2882574377853839517)
XLA Ops:
  0.6 42.5 %layers.1 = (bf16[2,4,4,16,1280]{4,3,2,1,0:T(8,128)(2,1)S(1)}, bf16[2,4,4,16,1280]{4,3,2,1,0:T(8,128)(2,1)S(1)}, f32[4,16,128]{2,1,0:T(8,128)S(1)}, f32[8,128]{1...) custom-call(bf16[2,256,512]{2,1,0:T(8,128)(2,1)} %refs_0_.1, s32[2,2]{1,0:T(2,128)} %refs_1_.1, ...), custom_call_target="tpu_custom_call" | custom-call | tf_op jit(solution)/shard_map/layers/pallas_call | solution.py:1153
  43.2 2.6 %lay_out.1 = (bf16[2,256,128]{2,1,0:T(8,128)(2,1)}, f32[2,256,128]{2,1,0:T(8,128)}, f32[2,512]{1,0:T(2,128)}, f32[2,512]{1,0:T(2,128)}, f32[2,192]{1,0:T(2,128)}...) custom-call(bf16[2,4,4,16,1280]{4,3,2,1,0:T(8,128)(2,1)S(1)} %get-tu, ...), custom_call_target="tpu_custom_call" | custom-call | tf_op jit(solution)/shard_map/lay_out/pallas_call | solution.py:1179

commit v8 on v7

--- a/solution.py
+++ b/solution.py
@@ -14,6 +14,7 @@
 BF16 = jnp.bfloat16
 SUB = 8
 QUAD = 4
+FAR_FIRST = (4, 6, 2, 3, 5, 7, 1)
 PART_SEMS = 9
 LATE_STATES = 3
 SUM_ROWS = (10, 8, 8, 8, 8, 8, 16)
@@ -86,7 +87,7 @@
     def to_all(self, slot, members, peer):
         self.members = members
         block = self.slots.at[slot]
-        for step in range(1, members):
+        for step in FAR_FIRST if members == 8 else range(1, members):
             to = (self.place.section, peer(step))
             remote(block, block, self.sems.at[0], self.sems.at[1], to)
 
@@ -631,6 +632,11 @@
         return slice(m * rows, (m + 1) * rows)
 
     gelu_chunk = 16
+    halves = (slice(0, rows // 2), slice(rows // 2, rows))
+
+    def moved(m, part):
+        return slice(m * rows + part.start, m * rows + part.stop)
+
 
     def mixer(l, m, center, inv):
         gain, bias, skip = row_of(r.gain, l), row_of(r.bias, l), row_of(r.skip, l)
@@ -653,7 +659,8 @@
         yield
         scan_states(l, m)
         yield
-        r.work[m] = matmul(r.joined[l, micro_rows(m), :], r.c_pad[l])
+        for part in halves:
+            r.work[m, part, :] = matmul(r.joined[l, moved(m, part), :], r.c_pad[l])
 
         yield
 
@@ -670,9 +677,10 @@
             r.active_low[l, to, :] = active.astype(BF16)
             return carry
 
-        sweep(rows // gelu_chunk, activate, 0)
-        yield
-        r.work[m] = matmul(r.active_low[l, micro_rows(m), :], r.gmat[l])
+        for k, part in enumerate(halves):
+            for t in range(rows // gelu_chunk // 2):
+                activate(k * (rows // gelu_chunk // 2) + t, 0)
+            r.work[m, part, :] = matmul(r.active_low[l, moved(m, part), :], r.gmat[l])
 
     def first_gate(m):
         gbias = row_of(r.gbias, 0)
@@ -906,12 +914,12 @@
     gate_weights(0, r.mine_1)
     lower.to_core(gate_part)
     take(branch_grad(0, 1))
-    out_weights(0, r.mine_1, width)
-    lower.to_core(out_part)
     upper.to_groups(gate_part)
     lower.to_quad(gate_part)
     last = mixer_grad(0, 1)
     next(last)
+    out_weights(0, r.mine_1, width)
+    lower.to_core(out_part)
     upper.to_groups(out_part)
     next(last)
     upper.to_groups(in_part)

time: 46.1 us -> 45.6 us (0.989)
  Pallas kernels: 45.1 us -> 44.6 us
    pallas_call x1, Pallas kernels: 42.5 us -> 42 us  [per_device(): pl.pallas_call(partial(main_kernel, cfg, names), name='layers', out_shape...]
where the time goes in v8:
time: 45.6 us; the launch traced here: 45.4 us
  Pallas kernels  44.6 us (98%)
  between operations  0.82 us (2%)
    pallas_call x1, Pallas kernels, per_device(): pl.pallas_call(partial(main_kernel, cfg, names), name='layers', out_shape...  42 us
    pallas_call x1, Pallas kernels, per_device(): pl.pallas_call(partial(lay_out_kernel, cfg), name='lay_out', out_shape=[j...  2.59 us

profile of v8, /device:TPU:0, one launch (start us, length us, event | category | flops | bytes accessed | tf_op | source)
XLA Modules:
  0.0 45.4 jit_solution(9615465324128249896)
XLA Ops:
  0.6 42.0 %layers.1 = (bf16[2,4,4,16,1280]{4,3,2,1,0:T(8,128)(2,1)S(1)}, bf16[2,4,4,16,1280]{4,3,2,1,0:T(8,128)(2,1)S(1)}, f32[4,16,128]{2,1,0:T(8,128)S(1)}, f32[8,128]{1...) custom-call(bf16[2,256,512]{2,1,0:T(8,128)(2,1)} %refs_0_.1, s32[2,2]{1,0:T(2,128)} %refs_1_.1, ...), custom_call_target="tpu_custom_call" | custom-call | tf_op jit(solution)/shard_map/layers/pallas_call | solution.py:1161
  42.6 2.6 %lay_out.1 = (bf16[2,256,128]{2,1,0:T(8,128)(2,1)}, f32[2,256,128]{2,1,0:T(8,128)}, f32[2,512]{1,0:T(2,128)}, f32[2,512]{1,0:T(2,128)}, f32[2,192]{1,0:T(2,128)}...) custom-call(bf16[2,4,4,16,1280]{4,3,2,1,0:T(8,128)(2,1)S(1)} %get-tu, ...), custom_call_target="tpu_custom_call" | custom-call | tf_op jit(solution)/shard_map/lay_out/pallas_call | solution.py:1187

commit v9 on v8

--- a/solution.py
+++ b/solution.py
@@ -15,7 +15,6 @@
 SUB = 8
 QUAD = 4
 FAR_FIRST = (4, 6, 2, 3, 5, 7, 1)
-PART_SEMS = 9
 LATE_STATES = 3
 SUM_ROWS = (10, 8, 8, 8, 8, 8, 16)
 
@@ -121,15 +120,17 @@
 
 
 class GradSum:
+    part_sems, sends = 6, 5
+
     def __init__(self, place, parts, refs, send_sems, recv_sems):
         self.place, self.parts = place, parts
         self.mine, self.theirs, self.chip_part, self.quad_in, self.group_in, self.full = refs
         self.send_sems, self.recv_sems = send_sems, recv_sems
 
     def recv(self, part, k):
-        if k == PART_SEMS:
-            return self.recv_sems.at[1 + 3 * PART_SEMS + part]
-        return self.recv_sems.at[1 + part * PART_SEMS + k]
+        if k == self.part_sems:
+            return self.recv_sems.at[1 + 3 * self.part_sems + part]
+        return self.recv_sems.at[1 + part * self.part_sems + k]
 
     def send(self, part, src, dst, send, recv, device):
         columns = self.parts[part]
@@ -166,8 +167,8 @@
             mine = self.group_in.at[at.group]
             mine[:, columns] = total.astype(BF16)
             for step in range(1, at.groups):
-                self.send(part, mine, mine, 7, PART_SEMS, (at.section, at.chip_peer(step * QUAD)))
-            self.landed(part, self.group_in.at[0 : at.groups - 1], PART_SEMS)
+                self.send(part, mine, mine, self.sends, self.part_sems, (at.section, at.chip_peer(step * QUAD)))
+            self.landed(part, self.group_in.at[0 : at.groups - 1], self.part_sems)
             total = self.group_in[0, :, columns].astype(F32)
             for other in range(1, at.groups):
                 total = total + self.group_in[other, :, columns].astype(F32)
@@ -186,7 +187,7 @@
         at = self.place
         piece = self.full.at[at.core, at.section, quad]
         for k in (1, 2, 3):
-            self.send(part, piece, piece, 3, 4 + k, (at.beyond(k), at.dp))
+            self.send(part, piece, piece, 3, 5, (at.beyond(k), at.dp))
 
     def to_sections(self, part):
         at = self.place
@@ -203,8 +204,8 @@
 
     def to_sibling(self, part):
         at = self.place
+        self.landed(part, self.full.at[at.core, 0 : at.sections - 1], 5)
         for k in (1, 2, 3):
-            self.landed(part, self.full.at[at.core, at.beyond(k)], 4 + k)
             self.to_other(part, at.beyond(k))
 
     def end(self):
@@ -216,7 +217,7 @@
         self.end_sections()
         landed(self.full.at[at.core], self.send_sems.at[4])
         if at.groups > 1:
-            landed(self.group_in.at[0 : at.groups - 1], self.send_sems.at[7])
+            landed(self.group_in.at[0 : at.groups - 1], self.send_sems.at[self.sends])
 
 
     def end_sections(self):
@@ -225,31 +226,33 @@
 
 
 class CornerSum(GradSum):
+    part_sems, sends = 8, 7
+
     def to_members(self, part):
         at = self.place
         piece = self.full.at[at.core, at.section, at.quad]
-        self.send(part, piece, piece, 5, 7, (at.beyond(3), at.dp))
+        self.send(part, piece, piece, 5, 6, (at.beyond(3), at.dp))
         super().to_members(part)
 
     def over_sections(self, part, quad):
         at = self.place
         piece = self.full.at[at.core, at.section, quad]
         for k in (1, 2):
-            self.send(part, piece, piece, 3, 4 + k, (at.beyond(k), at.dp))
+            self.send(part, piece, piece, 3, 5, (at.beyond(k), at.dp))
 
     def to_corner(self, part):
         at = self.place
         piece = self.full.at[at.core, at.beyond(3), at.quad]
-        self.landed(part, piece, 7)
+        self.landed(part, piece, 6)
         for step in range(1, QUAD):
-            self.send(part, piece, piece, 6, 8, (at.section, at.quad_peer(step)))
+            self.send(part, piece, piece, 6, 7, (at.section, at.quad_peer(step)))
 
     def to_sibling(self, part):
         at = self.place
+        self.landed(part, self.full.at[at.core, 0:2], 5)
         for k in (1, 2):
-            self.landed(part, self.full.at[at.core, at.beyond(k)], 4 + k)
             self.to_other(part, at.beyond(k))
-        self.landed(part, self.full.at[at.core, at.beyond(3), 0 : QUAD - 1], 8)
+        self.landed(part, self.full.at[at.core, at.beyond(3), 0 : QUAD - 1], 7)
         self.to_other(part, at.beyond(3))
 
     def end_sections(self):
@@ -283,6 +286,14 @@
         self.landed(part, self.full.at[at.core, at.section, last], 4)
         self.over_sections(part, last)
         self.to_other(part, at.section)
+
+
+def grad_sems(groups):
+    ends = [0]
+    for kind in (RelaySum, CornerSum):
+        ends.append(ends[-1] + kind.sends + (groups > 1))
+        ends.append(ends[-1] + 1 + 3 * (kind.part_sems + (groups > 1)))
+    return ends
 
 
 def main_kernel(cfg, names, *refs):
@@ -357,13 +368,14 @@
     late_sum = small[6]
     gate_part, out_part, in_part = range(3)
     bounds = (0, width, width + states, width + 2 * states)
+    ends = grad_sems(place.groups)
     batches = [
         (RelaySum if k == 0 else CornerSum)(
             place,
             [slice(*bounds[k : k + 2]) for k in range(3)],
             [getattr(r, f"{part}_{k}") for part in STAGES],
-            r.grad_send.at[k],
-            r.grad_recv.at[k],
+            r.grad_sem.at[ends[2 * k] : ends[2 * k + 1]],
+            r.grad_sem.at[ends[2 * k + 1] : ends[2 * k + 2]],
         )
         for k in range(2)
     ]
@@ -1106,8 +1118,7 @@
         late_own=vmem((sections, 16, 128), F32),
         late_sem=dma((2,)),
         sum_sem=dma((first_sems(cfg)[-1],)),
-        grad_send=dma((2, 7 + (groups > 1))),
-        grad_recv=dma((2, 1 + 3 * (PART_SEMS + (groups > 1)))),
+        grad_sem=dma((grad_sems(groups)[-1],)),
         fetch_sem=dma((9,)),
         lengths=pltpu.SMEM((2, 2), jnp.int32),
         tokens=vmem((2, rows, width), BF16),

time: 45.6 us -> 45.4 us (level)
  no operation moved by 1% of the time
where the time goes in v9:
time: 45.4 us; the launch traced here: 45.3 us
  Pallas kernels  44.4 us (98%)
  between operations  0.82 us (2%)
    pallas_call x1, Pallas kernels, per_device(): pl.pallas_call(partial(main_kernel, cfg, names), name='layers', out_shape...  41.9 us
    pallas_call x1, Pallas kernels, per_device(): pl.pallas_call(partial(lay_out_kernel, cfg), name='lay_out', out_shape=[j...  2.59 us

profile of v9, /device:TPU:0, one launch (start us, length us, event | category | flops | bytes accessed | tf_op | source)
XLA Modules:
  0.0 45.3 jit_solution(2932912984623097862)
XLA Ops:
  0.6 41.9 %layers.1 = (bf16[2,4,4,16,1280]{4,3,2,1,0:T(8,128)(2,1)S(1)}, bf16[2,4,4,16,1280]{4,3,2,1,0:T(8,128)(2,1)S(1)}, f32[4,16,128]{2,1,0:T(8,128)S(1)}, f32[8,128]{1...) custom-call(bf16[2,256,512]{2,1,0:T(8,128)(2,1)} %refs_0_.1, s32[2,2]{1,0:T(2,128)} %refs_1_.1, ...), custom_call_target="tpu_custom_call" | custom-call | tf_op jit(solution)/shard_map/layers/pallas_call | solution.py:1172
  42.5 2.6 %lay_out.1 = (bf16[2,256,128]{2,1,0:T(8,128)(2,1)}, f32[2,256,128]{2,1,0:T(8,128)}, f32[2,512]{1,0:T(2,128)}, f32[2,512]{1,0:T(2,128)}, f32[2,192]{1,0:T(2,128)}...) custom-call(bf16[2,4,4,16,1280]{4,3,2,1,0:T(8,128)(2,1)S(1)} %get-tu, ...), custom_call_target="tpu_custom_call" | custom-call | tf_op jit(solution)/shard_map/lay_out/pallas_call | solution.py:1198
